TPU v7x, 256 devices: a whole 4x4x8 slice. The times are simulated.
256 devices in a mesh: seq: 64 (over z_hi, y, x), head: 4 (over z_lo, core).
Axes of the slice: x: 4, y: 4, z: 8 (z_hi: 4, z_lo: 2; z = z_hi * 2 + z_lo), core: 2. Of those that a mesh axis runs over, the one named last changes fastest.
Arguments:
- queries: bfloat16 [16384, 20, 128], P(('seq', 'head')), may hold values from -6 to 6
- key_vectors: bfloat16 [16384, 20, 128], P(('seq', 'head')), may hold values from -6 to 6
- value_vectors: bfloat16 [16384, 20, 128], P(('seq', 'head')), may hold values from -40 to 40
- grad_output: bfloat16 [16384, 20, 128], P(('seq', 'head')), may hold values from -40 to 40
- block_mask: int32 [128, 128], replicated, may hold values from 0 to 1, as said below
- block_frame: int32 [128], replicated, may hold values from 0 to 20, as said below
Outputs:
- attended: bfloat16 [16384, 20, 128], P(('seq', 'head'))
- grad_queries: bfloat16 [16384, 20, 128], P(('seq', 'head'))
- grad_keys: bfloat16 [16384, 20, 128], P(('seq', 'head'))
- grad_values: bfloat16 [16384, 20, 128], P(('seq', 'head'))
Inputs may be any that keep to these rules, and one draw needn't show every extreme that they name: Frame groups are runs of 2 blocks. block_mask is 1 on the diagonal, and 0 unless the frame groups of its row and column are equal or differ by a power of two. `block_frame`: Nondecreasing; block 0 lies in frame 0 and the last block in frame 21 - 1.
All inputs are finite; a program needn't handle non-finite values.
Results may differ from a plain program's by a relative error of at most 0.038.
Values may be sent and summed in bfloat16 or wider, within the bound.
No kernel may reach another device: no remote copies, remote signals or barrier semaphores. Data moves between devices by JAX's collectives and lax.ppermute only.
A program may use at most 128 MiB of HBM per device.

v0:
```python
import math

import jax
import jax.numpy as jnp
from jax import lax
from jax.sharding import PartitionSpec as P

ROT = 44
BLK = 128


def from_behind(value, axis, by):
    length = lax.axis_size(axis)
    pairs = [(i, i + by) for i in range(length) if 0 <= i + by < length]
    return lax.ppermute(value, axis, pairs)


def distance_list(count):
    found = []
    stride = 1
    while stride < count:
        found.append(stride)
        stride = stride * 2
    return found


def rotate(values_in, frame_rows, inverse):
    half_dims = ROT // 2
    inv_freq = 10000.0 ** (-2.0 * jnp.arange(half_dims, dtype=jnp.float32) / ROT)
    angles = frame_rows.astype(jnp.float32)[:, None] * inv_freq[None, :]
    cosine = jnp.cos(angles)[:, None, :]
    sine_part = jnp.sin(angles)[:, None, :]
    if inverse:
        sine_part = -sine_part
    first_half = values_in[..., :half_dims]
    second_half = values_in[..., half_dims:ROT]
    return jnp.concatenate(
        [
            first_half * cosine - second_half * sine_part,
            first_half * sine_part + second_half * cosine,
            values_in[..., ROT:],
        ],
        axis=-1,
    )


def token_mask(block_mask, row_group, col_group, groups, per_group):
    inside = (
        (row_group >= 0) & (row_group < groups) & (col_group >= 0) & (col_group < groups)
    ).astype(jnp.int32)
    row_start = jnp.clip(row_group, 0, groups - 1) * per_group
    col_start = jnp.clip(col_group, 0, groups - 1) * per_group
    block_piece = (
        lax.dynamic_slice(block_mask, (row_start, col_start), (per_group, per_group)) * inside
    )
    expanded = jnp.broadcast_to(block_piece[:, None, :, None], (per_group, BLK, per_group, BLK))
    return expanded.reshape(per_group * BLK, per_group * BLK) > 0


def pair_terms(q_rows, grad_rows, log_total, row_delta, k_rows, v_rows, allowed, score_scale):
    scores = (
        jnp.einsum("qhe,khe->hqk", q_rows, k_rows, preferred_element_type=jnp.float32) * score_scale
    )
    weights = jnp.exp(jnp.where(allowed[None], scores - log_total[:, :, None], -1e30))
    dweights = jnp.einsum("qhe,khe->hqk", grad_rows, v_rows, preferred_element_type=jnp.float32)
    dscore = (weights * (dweights - row_delta[:, :, None])).astype(jnp.bfloat16)
    return (weights.astype(jnp.bfloat16), dscore)


def shards(queries, key_vectors, value_vectors, grad_output, block_mask, block_frame):
    stacked = jnp.stack([queries, key_vectors, value_vectors, grad_output])
    arrived = lax.all_to_all(stacked, "head", split_axis=2, concat_axis=1, tiled=True)
    tok_rows = arrived.shape[1]
    head_count = arrived.shape[2]
    head_dims = arrived.shape[3]
    score_scale = 1.0 / math.sqrt(head_dims)
    groups = lax.axis_size("seq")
    position = lax.axis_index("seq")
    per_group = tok_rows // BLK
    frames_here = lax.dynamic_slice_in_dim(block_frame, position * per_group, per_group)
    frame_rows = jnp.repeat(frames_here, BLK)
    q_loc = rotate(arrived[0].astype(jnp.float32), frame_rows, False).astype(jnp.bfloat16)
    k_loc = rotate(arrived[1].astype(jnp.float32), frame_rows, False).astype(jnp.bfloat16)
    v_loc = arrived[2]
    grad_loc = arrived[3]
    strides = distance_list(groups)
    offsets = []
    for stride in strides:
        offsets = offsets + [stride, -stride]
    sources = [(k_loc, v_loc, token_mask(block_mask, position, position, groups, per_group), 0)]
    for offset in offsets:
        pair_kv = from_behind(jnp.stack([k_loc, v_loc]), "seq", offset)
        sources.append(
            (
                pair_kv[0],
                pair_kv[1],
                token_mask(block_mask, position, position - offset, groups, per_group),
                offset,
            )
        )
    running_max = jnp.full((head_count, tok_rows), -1e30, jnp.float32)
    denominator = jnp.zeros((head_count, tok_rows), jnp.float32)
    accumulated = jnp.zeros((tok_rows, head_count, head_dims), jnp.float32)
    for k_src, v_src, allowed, offset in sources:
        scores = (
            jnp.einsum("qhe,khe->hqk", q_loc, k_src, preferred_element_type=jnp.float32)
            * score_scale
        )
        masked = jnp.where(allowed[None], scores, -1e30)
        new_max = jnp.maximum(running_max, jnp.max(masked, axis=2))
        shrink = jnp.exp(running_max - new_max)
        scaled = jnp.exp(masked - new_max[:, :, None])
        denominator = denominator * shrink + jnp.sum(scaled, axis=2)
        accumulated = accumulated * shrink.T[:, :, None] + jnp.einsum(
            "hqk,khe->qhe", scaled.astype(jnp.bfloat16), v_src, preferred_element_type=jnp.float32
        )
        running_max = new_max
    attended = (accumulated / denominator.T[:, :, None]).astype(jnp.bfloat16)
    log_total = running_max + jnp.log(denominator)
    row_delta = jnp.sum(grad_loc.astype(jnp.float32) * attended.astype(jnp.float32), axis=2).T
    dq_sum = jnp.zeros((tok_rows, head_count, head_dims), jnp.float32)
    dk_sum = jnp.zeros((tok_rows, head_count, head_dims), jnp.float32)
    dv_sum = jnp.zeros((tok_rows, head_count, head_dims), jnp.float32)
    for k_src, v_src, allowed, offset in sources:
        weights_bf, dscore = pair_terms(
            q_loc, grad_loc, log_total, row_delta, k_src, v_src, allowed, score_scale
        )
        dq_sum = dq_sum + jnp.einsum(
            "hqk,khe->qhe", dscore, k_src, preferred_element_type=jnp.float32
        )
        dk_part = jnp.einsum("hqk,qhe->khe", dscore, q_loc, preferred_element_type=jnp.float32)
        dv_part = jnp.einsum(
            "hqk,qhe->khe", weights_bf, grad_loc, preferred_element_type=jnp.float32
        )
        if offset == 0:
            dk_sum = dk_part
            dv_sum = dv_part
        else:
            outgoing = jnp.stack([dk_part, dv_part]).astype(jnp.bfloat16)
            returned = from_behind(outgoing, "seq", -offset)
            dk_sum = dk_sum + returned[0].astype(jnp.float32)
            dv_sum = dv_sum + returned[1].astype(jnp.float32)
    grad_q = rotate(dq_sum * score_scale, frame_rows, True).astype(jnp.bfloat16)
    grad_k = rotate(dk_sum * score_scale, frame_rows, True).astype(jnp.bfloat16)
    grad_v = dv_sum.astype(jnp.bfloat16)
    leaving = lax.all_to_all(
        jnp.stack([attended, grad_q, grad_k, grad_v]),
        "head",
        split_axis=1,
        concat_axis=2,
        tiled=True,
    )
    return (leaving[0], leaving[1], leaving[2], leaving[3])


def solution(mesh):
    in_specs = (
        P(("seq", "head"), None, None),
        P(("seq", "head"), None, None),
        P(("seq", "head"), None, None),
        P(("seq", "head"), None, None),
        P(),
        P(),
    )
    out_specs = (
        P(("seq", "head"), None, None),
        P(("seq", "head"), None, None),
        P(("seq", "head"), None, None),
        P(("seq", "head"), None, None),
    )
    return jax.shard_map(shards, mesh=mesh, in_specs=in_specs, out_specs=out_specs, check_vma=False)
```

profile of v0, /device:TPU:64, one launch (start us, length us, event | category | flops | bytes accessed | tf_op | source)
XLA Modules:
  0.0 491.6 jit_solution(2351598856248280209)
XLA Ops:
  0.6 2.5 pad_maximum_fusion
  3.1 3.7 all-to-all-start
  7.0 1.2 fusion.251
  8.2 15.9 %all-to-all-done = bf16[4,64,20,128]{3,1,0,2:T(8,128)(2,1)S(1)} async-done(((bf16[4,64,20,128]{3,1,0,2:T(8,128)(2,1)}), bf16[4,64,20,128]{3,1,0,2:T(8,128)(2,1)S(1)}, u32[]{:S(2)}, u32[]{:S(2)}) %all-to-all-start) | async-done | bytes 1310752 | tf_op jit(solution)/shard_map/all_to_all | solution.py:72
  25.2 1.2 pad_maximum_fusion.2
  26.4 1.3 collective-permute-start.11
  30.0 1.1 multiply_compare_fusion.12
  39.7 9.3 %collective-permute-start.10 = (bf16[2,256,5,128]{3,1,2,0:T(8,128)(2,1)}, bf16[2,256,5,128]{3,1,2,0:T(8,128)(2,1)S(1)}, u32[]{:S(2)}, u32[]{:S(2)}) collective-permute-start(bf16[2,256,5,128]{3,1,2,0:T(8,128)(2,1)} %pad_maximum_fusion.2), channel_id=1, source_target_pairs={{0,128},{4,132},{8,136},{12,140},{16,144},{20,148},{24,152},{28,15... | collective-permute-start | bytes 1966088 | tf_op jit(solution)/shard_map/ppermute | solution.py:15
  48.9 3.3 collective-permute-start.9
  52.2 2.8 collective-permute-start.7
  55.1 4.5 collective-permute-start.6
  60.6 2.2 collective-permute-done.11
  62.9 2.2 collective-permute-start.5
  65.1 1.3 select_reduce_fusion
  66.5 76.5 %collective-permute-done.7 = bf16[2,256,5,128]{3,1,2,0:T(8,128)(2,1)S(1)} collective-permute-done((bf16[2,256,5,128]{3,1,2,0:T(8,128)(2,1)}, bf16[2,256,5,128]{3,1,2,0:T(8,128)(2,1)S(1)}, u32[]{:S(2)}, u32[]{:S(2)}) %collective-permute-start.7) | collective-permute-done | bytes 655392 | tf_op jit(solution)/shard_map/ppermute | solution.py:15
  142.9 1.9 collective-permute-start.4
  145.2 1.9 collective-permute-start.3
  147.5 14.9 %collective-permute-done.5 = bf16[2,256,5,128]{3,1,2,0:T(8,128)(2,1)S(1)} collective-permute-done((bf16[2,256,5,128]{3,1,2,0:T(8,128)(2,1)}, bf16[2,256,5,128]{3,1,2,0:T(8,128)(2,1)S(1)}, u32[]{:S(2)}, u32[]{:S(2)}) %collective-permute-start.5) | collective-permute-done | bytes 655392 | tf_op jit(solution)/shard_map/ppermute | solution.py:15
  162.5 1.9 collective-permute-start.2
  164.8 1.9 collective-permute-start.1
  167.1 9.5 %collective-permute-done.3 = bf16[2,256,5,128]{3,1,2,0:T(8,128)(2,1)S(1)} collective-permute-done((bf16[2,256,5,128]{3,1,2,0:T(8,128)(2,1)}, bf16[2,256,5,128]{3,1,2,0:T(8,128)(2,1)S(1)}, u32[]{:S(2)}, u32[]{:S(2)}) %collective-permute-start.3) | collective-permute-done | bytes 655392 | tf_op jit(solution)/shard_map/ppermute | solution.py:15
  176.6 1.9 collective-permute-start
  178.8 15.0 %collective-permute-done.2 = bf16[2,256,5,128]{3,1,2,0:T(8,128)(2,1)S(1)} collective-permute-done((bf16[2,256,5,128]{3,1,2,0:T(8,128)(2,1)}, bf16[2,256,5,128]{3,1,2,0:T(8,128)(2,1)S(1)}, u32[]{:S(2)}, u32[]{:S(2)}) %collective-permute-start.2) | collective-permute-done | bytes 655392 | tf_op jit(solution)/shard_map/ppermute | solution.py:15
  193.8 19.0 %collective-permute-start.8 = (bf16[2,256,5,128]{3,1,2,0:T(8,128)(2,1)}, bf16[2,256,5,128]{3,1,2,0:T(8,128)(2,1)S(1)}, u32[]{:S(2)}, u32[]{:S(2)}) collective-permute-start(bf16[2,256,5,128]{3,1,2,0:T(8,128)(2,1)} %pad_maximum_fusion.2), channel_id=1, source_target_pairs={{0,64},{4,68},{8,72},{12,76},{16,80},{20,84},{24,88},{28,92},{32,9... | collective-permute-start | bytes 1966088 | tf_op jit(solution)/shard_map/ppermute | solution.py:15
  215.6 23.7 %collective-permute-done.8 = bf16[2,256,5,128]{3,1,2,0:T(8,128)(2,1)S(1)} collective-permute-done((bf16[2,256,5,128]{3,1,2,0:T(8,128)(2,1)}, bf16[2,256,5,128]{3,1,2,0:T(8,128)(2,1)S(1)}, u32[]{:S(2)}, u32[]{:S(2)}) %collective-permute-start.8) | collective-permute-done | bytes 655392 | tf_op jit(solution)/shard_map/ppermute | solution.py:15
  255.1 1.7 multiply_reduce_fusion
  257.3 1.4 fusion.13
  259.1 1.3 collective-permute-start.23
  261.3 1.3 collective-permute-start.22
  263.5 31.8 %collective-permute-start.21 = (bf16[2,256,5,128]{3,1,2,0:T(8,128)(2,1)S(1)}, bf16[2,256,5,128]{3,1,2,0:T(8,128)(2,1)S(1)}, u32[]{:S(2)}, u32[]{:S(2)}) collective-permute-start(bf16[2,256,5,128]{3,1,2,0:T(8,128)(2,1)S(1)} %pad_maximum_fusion.12), channel_id=1, source_target_pairs={{0,64},{4,68},{8,72},{12,76},{16,80},{20,84},{24,88},{28,92},{32,9... | collective-permute-start | bytes 1966088 | tf_op jit(solution)/shard_map/ppermute | solution.py:15
  296.1 1.9 collective-permute-start.20
  298.9 2.1 collective-permute-start.19
  307.5 1.3 fusion.250
  312.0 7.2 %collective-permute-start.18 = (bf16[2,256,5,128]{3,1,2,0:T(8,128)(2,1)S(1)}, bf16[2,256,5,128]{3,1,2,0:T(8,128)(2,1)S(1)}, u32[]{:S(2)}, u32[]{:S(2)}) collective-permute-start(bf16[2,256,5,128]{3,1,2,0:T(8,128)(2,1)S(1)} %pad_maximum_fusion.9), channel_id=1, source_target_pairs={{32,0},{36,4},{40,8},{44,12},{48,16},{52,20},{56,24},{60,28},{64,3... | collective-permute-start | bytes 1966088 | tf_op jit(solution)/shard_map/ppermute | solution.py:15
  319.2 1.9 collective-permute-start.17
  322.0 6.9 %collective-permute-start.16 = (bf16[2,256,5,128]{3,1,2,0:T(8,128)(2,1)S(1)}, bf16[2,256,5,128]{3,1,2,0:T(8,128)(2,1)S(1)}, u32[]{:S(2)}, u32[]{:S(2)}) collective-permute-start(bf16[2,256,5,128]{3,1,2,0:T(8,128)(2,1)S(1)} %pad_maximum_fusion.7), channel_id=1, source_target_pairs={{16,0},{20,4},{24,8},{28,12},{32,16},{36,20},{40,24},{44,28},{48,3... | collective-permute-start | bytes 1966088 | tf_op jit(solution)/shard_map/ppermute | solution.py:15
  328.9 16.8 %collective-permute-done.20 = bf16[2,256,5,128]{3,1,2,0:T(8,128)(2,1)S(1)} collective-permute-done((bf16[2,256,5,128]{3,1,2,0:T(8,128)(2,1)S(1)}, bf16[2,256,5,128]{3,1,2,0:T(8,128)(2,1)S(1)}, u32[]{:S(2)}, u32[]{:S(2)}) %collective-permute-start.20) | collective-permute-done | bytes 655392 | tf_op jit(solution)/shard_map/ppermute | solution.py:15
  345.7 1.9 collective-permute-start.15
  347.7 9.3 %collective-permute-start.14 = (bf16[2,256,5,128]{3,1,2,0:T(8,128)(2,1)S(1)}, bf16[2,256,5,128]{3,1,2,0:T(8,128)(2,1)S(1)}, u32[]{:S(2)}, u32[]{:S(2)}) collective-permute-start(bf16[2,256,5,128]{3,1,2,0:T(8,128)(2,1)S(1)} %pad_maximum_fusion.5), channel_id=1, source_target_pairs={{8,0},{12,4},{16,8},{20,12},{24,16},{28,20},{32,24},{36,28},{40,32... | collective-permute-start | bytes 1966088 | tf_op jit(solution)/shard_map/ppermute | solution.py:15
  357.0 15.3 %collective-permute-done.18 = bf16[2,256,5,128]{3,1,2,0:T(8,128)(2,1)S(1)} collective-permute-done((bf16[2,256,5,128]{3,1,2,0:T(8,128)(2,1)S(1)}, bf16[2,256,5,128]{3,1,2,0:T(8,128)(2,1)S(1)}, u32[]{:S(2)}, u32[]{:S(2)}) %collective-permute-start.18) | collective-permute-done | bytes 655392 | tf_op jit(solution)/shard_map/ppermute | solution.py:15
  372.3 1.9 collective-permute-start.13
  374.2 9.3 %collective-permute-start.12 = (bf16[2,256,5,128]{3,1,2,0:T(8,128)(2,1)S(1)}, bf16[2,256,5,128]{3,1,2,0:T(8,128)(2,1)S(1)}, u32[]{:S(2)}, u32[]{:S(2)}) collective-permute-start(bf16[2,256,5,128]{3,1,2,0:T(8,128)(2,1)S(1)} %pad_maximum_fusion.3), channel_id=1, source_target_pairs={{4,0},{8,4},{12,8},{16,12},{20,16},{24,20},{28,24},{32,28},{36,32}... | collective-permute-start | bytes 1966088 | tf_op jit(solution)/shard_map/ppermute | solution.py:15
  384.3 2.1 collective-permute-done.16
  386.4 14.0 %collective-permute-done.14 = bf16[2,256,5,128]{3,1,2,0:T(8,128)(2,1)S(1)} collective-permute-done((bf16[2,256,5,128]{3,1,2,0:T(8,128)(2,1)S(1)}, bf16[2,256,5,128]{3,1,2,0:T(8,128)(2,1)S(1)}, u32[]{:S(2)}, u32[]{:S(2)}) %collective-permute-start.14) | collective-permute-done | bytes 655392 | tf_op jit(solution)/shard_map/ppermute | solution.py:15
  400.4 12.9 %collective-permute-done.12 = bf16[2,256,5,128]{3,1,2,0:T(8,128)(2,1)S(1)} collective-permute-done((bf16[2,256,5,128]{3,1,2,0:T(8,128)(2,1)S(1)}, bf16[2,256,5,128]{3,1,2,0:T(8,128)(2,1)S(1)}, u32[]{:S(2)}, u32[]{:S(2)}) %collective-permute-start.12) | collective-permute-done | bytes 655392 | tf_op jit(solution)/shard_map/ppermute | solution.py:15
  416.2 1.0 copy.956
  417.2 68.8 %all_to_all.30 = bf16[4,256,5,128]{3,0,2,1:T(4,128)(2,1)S(1)} all-to-all(bf16[4,256,5,128]{3,0,2,1:T(4,128)(2,1)S(1)} %copy.956), channel_id=1, replica_groups=mesh['seq'=64,'head'=4] {'head'}, dimensions={1} | all-to-all | bytes 2621440 | tf_op jit(solution)/shard_map/all_to_all | solution.py:146
  486.0 1.9 fusion.301
  (189 shorter events, 54.1 us)
Async XLA Ops:
  3.1 3.7 copy-start.7
  3.1 20.9 %all-to-all-start = ((bf16[4,64,20,128]{3,1,0,2:T(8,128)(2,1)}), bf16[4,64,20,128]{3,1,0,2:T(8,128)(2,1)S(1)}, u32[]{:S(2)}, u32[]{:S(2)}) async-start(bf16[4,64,20,128]{3,1,0,2:T(8,128)(2,1)} %pad_maximum_fusion), calls=%async_computation | async-start | bytes 2621440 | tf_op jit(solution)/shard_map/all_to_all | solution.py:72
  26.4 36.5 %collective-permute-start.11 = (bf16[2,256,5,128]{3,1,2,0:T(8,128)(2,1)}, bf16[2,256,5,128]{3,1,2,0:T(8,128)(2,1)}, u32[]{:S(2)}, u32[]{:S(2)}) collective-permute-start(bf16[2,256,5,128]{3,1,2,0:T(8,128)(2,1)} %pad_maximum_fusion.2), channel_id=1, source_target_pairs={{128,0},{132,4},{136,8},{140,12},{144,16},{148,20},{152,24},{156,2... | collective-permute-start | bytes 1966088 | tf_op jit(solution)/shard_map/ppermute | solution.py:15
  39.7 174.8 %collective-permute-start.10 = (bf16[2,256,5,128]{3,1,2,0:T(8,128)(2,1)}, bf16[2,256,5,128]{3,1,2,0:T(8,128)(2,1)S(1)}, u32[]{:S(2)}, u32[]{:S(2)}) collective-permute-start(bf16[2,256,5,128]{3,1,2,0:T(8,128)(2,1)} %pad_maximum_fusion.2), channel_id=1, source_target_pairs={{0,128},{4,132},{8,136},{12,140},{16,144},{20,148},{24,152},{28,15... | collective-permute-start | bytes 1966088 | tf_op jit(solution)/shard_map/ppermute | solution.py:15
  48.9 165.9 %collective-permute-start.9 = (bf16[2,256,5,128]{3,1,2,0:T(8,128)(2,1)}, bf16[2,256,5,128]{3,1,2,0:T(8,128)(2,1)S(1)}, u32[]{:S(2)}, u32[]{:S(2)}) collective-permute-start(bf16[2,256,5,128]{3,1,2,0:T(8,128)(2,1)} %pad_maximum_fusion.2), channel_id=1, source_target_pairs={{64,0},{68,4},{72,8},{76,12},{80,16},{84,20},{88,24},{92,28},{96,3... | collective-permute-start | bytes 1966088 | tf_op jit(solution)/shard_map/ppermute | solution.py:15
  52.2 90.7 %collective-permute-start.7 = (bf16[2,256,5,128]{3,1,2,0:T(8,128)(2,1)}, bf16[2,256,5,128]{3,1,2,0:T(8,128)(2,1)S(1)}, u32[]{:S(2)}, u32[]{:S(2)}) collective-permute-start(bf16[2,256,5,128]{3,1,2,0:T(8,128)(2,1)} %pad_maximum_fusion.2), channel_id=1, source_target_pairs={{32,0},{36,4},{40,8},{44,12},{48,16},{52,20},{56,24},{60,28},{64,3... | collective-permute-start | bytes 1966088 | tf_op jit(solution)/shard_map/ppermute | solution.py:15
  55.1 90.1 %collective-permute-start.6 = (bf16[2,256,5,128]{3,1,2,0:T(8,128)(2,1)}, bf16[2,256,5,128]{3,1,2,0:T(8,128)(2,1)S(1)}, u32[]{:S(2)}, u32[]{:S(2)}) collective-permute-start(bf16[2,256,5,128]{3,1,2,0:T(8,128)(2,1)} %pad_maximum_fusion.2), channel_id=1, source_target_pairs={{0,32},{4,36},{8,40},{12,44},{16,48},{20,52},{24,56},{28,60},{32,6... | collective-permute-start | bytes 1966088 | tf_op jit(solution)/shard_map/ppermute | solution.py:15
  60.1 5.0 %copy-start.5 = (pred[256,256]{0,1:T(8,128)(4,1)S(1)}, pred[256,256]{0,1:T(8,128)(4,1)}, u32[]{:S(2)}) copy-start(pred[256,256]{0,1:T(8,128)(4,1)} %copy.821) | copy-start | bytes 196612
  62.9 99.6 %collective-permute-start.5 = (bf16[2,256,5,128]{3,1,2,0:T(8,128)(2,1)}, bf16[2,256,5,128]{3,1,2,0:T(8,128)(2,1)S(1)}, u32[]{:S(2)}, u32[]{:S(2)}) collective-permute-start(bf16[2,256,5,128]{3,1,2,0:T(8,128)(2,1)} %pad_maximum_fusion.2), channel_id=1, source_target_pairs={{16,0},{20,4},{24,8},{28,12},{32,16},{36,20},{40,24},{44,28},{48,3... | collective-permute-start | bytes 1966088 | tf_op jit(solution)/shard_map/ppermute | solution.py:15
  142.9 21.8 %collective-permute-start.4 = (bf16[2,256,5,128]{3,1,2,0:T(8,128)(2,1)}, bf16[2,256,5,128]{3,1,2,0:T(8,128)(2,1)S(1)}, u32[]{:S(2)}, u32[]{:S(2)}) collective-permute-start(bf16[2,256,5,128]{3,1,2,0:T(8,128)(2,1)} %pad_maximum_fusion.2), channel_id=1, source_target_pairs={{0,16},{4,20},{8,24},{12,28},{16,32},{20,36},{24,40},{28,44},{32,4... | collective-permute-start | bytes 1966088 | tf_op jit(solution)/shard_map/ppermute | solution.py:15
  145.2 31.3 %collective-permute-start.3 = (bf16[2,256,5,128]{3,1,2,0:T(8,128)(2,1)}, bf16[2,256,5,128]{3,1,2,0:T(8,128)(2,1)S(1)}, u32[]{:S(2)}, u32[]{:S(2)}) collective-permute-start(bf16[2,256,5,128]{3,1,2,0:T(8,128)(2,1)} %pad_maximum_fusion.2), channel_id=1, source_target_pairs={{8,0},{12,4},{16,8},{20,12},{24,16},{28,20},{32,24},{36,28},{40,32... | collective-permute-start | bytes 1966088 | tf_op jit(solution)/shard_map/ppermute | solution.py:15
  162.5 31.4 %collective-permute-start.2 = (bf16[2,256,5,128]{3,1,2,0:T(8,128)(2,1)}, bf16[2,256,5,128]{3,1,2,0:T(8,128)(2,1)S(1)}, u32[]{:S(2)}, u32[]{:S(2)}) collective-permute-start(bf16[2,256,5,128]{3,1,2,0:T(8,128)(2,1)} %pad_maximum_fusion.2), channel_id=1, source_target_pairs={{0,8},{4,12},{8,16},{12,20},{16,24},{20,28},{24,32},{28,36},{32,40... | collective-permute-start | bytes 1966088 | tf_op jit(solution)/shard_map/ppermute | solution.py:15
  164.8 48.4 %collective-permute-start.1 = (bf16[2,256,5,128]{3,1,2,0:T(8,128)(2,1)}, bf16[2,256,5,128]{3,1,2,0:T(8,128)(2,1)S(1)}, u32[]{:S(2)}, u32[]{:S(2)}) collective-permute-start(bf16[2,256,5,128]{3,1,2,0:T(8,128)(2,1)} %pad_maximum_fusion.2), channel_id=1, source_target_pairs={{4,0},{8,4},{12,8},{16,12},{20,16},{24,20},{28,24},{32,28},{36,32}... | collective-permute-start | bytes 1966088 | tf_op jit(solution)/shard_map/ppermute | solution.py:15
  167.1 45.8 %copy-start = (pred[256,256]{0,1:T(8,128)(4,1)S(1)}, pred[256,256]{0,1:T(8,128)(4,1)}, u32[]{:S(2)}) copy-start(pred[256,256]{0,1:T(8,128)(4,1)} %copy.785) | copy-start | bytes 196612
  176.6 37.0 %collective-permute-start = (bf16[2,256,5,128]{3,1,2,0:T(8,128)(2,1)}, bf16[2,256,5,128]{3,1,2,0:T(8,128)(2,1)S(1)}, u32[]{:S(2)}, u32[]{:S(2)}) collective-permute-start(bf16[2,256,5,128]{3,1,2,0:T(8,128)(2,1)} %pad_maximum_fusion.2), channel_id=1, source_target_pairs={{0,4},{4,8},{8,12},{12,16},{16,20},{20,24},{24,28},{28,32},{32,36}... | collective-permute-start | bytes 1966088 | tf_op jit(solution)/shard_map/ppermute | solution.py:15
  178.8 34.4 %copy-start.2 = (pred[256,256]{0,1:T(8,128)(4,1)S(1)}, pred[256,256]{0,1:T(8,128)(4,1)}, u32[]{:S(2)}) copy-start(pred[256,256]{0,1:T(8,128)(4,1)} %copy.781) | copy-start | bytes 196612
  193.8 45.5 %collective-permute-start.8 = (bf16[2,256,5,128]{3,1,2,0:T(8,128)(2,1)}, bf16[2,256,5,128]{3,1,2,0:T(8,128)(2,1)S(1)}, u32[]{:S(2)}, u32[]{:S(2)}) collective-permute-start(bf16[2,256,5,128]{3,1,2,0:T(8,128)(2,1)} %pad_maximum_fusion.2), channel_id=1, source_target_pairs={{0,64},{4,68},{8,72},{12,76},{16,80},{20,84},{24,88},{28,92},{32,9... | collective-permute-start | bytes 1966088 | tf_op jit(solution)/shard_map/ppermute | solution.py:15
  213.2 0.8 copy-start.3
  214.4 0.8 copy-start.4
  214.8 24.5 %copy-start.1 = (pred[256,256]{0,1:T(8,128)(4,1)S(1)}, pred[256,256]{0,1:T(8,128)(4,1)}, u32[]{:S(2)}) copy-start(pred[256,256]{0,1:T(8,128)(4,1)} %copy.809) | copy-start | bytes 196612
  259.1 52.9 %collective-permute-start.23 = (bf16[2,256,5,128]{3,1,2,0:T(8,128)(2,1)S(1)}, bf16[2,256,5,128]{3,1,2,0:T(8,128)(2,1)S(1)}, u32[]{:S(2)}, u32[]{:S(2)}) collective-permute-start(bf16[2,256,5,128]{3,1,2,0:T(8,128)(2,1)S(1)} %pad_maximum_fusion.14), channel_id=1, source_target_pairs={{0,128},{4,132},{8,136},{12,140},{16,144},{20,148},{24,152},{28,15... | collective-permute-start | bytes 1966088 | tf_op jit(solution)/shard_map/ppermute | solution.py:15
  261.3 57.9 %collective-permute-start.22 = (bf16[2,256,5,128]{3,1,2,0:T(8,128)(2,1)S(1)}, bf16[2,256,5,128]{3,1,2,0:T(8,128)(2,1)S(1)}, u32[]{:S(2)}, u32[]{:S(2)}) collective-permute-start(bf16[2,256,5,128]{3,1,2,0:T(8,128)(2,1)S(1)} %pad_maximum_fusion.13), channel_id=1, source_target_pairs={{128,0},{132,4},{136,8},{140,12},{144,16},{148,20},{152,24},{156,2... | collective-permute-start | bytes 1966088 | tf_op jit(solution)/shard_map/ppermute | solution.py:15
  263.5 58.5 %collective-permute-start.21 = (bf16[2,256,5,128]{3,1,2,0:T(8,128)(2,1)S(1)}, bf16[2,256,5,128]{3,1,2,0:T(8,128)(2,1)S(1)}, u32[]{:S(2)}, u32[]{:S(2)}) collective-permute-start(bf16[2,256,5,128]{3,1,2,0:T(8,128)(2,1)S(1)} %pad_maximum_fusion.12), channel_id=1, source_target_pairs={{0,64},{4,68},{8,72},{12,76},{16,80},{20,84},{24,88},{28,92},{32,9... | collective-permute-start | bytes 1966088 | tf_op jit(solution)/shard_map/ppermute | solution.py:15
  296.1 49.6 %collective-permute-start.20 = (bf16[2,256,5,128]{3,1,2,0:T(8,128)(2,1)S(1)}, bf16[2,256,5,128]{3,1,2,0:T(8,128)(2,1)S(1)}, u32[]{:S(2)}, u32[]{:S(2)}) collective-permute-start(bf16[2,256,5,128]{3,1,2,0:T(8,128)(2,1)S(1)} %pad_maximum_fusion.11), channel_id=1, source_target_pairs={{64,0},{68,4},{72,8},{76,12},{80,16},{84,20},{88,24},{92,28},{96,3... | collective-permute-start | bytes 1966088 | tf_op jit(solution)/shard_map/ppermute | solution.py:15
  298.9 48.8 %collective-permute-start.19 = (bf16[2,256,5,128]{3,1,2,0:T(8,128)(2,1)S(1)}, bf16[2,256,5,128]{3,1,2,0:T(8,128)(2,1)S(1)}, u32[]{:S(2)}, u32[]{:S(2)}) collective-permute-start(bf16[2,256,5,128]{3,1,2,0:T(8,128)(2,1)S(1)} %pad_maximum_fusion.10), channel_id=1, source_target_pairs={{0,32},{4,36},{8,40},{12,44},{16,48},{20,52},{24,56},{28,60},{32,6... | collective-permute-start | bytes 1966088 | tf_op jit(solution)/shard_map/ppermute | solution.py:15
  312.0 60.3 %collective-permute-start.18 = (bf16[2,256,5,128]{3,1,2,0:T(8,128)(2,1)S(1)}, bf16[2,256,5,128]{3,1,2,0:T(8,128)(2,1)S(1)}, u32[]{:S(2)}, u32[]{:S(2)}) collective-permute-start(bf16[2,256,5,128]{3,1,2,0:T(8,128)(2,1)S(1)} %pad_maximum_fusion.9), channel_id=1, source_target_pairs={{32,0},{36,4},{40,8},{44,12},{48,16},{52,20},{56,24},{60,28},{64,3... | collective-permute-start | bytes 1966088 | tf_op jit(solution)/shard_map/ppermute | solution.py:15
  319.2 55.0 %collective-permute-start.17 = (bf16[2,256,5,128]{3,1,2,0:T(8,128)(2,1)S(1)}, bf16[2,256,5,128]{3,1,2,0:T(8,128)(2,1)S(1)}, u32[]{:S(2)}, u32[]{:S(2)}) collective-permute-start(bf16[2,256,5,128]{3,1,2,0:T(8,128)(2,1)S(1)} %pad_maximum_fusion.8), channel_id=1, source_target_pairs={{0,16},{4,20},{8,24},{12,28},{16,32},{20,36},{24,40},{28,44},{32,4... | collective-permute-start | bytes 1966088 | tf_op jit(solution)/shard_map/ppermute | solution.py:15
  322.0 64.4 %collective-permute-start.16 = (bf16[2,256,5,128]{3,1,2,0:T(8,128)(2,1)S(1)}, bf16[2,256,5,128]{3,1,2,0:T(8,128)(2,1)S(1)}, u32[]{:S(2)}, u32[]{:S(2)}) collective-permute-start(bf16[2,256,5,128]{3,1,2,0:T(8,128)(2,1)S(1)} %pad_maximum_fusion.7), channel_id=1, source_target_pairs={{16,0},{20,4},{24,8},{28,12},{32,16},{36,20},{40,24},{44,28},{48,3... | collective-permute-start | bytes 1966088 | tf_op jit(solution)/shard_map/ppermute | solution.py:15
  345.7 40.6 %collective-permute-start.15 = (bf16[2,256,5,128]{3,1,2,0:T(8,128)(2,1)S(1)}, bf16[2,256,5,128]{3,1,2,0:T(8,128)(2,1)S(1)}, u32[]{:S(2)}, u32[]{:S(2)}) collective-permute-start(bf16[2,256,5,128]{3,1,2,0:T(8,128)(2,1)S(1)} %pad_maximum_fusion.6), channel_id=1, source_target_pairs={{0,8},{4,12},{8,16},{12,20},{16,24},{20,28},{24,32},{28,36},{32,40... | collective-permute-start | bytes 1966088 | tf_op jit(solution)/shard_map/ppermute | solution.py:15
  347.7 52.7 %collective-permute-start.14 = (bf16[2,256,5,128]{3,1,2,0:T(8,128)(2,1)S(1)}, bf16[2,256,5,128]{3,1,2,0:T(8,128)(2,1)S(1)}, u32[]{:S(2)}, u32[]{:S(2)}) collective-permute-start(bf16[2,256,5,128]{3,1,2,0:T(8,128)(2,1)S(1)} %pad_maximum_fusion.5), channel_id=1, source_target_pairs={{8,0},{12,4},{16,8},{20,12},{24,16},{28,20},{32,24},{36,28},{40,32... | collective-permute-start | bytes 1966088 | tf_op jit(solution)/shard_map/ppermute | solution.py:15
  372.3 28.1 %collective-permute-start.13 = (bf16[2,256,5,128]{3,1,2,0:T(8,128)(2,1)S(1)}, bf16[2,256,5,128]{3,1,2,0:T(8,128)(2,1)S(1)}, u32[]{:S(2)}, u32[]{:S(2)}) collective-permute-start(bf16[2,256,5,128]{3,1,2,0:T(8,128)(2,1)S(1)} %pad_maximum_fusion.4), channel_id=1, source_target_pairs={{0,4},{4,8},{8,12},{12,16},{16,20},{20,24},{24,28},{28,32},{32,36}... | collective-permute-start | bytes 1966088 | tf_op jit(solution)/shard_map/ppermute | solution.py:15
  374.2 39.0 %collective-permute-start.12 = (bf16[2,256,5,128]{3,1,2,0:T(8,128)(2,1)S(1)}, bf16[2,256,5,128]{3,1,2,0:T(8,128)(2,1)S(1)}, u32[]{:S(2)}, u32[]{:S(2)}) collective-permute-start(bf16[2,256,5,128]{3,1,2,0:T(8,128)(2,1)S(1)} %pad_maximum_fusion.3), channel_id=1, source_target_pairs={{4,0},{8,4},{12,8},{16,12},{20,16},{24,20},{28,24},{32,28},{36,32}... | collective-permute-start | bytes 1966088 | tf_op jit(solution)/shard_map/ppermute | solution.py:15
  384.2 29.9 %copy-start.6 = (f32[256,22]{1,0:T(8,128)S(1)}, f32[256,22]{1,0:T(8,128)}, u32[]{:S(2)}) copy-start(f32[256,22]{1,0:T(8,128)} %get-tuple-element.68) | copy-start | bytes 67588
where the time goes:
time: 500 us; the launch traced here: 492 us
  waiting for transfers between devices  219 us (44%)
  starting transfers between devices  133 us (27%)
  blocking collectives  68.8 us (14%)
  matrix products  37.8 us (8%)
  local copies, waits for them, and re-layouts  17.6 us (4%)
  other arithmetic  13.3 us (3%)
    ppermute x24, waiting for transfers between devices, from_behind(): return lax.ppermute(value, axis, pairs)  203 us
    ppermute x24, starting transfers between devices, from_behind(): return lax.ppermute(value, axis, pairs)  129 us
    all_to_all x1, blocking collectives, shards(): lax.all_to_all(jnp.stack([attended, grad_q, grad_k, grad_v]), 'head', spl...  68.8 us
    all_to_all x1, waiting for transfers between devices, shards(): lax.all_to_all(stacked, 'head', split_axis=2, concat_axis=1, tiled=True)  15.9 us
  transfers between devices with their start and end apart: 25, of which 12 were waited for; matrix products, arithmetic and copies ran while one was open for 7% of the time, Pallas kernels for 0%

commit v1 on v0

v1 whole, which is shorter than its diff:
```python
import functools
import math

import jax
import jax.numpy as jnp
import numpy as np
from jax import lax
from jax.experimental import pallas as pl
from jax.experimental.pallas import tpu as pltpu
from jax.sharding import Mesh, PartitionSpec as P

ROT = 44
HALF = ROT // 2
BLK = 128
E = 128
TOK = 256
QTR = 64
GROUPS = 64
PLANE = 16
ZG = 4
UNITS = 5
NEG = -1e30
SHIFTS = (1, -1, 2, -2, 4, -4, 8)
OFFSETS = (0, 1, -1, 2, -2, 4, -4, 8, -8, 16, -16, 32, -32)
OWN = 36
ABOVE = 42
SLOTS = 45
SCALE = 1.0 / math.sqrt(E)
LOG2E = 1.4426950408889634
COEF = SCALE * LOG2E
F32 = jnp.float32
BF16 = jnp.bfloat16
ANY = pl.BlockSpec(memory_space=pl.ANY)
SMEM = pl.BlockSpec(memory_space=pltpu.SMEM)
VMEM = pl.BlockSpec(memory_space=pltpu.VMEM)


def dot(a, b, ca, cb):
    return lax.dot_general(a, b, (((ca,), (cb,)), ((), ())), preferred_element_type=F32)


def turn(x, c, s1, s2):
    return x * c + pltpu.roll(x, HALF, x.ndim - 1) * s1 + pltpu.roll(x, E - HALF, x.ndim - 1) * s2


def pack_kernel(pos, tab, a_ref, b_ref, m_ref, x_ref):
    row = 2 * pos[0] + pos[2] // 2
    t = tab[row]
    a = turn(a_ref[...].astype(F32), t[0:1][None], t[1:2][None], t[2:3][None])
    a = jnp.swapaxes(a, 0, 1).astype(BF16)
    b = jnp.swapaxes(b_ref[...].astype(F32), 0, 1).astype(BF16)
    m_ref[:, 0] = a[:16]
    m_ref[:, 1] = b[:16]
    x_ref[:, 0] = a[16:]
    x_ref[:, 1] = b[16:]


def pack(pos, tab, a, b):
    return pl.pallas_call(
        pack_kernel,
        out_shape=(
            jax.ShapeDtypeStruct((16, 2, QTR, E), BF16),
            jax.ShapeDtypeStruct((4, 2, QTR, E), BF16),
        ),
        in_specs=[SMEM, VMEM, VMEM, VMEM],
        out_specs=(VMEM, VMEM),
        compiler_params=pltpu.CompilerParams(vmem_limit_bytes=40 * 2**20),
        name="pack",
    )(pos, tab, a, b)


def unpack_kernel(m_ref, x_ref, a_ref, b_ref):
    for i, o in ((0, a_ref), (1, b_ref)):
        v = jnp.concatenate([m_ref[:, i], x_ref[:, i]], axis=0).astype(F32)
        o[...] = jnp.swapaxes(v, 0, 1).astype(BF16)


def unpack(m, x):
    shape = jax.ShapeDtypeStruct((QTR, 20, E), BF16)
    return pl.pallas_call(
        unpack_kernel,
        out_shape=(shape, shape),
        in_specs=[VMEM, VMEM],
        out_specs=(VMEM, VMEM),
        compiler_params=pltpu.CompilerParams(vmem_limit_bytes=40 * 2**20),
        name="unpack",
    )(m, x)


def source(offset, unit, zh, p):
    is_x = unit == 4
    z = jnp.where(is_x, zh, unit)
    group = z * PLANE + p
    other = group - offset
    valid = (other >= 0) & (other < GROUPS)
    if offset == 0:
        slot = OWN + jnp.where(is_x, 0, 1 + z)
    elif abs(offset) >= PLANE:
        m = OWN + 1 + jnp.clip(z - offset // PLANE, 0, ZG - 1)
        x = {16: ABOVE, -16: ABOVE + 1}.get(offset, ABOVE + 2)
        slot = jnp.where(is_x, x, m)
    else:
        at = p - offset
        w = jnp.where((at < 0) | (at >= PLANE), 1, 0)
        step = jnp.where(at < 0, -1, jnp.where(at >= PLANE, 1, 0))
        zz = jnp.clip(z + step, 0, ZG - 1)
        if abs(offset) < 8:
            slot = 5 * SHIFTS.index(offset) + jnp.where(is_x, 4 * w, zz + 1 - w)
        else:
            slot = 30 + jnp.where(is_x, 5 * w, 1 + zz)
    return group, jnp.clip(other, 0, GROUPS - 1), valid, slot


def add_bias(st, bias):
    top = jnp.concatenate([st[:BLK, :BLK] + bias[0][0], st[:BLK, BLK:] + bias[0][1]], axis=1)
    low = jnp.concatenate([st[BLK:, :BLK] + bias[1][0], st[BLK:, BLK:] + bias[1][1]], axis=1)
    return jnp.concatenate([top, low], axis=0)


def bias_of(mask, q_group, k_group, valid):
    return [
        [
            jnp.where(valid & (mask[2 * q_group + qb, 2 * k_group + kb] != 0), 0.0, NEG)
            for qb in range(2)
        ]
        for kb in range(2)
    ]


def fetch(parts, pool, sems):
    at = 0
    copies = []
    for n, ref in enumerate(parts):
        copy = pltpu.make_async_copy(ref, pool.at[pl.ds(at, ref.shape[0])], sems.at[n])
        copy.start()
        copies.append(copy)
        at += ref.shape[0]
    for copy in copies:
        copy.wait()


def rows_of(ref, *index):
    return ref[index[0], :, index[1]].reshape(TOK, E)


def unturn(x, tab, z):
    halves = []
    for blk in range(2):
        t = tab[2 * z + blk]
        halves.append(turn(x[blk * BLK : (blk + 1) * BLK], t[0:1], -t[1:2], -t[2:3]))
    return jnp.concatenate(halves, axis=0)


def put(unit, m_ref, x_ref, which, val):
    for b in range(4):
        piece = val[b * QTR : (b + 1) * QTR]

        @pl.when(unit < 4)
        def _():
            m_ref[unit * 4 + b, which] = piece

        @pl.when(unit == 4)
        def _():
            x_ref[b, which] = piece


def query_kernel(pos, mask, tab, *refs):
    parts, qg = refs[:11], refs[11]
    m_ref, x_ref, stats, pool, sems, scores = refs[12:]
    fetch(parts, pool, sems)
    zh, p = pos[0], pos[1]

    def body(unit, carry):
        z = jnp.where(unit == 4, zh, unit)
        own = jnp.where(unit == 4, 0, unit + 1)
        q = rows_of(qg, own, 0)
        g = rows_of(qg, own, 1)
        gt = jnp.transpose(g.astype(F32))
        slots = []
        top = jnp.full((1, TOK), NEG, F32)
        for n, offset in enumerate(OFFSETS):
            group, other, valid, slot = source(offset, unit, zh, p)
            slots.append(slot)
            st = add_bias(dot(rows_of(pool, slot, 0), q, 1, 1), bias_of(mask, group, other, valid))
            scores[n] = st
            top = jnp.maximum(top, jnp.max(st, axis=0, keepdims=True))
        top = top * COEF
        total = jnp.zeros((1, TOK), F32)
        out = jnp.zeros((E, TOK), F32)
        for n in range(len(OFFSETS)):
            w = jnp.exp2(scores[n] * COEF - top)
            scores[n] = w
            total = total + jnp.sum(w, axis=0, keepdims=True)
            out = out + dot(rows_of(pool, slots[n], 1), w.astype(BF16), 0, 0)
        inv = 1.0 / total
        att = (out * inv).astype(BF16)
        delta = jnp.sum(gt * att.astype(F32), axis=0, keepdims=True)
        stats[pl.ds(2 * unit, 1), :] = top + jnp.log2(total)
        stats[pl.ds(2 * unit + 1, 1), :] = delta
        dq = jnp.zeros((E, TOK), F32)
        for n in range(len(OFFSETS)):
            dp = dot(rows_of(pool, slots[n], 1), g, 1, 1)
            ds = (scores[n] * inv * (dp - delta)).astype(BF16)
            dq = dq + dot(rows_of(pool, slots[n], 0), ds, 0, 0)
        put(unit, m_ref, x_ref, 0, jnp.transpose(att.astype(F32)).astype(BF16))
        put(unit, m_ref, x_ref, 1, unturn(jnp.transpose(dq * SCALE), tab, z).astype(BF16))
        return carry

    stats[...] = jnp.zeros_like(stats)
    lax.fori_loop(0, UNITS, body, 0)


def key_kernel(pos, mask, tab, stats, *refs):
    parts, kv = refs[:11], refs[11]
    m_ref, x_ref, pool, sems = refs[12:]
    fetch(parts, pool, sems)
    zh, p = pos[0], pos[1]

    def body(unit, carry):
        is_x = unit == 4
        z = jnp.where(is_x, zh, unit)
        own = jnp.where(is_x, 0, unit + 1)
        k = rows_of(kv, own, 0)
        v = rows_of(kv, own, 1)
        dk = jnp.zeros((TOK, E), F32)
        dv = jnp.zeros((TOK, E), F32)
        for offset in OFFSETS:
            group, other, valid, slot = source(offset, unit, zh, p)
            at = jnp.where(is_x, other, zh * PLANE + lax.rem(other, PLANE))
            row = 2 * jnp.where(is_x, 4, lax.div(other, PLANE))
            total = stats[at, pl.ds(row, 1), :]
            delta = stats[at, pl.ds(row + 1, 1), :]
            q = rows_of(pool, slot, 0)
            g = rows_of(pool, slot, 1)
            st = add_bias(dot(k, q, 1, 1), bias_of(mask, other, group, valid))
            w = jnp.exp2(st * COEF - total)
            ds = (w * (dot(v, g, 1, 1) - delta)).astype(BF16)
            dv = dv + dot(w.astype(BF16), g, 1, 0)
            dk = dk + dot(ds, q, 1, 0)
        put(unit, m_ref, x_ref, 0, unturn(dk * SCALE, tab, z).astype(BF16))
        put(unit, m_ref, x_ref, 1, dv.astype(BF16))
        return carry

    lax.fori_loop(0, UNITS, body, 0)


M_OUT = jax.ShapeDtypeStruct((16, 2, QTR, E), BF16)
X_OUT = jax.ShapeDtypeStruct((4, 2, QTR, E), BF16)


def query_side(pos, mask, tab, parts, qg):
    return pl.pallas_call(
        query_kernel,
        out_shape=(M_OUT, X_OUT, jax.ShapeDtypeStruct((16, TOK), F32)),
        in_specs=[SMEM, SMEM, VMEM] + [ANY] * 11 + [VMEM],
        out_specs=(VMEM, VMEM, VMEM),
        scratch_shapes=[
            pltpu.VMEM((SLOTS, 4, 2, QTR, E), BF16),
            pltpu.SemaphoreType.DMA((11,)),
            pltpu.VMEM((len(OFFSETS), TOK, TOK), F32),
        ],
        compiler_params=pltpu.CompilerParams(vmem_limit_bytes=40 * 2**20),
        cost_estimate=pl.CostEstimate(
            flops=65 * 5 * 2 * TOK * TOK * E, bytes_accessed=8 * 2**20, transcendentals=65 * TOK * TOK
        ),
        name="query_side",
    )(pos, mask, tab, *parts, qg)


def key_side(pos, mask, tab, stats, parts, kv):
    return pl.pallas_call(
        key_kernel,
        out_shape=(M_OUT, X_OUT),
        in_specs=[SMEM, SMEM, VMEM, VMEM] + [ANY] * 11 + [VMEM],
        out_specs=(VMEM, VMEM),
        scratch_shapes=[
            pltpu.VMEM((SLOTS, 4, 2, QTR, E), BF16),
            pltpu.SemaphoreType.DMA((11,)),
        ],
        compiler_params=pltpu.CompilerParams(vmem_limit_bytes=40 * 2**20),
        cost_estimate=pl.CostEstimate(
            flops=65 * 4 * 2 * TOK * TOK * E, bytes_accessed=8 * 2**20, transcendentals=65 * TOK * TOK
        ),
        name="key_side",
    )(pos, mask, tab, stats, *parts, kv)


def tables(block_frame, p):
    inv = np.zeros((E,), np.float32)
    inv[:HALF] = 10000.0 ** (-2.0 * np.arange(HALF, dtype=np.float32) / ROT)
    inv[HALF:ROT] = inv[:HALF]
    first = (np.arange(E) < HALF).astype(np.float32)
    second = ((np.arange(E) >= HALF) & (np.arange(E) < ROT)).astype(np.float32)
    frames = block_frame.reshape(ZG, PLANE, 2)
    frames = lax.dynamic_slice(frames, (0, p, 0), (ZG, 1, 2)).reshape(2 * ZG)
    angles = frames.astype(F32)[:, None] * inv[None]
    sine = jnp.sin(angles)
    zero = jnp.zeros_like(sine)
    return jnp.stack(
        [jnp.cos(angles), sine * second, -sine * first, zero, zero, zero, zero, zero], axis=1
    )


def spread(m, x, p):
    m = lax.all_to_all(m, ("zh", "h"), 0, 0, tiled=True).reshape(4, 4, 2, QTR, E)
    x = lax.all_to_all(x, "h", 0, 0, tiled=True).reshape(1, 4, 2, QTR, E)
    above = lax.ppermute(x, "zh", [(0, 1), (1, 2), (2, 3)])
    below = lax.ppermute(x, "zh", [(1, 0), (2, 1), (3, 2)])
    across = lax.ppermute(x, "zh", [(0, 2), (2, 0), (1, 3), (3, 1)])
    last = jnp.where(p < 8, below, above)
    own = jnp.concatenate([x, m, last], axis=0)
    parts = []
    for s in SHIFTS:
        if s == 8:
            message = own
        else:
            wraps = (p + s < 0) | (p + s >= PLANE)
            message = lax.dynamic_slice_in_dim(own, jnp.where(wraps, 1, 0), 5, axis=0)
        parts.append(lax.ppermute(message, "p", [(i, (i + s) % PLANE) for i in range(PLANE)]))
    return own, parts + [own, above, below, across]


def leave(m, x):
    m = lax.all_to_all(m, ("zh", "h"), 0, 0, tiled=True)
    x = lax.all_to_all(x, "h", 0, 0, tiled=True)
    return unpack(m, x)


def shards(queries, key_vectors, value_vectors, grad_output, block_mask, block_frame):
    zh, p, h = lax.axis_index("zh"), lax.axis_index("p"), lax.axis_index("h")
    pos = jnp.stack([zh, p, h]).astype(jnp.int32)
    tab = tables(block_frame, p)
    km, kx = pack(pos, tab, key_vectors, value_vectors)
    qm, qx = pack(pos, tab, queries, grad_output)
    kv, kv_parts = spread(km, kx, p)
    qg, qg_parts = spread(qm, qx, p)
    am, ax, stats = query_side(pos, block_mask, tab, kv_parts, qg)
    stats = lax.all_gather(stats, ("zh", "p"), axis=0, tiled=False)
    bm, bx = key_side(pos, block_mask, tab, stats, qg_parts, kv)
    attended, grad_q = leave(am, ax)
    grad_k, grad_v = leave(bm, bx)
    return attended, grad_q, grad_k, grad_v


def solution(mesh):
    fine = Mesh(mesh.devices.reshape(ZG, PLANE, 4), ("zh", "p", "h"))
    tok = P(("zh", "p", "h"), None, None)
    return jax.shard_map(
        shards,
        mesh=fine,
        in_specs=(tok, tok, tok, tok, P(), P()),
        out_specs=(tok, tok, tok, tok),
        check_vma=False,
    )
```

time: 500 us -> 324 us (0.65)
  the two profiles are of different devices: /device:TPU:64 before, /device:TPU:1 now
where the time goes in v1:
time: 324 us; the launch traced here: 322 us
  waiting for transfers between devices  141 us (44%)
  starting transfers between devices  88.1 us (27%)
  Pallas kernels  46.1 us (14%)
  blocking collectives  16.7 us (5%)
  local copies, waits for them, and re-layouts  14.9 us (5%)
  between operations  14.3 us (4%)
    ppermute x14, waiting for transfers between devices, spread(): lax.ppermute(message, 'p', [(i, (i + s) % PLANE) for i in range(PLANE)])  63.7 us
    all_gather x1, waiting for transfers between devices, shards(): stats = lax.all_gather(stats, ('zh', 'p'), axis=0, tiled=False)  38.3 us
    ppermute x14, starting transfers between devices, spread(): lax.ppermute(message, 'p', [(i, (i + s) % PLANE) for i in range(PLANE)])  24.8 us
    pallas_call x1, Pallas kernels, query_side(): pl.pallas_call(query_kernel, out_shape=(M_OUT, X_OUT, jax.ShapeDtypeStruc...  21.6 us
    pallas_call x1, Pallas kernels, key_side(): pl.pallas_call(key_kernel, out_shape=(M_OUT, X_OUT), in_specs=[SMEM, SMEM...  20 us
    all_to_all x2, starting transfers between devices, leave(): m = lax.all_to_all(m, ('zh', 'h'), 0, 0, tiled=True)  18.6 us
    all_to_all x2, waiting for transfers between devices, leave(): m = lax.all_to_all(m, ('zh', 'h'), 0, 0, tiled=True)  15.4 us
    all_to_all x2, starting transfers between devices, spread(): lax.all_to_all(m, ('zh', 'h'), 0, 0, tiled=True).reshape(4, 4, 2, QTR, E)  14.5 us
  transfers between devices with their start and end apart: 27, of which 11 were waited for; matrix products, arithmetic and copies ran while one was open for 2% of the time, Pallas kernels for 7%

profile of v1, /device:TPU:1, one launch (start us, length us, event | category | flops | bytes accessed | tf_op | source)
XLA Modules:
  0.0 322.4 jit_solution(10959132022203301370)
XLA Ops:
  8.1 1.2 copy.30.a_ref
  9.7 0.7 copy-done.10
  10.6 1.9 pack.2
  12.5 9.2 %all_to_all.40 = bf16[4,2,64,128]{3,2,1,0:T(8,128)(2,1)S(1)} all-to-all(bf16[4,2,64,128]{3,2,1,0:T(8,128)(2,1)S(1)} %get-tuple-element.17), channel_id=1, replica_groups=mesh['zh'=4,'p'=16,'h'=4] {'h'}, dimensions={0} | all-to-all | bytes 262144 | tf_op jit(solution)/shard_map/all_to_all | solution.py:306
  21.8 7.9 %all-to-all-start.1 = ((bf16[16,2,64,128]{3,2,1,0:T(8,128)(2,1)}), bf16[16,2,64,128]{3,2,1,0:T(8,128)(2,1)S(1)}, u32[]{:S(2)}, u32[]{:S(2)}) async-start(bf16[16,2,64,128]{3,2,1,0:T(8,128)(2,1)} %get-tuple-element.18), calls=%async_computation.1 | async-start | bytes 1048576 | tf_op jit(solution)/shard_map/all_to_all | solution.py:305
  29.7 1.3 collective-permute-start
  31.0 4.9 %collective-permute-start.1 = (bf16[1,4,2,64,128]{4,3,2,1,0:T(8,128)(2,1)S(1)}, bf16[1,4,2,64,128]{4,3,2,1,0:T(8,128)(2,1)S(1)}, u32[]{:S(2)}, u32[]{:S(2)}) collective-permute-start(bf16[1,4,2,64,128]{4,3,2,1,0:T(8,128)(2,1)S(1)} %bitcast.16), channel_id=1, source_target_pairs={{0,64},{64,128},{128,192},{1,65},{65,129},{129,193},{2,66},{66,130... | collective-permute-start | bytes 393224 | tf_op jit(solution)/shard_map/ppermute | solution.py:307
  36.2 0.7 copy-done.8
  37.1 1.9 pack.3
  39.1 10.8 %collective-permute-done.refs_9_ = bf16[1,4,2,64,128]{4,3,2,1,0:T(8,128)(2,1)S(1)} collective-permute-done((bf16[1,4,2,64,128]{4,3,2,1,0:T(8,128)(2,1)S(1)}, bf16[1,4,2,64,128]{4,3,2,1,0:T(8,128)(2,1)S(1)}, u32[]{:S(2)}, u32[]{:S(2)}) %collective-permute-start) | collective-permute-done | bytes 131104 | tf_op jit(solution)/shard_map/ppermute | solution.py:308
  49.9 4.2 %all-to-all-start.2 = ((bf16[4,2,64,128]{3,2,1,0:T(8,128)(2,1)}), bf16[4,2,64,128]{3,2,1,0:T(8,128)(2,1)S(1)}, u32[]{:S(2)}, u32[]{:S(2)}) async-start(bf16[4,2,64,128]{3,2,1,0:T(8,128)(2,1)} %get-tuple-element.19), calls=%async_computation.2 | async-start | bytes 262144 | tf_op jit(solution)/shard_map/all_to_all | solution.py:306
  54.2 2.2 constant_dynamic-slice_fusion.6
  56.4 1.2 collective-permute-start.2
  57.6 3.7 %collective-permute-start.3 = (bf16[5,4,2,64,128]{4,3,2,1,0:T(8,128)(2,1)}, bf16[5,4,2,64,128]{4,3,2,1,0:T(8,128)(2,1)}, u32[]{:S(2)}, u32[]{:S(2)}) collective-permute-start(bf16[5,4,2,64,128]{4,3,2,1,0:T(8,128)(2,1)} %get-tuple-element.52), channel_id=1, source_target_pairs={{0,60},{4,0},{8,4},{12,8},{16,12},{20,16},{24,20},{28,24},{32,28},... | collective-permute-start | bytes 1966088 | tf_op jit(solution)/shard_map/ppermute | solution.py:319
  61.3 6.6 %all-to-all-start.3 = ((bf16[16,2,64,128]{3,2,1,0:T(8,128)(2,1)}), bf16[16,2,64,128]{3,2,1,0:T(8,128)(2,1)}, u32[]{:S(2)}, u32[]{:S(2)}) async-start(bf16[16,2,64,128]{3,2,1,0:T(8,128)(2,1)} %get-tuple-element.20), calls=%async_computation.3 | async-start | bytes 1048576 | tf_op jit(solution)/shard_map/all_to_all | solution.py:305
  67.9 5.4 %collective-permute-start.9 = (bf16[1,4,2,64,128]{4,3,2,1,0:T(8,128)(2,1)S(1)}, bf16[1,4,2,64,128]{4,3,2,1,0:T(8,128)(2,1)S(1)}, u32[]{:S(2)}, u32[]{:S(2)}) collective-permute-start(bf16[1,4,2,64,128]{4,3,2,1,0:T(8,128)(2,1)S(1)} %bitcast.18), channel_id=1, source_target_pairs={{0,128},{128,0},{64,192},{192,64},{1,129},{129,1},{65,193},{193,65... | collective-permute-start | bytes 393224 | tf_op jit(solution)/shard_map/ppermute | solution.py:309
  73.3 1.3 collective-permute-start.10
  74.6 4.9 %collective-permute-start.11 = (bf16[1,4,2,64,128]{4,3,2,1,0:T(8,128)(2,1)S(1)}, bf16[1,4,2,64,128]{4,3,2,1,0:T(8,128)(2,1)S(1)}, u32[]{:S(2)}, u32[]{:S(2)}) collective-permute-start(bf16[1,4,2,64,128]{4,3,2,1,0:T(8,128)(2,1)S(1)} %bitcast.12), channel_id=1, source_target_pairs={{0,64},{64,128},{128,192},{1,65},{65,129},{129,193},{2,66},{66,130... | collective-permute-start | bytes 393224 | tf_op jit(solution)/shard_map/ppermute | solution.py:307
  79.5 8.9 %collective-permute-done.9.refs_10_ = bf16[1,4,2,64,128]{4,3,2,1,0:T(8,128)(2,1)S(1)} collective-permute-done((bf16[1,4,2,64,128]{4,3,2,1,0:T(8,128)(2,1)S(1)}, bf16[1,4,2,64,128]{4,3,2,1,0:T(8,128)(2,1)S(1)}, u32[]{:S(2)}, u32[]{:S(2)}) %collective-permute-start.9) | collective-permute-done | bytes 131104 | tf_op jit(solution)/shard_map/ppermute | solution.py:309
  88.4 1.7 collective-permute-start.8
  90.1 3.5 %collective-permute-done.10.refs_9_ = bf16[1,4,2,64,128]{4,3,2,1,0:T(8,128)(2,1)S(1)} collective-permute-done((bf16[1,4,2,64,128]{4,3,2,1,0:T(8,128)(2,1)S(1)}, bf16[1,4,2,64,128]{4,3,2,1,0:T(8,128)(2,1)S(1)}, u32[]{:S(2)}, u32[]{:S(2)}) %collective-permute-start.10) | collective-permute-done | bytes 131104 | tf_op jit(solution)/shard_map/ppermute | solution.py:308
  93.7 5.1 %collective-permute-start.5 = (bf16[5,4,2,64,128]{4,3,2,1,0:T(8,128)(2,1)}, bf16[5,4,2,64,128]{4,3,2,1,0:T(8,128)(2,1)}, u32[]{:S(2)}, u32[]{:S(2)}) collective-permute-start(bf16[5,4,2,64,128]{4,3,2,1,0:T(8,128)(2,1)} %get-tuple-element.50), channel_id=1, source_target_pairs={{0,56},{4,60},{8,0},{12,4},{16,8},{20,12},{24,16},{28,20},{32,24},... | collective-permute-start | bytes 1966088 | tf_op jit(solution)/shard_map/ppermute | solution.py:319
  98.8 0.8 copy-done.1
  99.6 2.7 collective-permute-start.7
  102.3 1.2 pad_maximum_fusion.1.refs_11_.refs_7_
  103.5 9.5 %collective-permute-done.4.refs_2_ = bf16[5,4,2,64,128]{4,3,2,1,0:T(8,128)(2,1)} collective-permute-done((bf16[5,4,2,64,128]{4,3,2,1,0:T(8,128)(2,1)}, bf16[5,4,2,64,128]{4,3,2,1,0:T(8,128)(2,1)}, u32[]{:S(2)}, u32[]{:S(2)}) %collective-permute-start.4) | collective-permute-done | bytes 655392 | tf_op jit(solution)/shard_map/ppermute | solution.py:319
  113.1 11.6 %collective-permute-done.5.refs_3_ = bf16[5,4,2,64,128]{4,3,2,1,0:T(8,128)(2,1)} collective-permute-done((bf16[5,4,2,64,128]{4,3,2,1,0:T(8,128)(2,1)}, bf16[5,4,2,64,128]{4,3,2,1,0:T(8,128)(2,1)}, u32[]{:S(2)}, u32[]{:S(2)}) %collective-permute-start.5) | collective-permute-done | bytes 655392 | tf_op jit(solution)/shard_map/ppermute | solution.py:319
  124.6 13.0 %collective-permute-done.6.refs_4_ = bf16[5,4,2,64,128]{4,3,2,1,0:T(8,128)(2,1)} collective-permute-done((bf16[5,4,2,64,128]{4,3,2,1,0:T(8,128)(2,1)}, bf16[5,4,2,64,128]{4,3,2,1,0:T(8,128)(2,1)}, u32[]{:S(2)}, u32[]{:S(2)}) %collective-permute-start.6) | collective-permute-done | bytes 655392 | tf_op jit(solution)/shard_map/ppermute | solution.py:319
  137.6 21.6 %query_side.1 = (bf16[16,2,64,128]{3,2,1,0:T(8,128)(2,1)}, bf16[4,2,64,128]{3,2,1,0:T(8,128)(2,1)}, f32[16,256]{1,0:T(8,128)}) custom-call(s32[3]{0:T(128)S(1)} %pad_add_fusion.pos, s32[128,128]{1,0:T(8,128)S(1)} %copy-done.5, f32[8,8,128]{2,1,0:T(8,128)S(1)} %stack.26.tab, bf16[5,4,2,64,128]{4,3,2,1,0:T(8,128)(2,1)S(1)} %copy-done.2, ...), custom_call_target="tpu_custom_call" | custom-call | flops 5452595200 | bytes 8388608 | tf_op jit(solution)/shard_map/query_side/pallas_call | solution.py:252
  159.2 2.2 constant_dynamic-slice_fusion
  161.5 4.8 %collective-permute-start.13 = (bf16[5,4,2,64,128]{4,3,2,1,0:T(8,128)(2,1)}, bf16[5,4,2,64,128]{4,3,2,1,0:T(8,128)(2,1)}, u32[]{:S(2)}, u32[]{:S(2)}) collective-permute-start(bf16[5,4,2,64,128]{4,3,2,1,0:T(8,128)(2,1)} %get-tuple-element.46), channel_id=1, source_target_pairs={{0,60},{4,0},{8,4},{12,8},{16,12},{20,16},{24,20},{28,24},{32,28},... | collective-permute-start | bytes 1966088 | tf_op jit(solution)/shard_map/ppermute | solution.py:319
  167.0 8.0 %all-to-all-start.5 = ((bf16[4,2,64,128]{3,2,1,0:T(8,128)(2,1)}), bf16[4,2,64,128]{3,2,1,0:T(8,128)(2,1)S(1)}, u32[]{:S(2)}, u32[]{:S(2)}) async-start(bf16[4,2,64,128]{3,2,1,0:T(8,128)(2,1)} %get-tuple-element.22), calls=%async_computation.5 | async-start | bytes 262144 | tf_op jit(solution)/shard_map/all_to_all | solution.py:325
  175.0 5.1 %collective-permute-start.15 = (bf16[5,4,2,64,128]{4,3,2,1,0:T(8,128)(2,1)}, bf16[5,4,2,64,128]{4,3,2,1,0:T(8,128)(2,1)}, u32[]{:S(2)}, u32[]{:S(2)}) collective-permute-start(bf16[5,4,2,64,128]{4,3,2,1,0:T(8,128)(2,1)} %get-tuple-element.44), channel_id=1, source_target_pairs={{0,56},{4,60},{8,0},{12,4},{16,8},{20,12},{24,16},{28,20},{32,24},... | collective-permute-start | bytes 1966088 | tf_op jit(solution)/shard_map/ppermute | solution.py:319
  180.1 1.8 collective-permute-done.12.refs_0_
  181.9 26.2 %collective-permute-done.13.refs_1_ = bf16[5,4,2,64,128]{4,3,2,1,0:T(8,128)(2,1)} collective-permute-done((bf16[5,4,2,64,128]{4,3,2,1,0:T(8,128)(2,1)}, bf16[5,4,2,64,128]{4,3,2,1,0:T(8,128)(2,1)}, u32[]{:S(2)}, u32[]{:S(2)}) %collective-permute-start.13) | collective-permute-done | bytes 655392 | tf_op jit(solution)/shard_map/ppermute | solution.py:319
  208.1 13.2 %all-to-all-start.4 = ((bf16[16,2,64,128]{3,2,1,0:T(8,128)(2,1)}), bf16[16,2,64,128]{3,2,1,0:T(8,128)(2,1)S(1)}, u32[]{:S(2)}, u32[]{:S(2)}) async-start(bf16[16,2,64,128]{3,2,1,0:T(8,128)(2,1)} %get-tuple-element.21), calls=%async_computation.4 | async-start | bytes 1048576 | tf_op jit(solution)/shard_map/all_to_all | solution.py:324
  221.3 1.7 collective-permute-done.16.refs_4_
  223.0 38.3 %all-gather.3.cloned.1.call-done = f32[1024,256]{1,0:T(8,128)} async-done(((f32[16,256]{1,0:T(8,128)}), f32[1024,256]{1,0:T(8,128)}) %all-gather.3.cloned.1.call-update) | async-done | bytes 1048592 | tf_op jit(solution)/shard_map/all_gather | solution.py:338
  261.3 1.2 copy-done
  262.5 0.9 copy-done.4
  263.4 20.0 %key_side.1 = (bf16[16,2,64,128]{3,2,1,0:T(8,128)(2,1)}, bf16[4,2,64,128]{3,2,1,0:T(8,128)(2,1)S(1)}) custom-call(s32[3]{0:T(128)S(1)} %pad_add_fusion.pos, s32[128,128]{1,0:T(8,128)S(1)} %copy-done.5, f32[8,8,128]{2,1,0:T(8,128)S(1)} %stack.26.tab, f32[64,16,256]{2,1,0:T(8,128)S(1)} %bitcast.9, bf16[5,4,2,64,128]{4,3,2,1,0:T(8,128)(2,1)} %collective-permute-done.12.refs_0_, ...), custom_call_target="tpu_custom_call" | custom-call | flops 4362076160 | bytes 8388608 | tf_op jit(solution)/shard_map/key_side/pallas_call | solution.py:271
  283.5 7.5 %all_to_all.41.x_ref = bf16[4,2,64,128]{3,2,1,0:T(8,128)(2,1)S(1)} all-to-all(bf16[4,2,64,128]{3,2,1,0:T(8,128)(2,1)S(1)} %get-tuple-element.27), channel_id=1, replica_groups=mesh['zh'=4,'p'=16,'h'=4] {'h'}, dimensions={0} | all-to-all | bytes 262144 | tf_op jit(solution)/shard_map/all_to_all | solution.py:325
  290.9 5.4 %all-to-all-start.6 = ((bf16[16,2,64,128]{3,2,1,0:T(8,128)(2,1)}), bf16[16,2,64,128]{3,2,1,0:T(8,128)(2,1)S(1)}, u32[]{:S(2)}, u32[]{:S(2)}) async-start(bf16[16,2,64,128]{3,2,1,0:T(8,128)(2,1)} %get-tuple-element.26), calls=%async_computation.6 | async-start | bytes 1048576 | tf_op jit(solution)/shard_map/all_to_all | solution.py:324
  296.7 0.8 copy.34
  297.5 0.8 copy.35
  298.3 15.4 %all-to-all-done.6.m_ref = bf16[16,2,64,128]{3,2,1,0:T(8,128)(2,1)S(1)} async-done(((bf16[16,2,64,128]{3,2,1,0:T(8,128)(2,1)}), bf16[16,2,64,128]{3,2,1,0:T(8,128)(2,1)S(1)}, u32[]{:S(2)}, u32[]{:S(2)}) %all-to-all-start.6) | async-done | bytes 524320 | tf_op jit(solution)/shard_map/all_to_all | solution.py:324
  314.0 0.8 copy.36
  314.8 0.8 copy.37
  (64 shorter events, 3.6 us)
Async XLA Ops:
  7.2 0.7 copy-start.9
  8.1 1.3 copy-start.6
  9.7 0.7 copy-start.10
  9.7 0.7 copy-start.11
  9.7 0.7 copy-start.12
  21.8 14.2 %copy-start.7 = (bf16[64,20,128]{2,0,1:T(8,128)(2,1)S(1)}, bf16[64,20,128]{2,0,1:T(8,128)(2,1)}, u32[]{:S(2)}) copy-start(bf16[64,20,128]{2,0,1:T(8,128)(2,1)} %param.9) | copy-start | bytes 983044
  21.8 28.1 %all-to-all-start.1 = ((bf16[16,2,64,128]{3,2,1,0:T(8,128)(2,1)}), bf16[16,2,64,128]{3,2,1,0:T(8,128)(2,1)S(1)}, u32[]{:S(2)}, u32[]{:S(2)}) async-start(bf16[16,2,64,128]{3,2,1,0:T(8,128)(2,1)} %get-tuple-element.18), calls=%async_computation.1 | async-start | bytes 1048576 | tf_op jit(solution)/shard_map/all_to_all | solution.py:305
  29.7 20.2 %collective-permute-start = (bf16[1,4,2,64,128]{4,3,2,1,0:T(8,128)(2,1)S(1)}, bf16[1,4,2,64,128]{4,3,2,1,0:T(8,128)(2,1)S(1)}, u32[]{:S(2)}, u32[]{:S(2)}) collective-permute-start(bf16[1,4,2,64,128]{4,3,2,1,0:T(8,128)(2,1)S(1)} %bitcast.15), channel_id=1, source_target_pairs={{64,0},{128,64},{192,128},{65,1},{129,65},{193,129},{66,2},{130,66... | collective-permute-start | bytes 393224 | tf_op jit(solution)/shard_map/ppermute | solution.py:308
  31.0 18.9 %collective-permute-start.1 = (bf16[1,4,2,64,128]{4,3,2,1,0:T(8,128)(2,1)S(1)}, bf16[1,4,2,64,128]{4,3,2,1,0:T(8,128)(2,1)S(1)}, u32[]{:S(2)}, u32[]{:S(2)}) collective-permute-start(bf16[1,4,2,64,128]{4,3,2,1,0:T(8,128)(2,1)S(1)} %bitcast.16), channel_id=1, source_target_pairs={{0,64},{64,128},{128,192},{1,65},{65,129},{129,193},{2,66},{66,130... | collective-permute-start | bytes 393224 | tf_op jit(solution)/shard_map/ppermute | solution.py:307
  35.9 1.0 copy-start.8
  49.9 11.4 %all-to-all-start.2 = ((bf16[4,2,64,128]{3,2,1,0:T(8,128)(2,1)}), bf16[4,2,64,128]{3,2,1,0:T(8,128)(2,1)S(1)}, u32[]{:S(2)}, u32[]{:S(2)}) async-start(bf16[4,2,64,128]{3,2,1,0:T(8,128)(2,1)} %get-tuple-element.19), calls=%async_computation.2 | async-start | bytes 262144 | tf_op jit(solution)/shard_map/all_to_all | solution.py:306
  56.4 42.4 %collective-permute-start.2 = (bf16[5,4,2,64,128]{4,3,2,1,0:T(8,128)(2,1)}, bf16[5,4,2,64,128]{4,3,2,1,0:T(8,128)(2,1)S(1)}, u32[]{:S(2)}, u32[]{:S(2)}) collective-permute-start(bf16[5,4,2,64,128]{4,3,2,1,0:T(8,128)(2,1)} %get-tuple-element.53), channel_id=1, source_target_pairs={{0,4},{4,8},{8,12},{12,16},{16,20},{20,24},{24,28},{28,32},{32,36}... | collective-permute-start | bytes 1966088 | tf_op jit(solution)/shard_map/ppermute | solution.py:319
  57.6 42.0 %collective-permute-start.3 = (bf16[5,4,2,64,128]{4,3,2,1,0:T(8,128)(2,1)}, bf16[5,4,2,64,128]{4,3,2,1,0:T(8,128)(2,1)}, u32[]{:S(2)}, u32[]{:S(2)}) collective-permute-start(bf16[5,4,2,64,128]{4,3,2,1,0:T(8,128)(2,1)} %get-tuple-element.52), channel_id=1, source_target_pairs={{0,60},{4,0},{8,4},{12,8},{16,12},{20,16},{24,20},{28,24},{32,28},... | collective-permute-start | bytes 1966088 | tf_op jit(solution)/shard_map/ppermute | solution.py:319
  61.3 41.0 %all-to-all-start.3 = ((bf16[16,2,64,128]{3,2,1,0:T(8,128)(2,1)}), bf16[16,2,64,128]{3,2,1,0:T(8,128)(2,1)}, u32[]{:S(2)}, u32[]{:S(2)}) async-start(bf16[16,2,64,128]{3,2,1,0:T(8,128)(2,1)} %get-tuple-element.20), calls=%async_computation.3 | async-start | bytes 1048576 | tf_op jit(solution)/shard_map/all_to_all | solution.py:305
  67.9 193.4 %all-gather.3.cloned.1.call-start = ((), (), s32[]{:S(2)}) async-start(), calls=%async_computation.8 | async-start | bytes 1064960 | tf_op jit(solution)/shard_map/all_gather | solution.py:338
  67.9 20.5 %collective-permute-start.9 = (bf16[1,4,2,64,128]{4,3,2,1,0:T(8,128)(2,1)S(1)}, bf16[1,4,2,64,128]{4,3,2,1,0:T(8,128)(2,1)S(1)}, u32[]{:S(2)}, u32[]{:S(2)}) collective-permute-start(bf16[1,4,2,64,128]{4,3,2,1,0:T(8,128)(2,1)S(1)} %bitcast.18), channel_id=1, source_target_pairs={{0,128},{128,0},{64,192},{192,64},{1,129},{129,1},{65,193},{193,65... | collective-permute-start | bytes 393224 | tf_op jit(solution)/shard_map/ppermute | solution.py:309
  73.3 20.4 %collective-permute-start.10 = (bf16[1,4,2,64,128]{4,3,2,1,0:T(8,128)(2,1)S(1)}, bf16[1,4,2,64,128]{4,3,2,1,0:T(8,128)(2,1)S(1)}, u32[]{:S(2)}, u32[]{:S(2)}) collective-permute-start(bf16[1,4,2,64,128]{4,3,2,1,0:T(8,128)(2,1)S(1)} %bitcast.11), channel_id=1, source_target_pairs={{64,0},{128,64},{192,128},{65,1},{129,65},{193,129},{66,2},{130,66... | collective-permute-start | bytes 393224 | tf_op jit(solution)/shard_map/ppermute | solution.py:308
  74.6 19.1 %collective-permute-start.11 = (bf16[1,4,2,64,128]{4,3,2,1,0:T(8,128)(2,1)S(1)}, bf16[1,4,2,64,128]{4,3,2,1,0:T(8,128)(2,1)S(1)}, u32[]{:S(2)}, u32[]{:S(2)}) collective-permute-start(bf16[1,4,2,64,128]{4,3,2,1,0:T(8,128)(2,1)S(1)} %bitcast.12), channel_id=1, source_target_pairs={{0,64},{64,128},{128,192},{1,65},{65,129},{129,193},{2,66},{66,130... | collective-permute-start | bytes 393224 | tf_op jit(solution)/shard_map/ppermute | solution.py:307
  88.4 49.2 %collective-permute-start.8 = (bf16[6,4,2,64,128]{4,3,2,1,0:T(8,128)(2,1)S(1)}, bf16[6,4,2,64,128]{4,3,2,1,0:T(8,128)(2,1)S(1)}, u32[]{:S(2)}, u32[]{:S(2)}) collective-permute-start(bf16[6,4,2,64,128]{4,3,2,1,0:T(8,128)(2,1)S(1)} %pad_maximum_fusion.refs_7_.refs_11_), channel_id=1, source_target_pairs={{0,32},{4,36},{8,40},{12,44},{16,48},{20,52},{24,56},{28,60},{32,0... | collective-permute-start | bytes 2359304 | tf_op jit(solution)/shard_map/ppermute | solution.py:319
  93.7 19.4 %collective-permute-start.4 = (bf16[5,4,2,64,128]{4,3,2,1,0:T(8,128)(2,1)}, bf16[5,4,2,64,128]{4,3,2,1,0:T(8,128)(2,1)}, u32[]{:S(2)}, u32[]{:S(2)}) collective-permute-start(bf16[5,4,2,64,128]{4,3,2,1,0:T(8,128)(2,1)} %get-tuple-element.51), channel_id=1, source_target_pairs={{0,8},{4,12},{8,16},{12,20},{16,24},{20,28},{24,32},{28,36},{32,40... | collective-permute-start | bytes 1966088 | tf_op jit(solution)/shard_map/ppermute | solution.py:319
  93.7 31.0 %collective-permute-start.5 = (bf16[5,4,2,64,128]{4,3,2,1,0:T(8,128)(2,1)}, bf16[5,4,2,64,128]{4,3,2,1,0:T(8,128)(2,1)}, u32[]{:S(2)}, u32[]{:S(2)}) collective-permute-start(bf16[5,4,2,64,128]{4,3,2,1,0:T(8,128)(2,1)} %get-tuple-element.50), channel_id=1, source_target_pairs={{0,56},{4,60},{8,0},{12,4},{16,8},{20,12},{24,16},{28,20},{32,24},... | collective-permute-start | bytes 1966088 | tf_op jit(solution)/shard_map/ppermute | solution.py:319
  98.8 0.9 copy-start.1
  99.6 38.0 %collective-permute-start.6 = (bf16[5,4,2,64,128]{4,3,2,1,0:T(8,128)(2,1)}, bf16[5,4,2,64,128]{4,3,2,1,0:T(8,128)(2,1)}, u32[]{:S(2)}, u32[]{:S(2)}) collective-permute-start(bf16[5,4,2,64,128]{4,3,2,1,0:T(8,128)(2,1)} %get-tuple-element.49), channel_id=1, source_target_pairs={{0,16},{4,20},{8,24},{12,28},{16,32},{20,36},{24,40},{28,44},{32,4... | collective-permute-start | bytes 1966088 | tf_op jit(solution)/shard_map/ppermute | solution.py:319
  99.6 38.0 %collective-permute-start.7 = (bf16[5,4,2,64,128]{4,3,2,1,0:T(8,128)(2,1)}, bf16[5,4,2,64,128]{4,3,2,1,0:T(8,128)(2,1)}, u32[]{:S(2)}, u32[]{:S(2)}) collective-permute-start(bf16[5,4,2,64,128]{4,3,2,1,0:T(8,128)(2,1)} %get-tuple-element.48), channel_id=1, source_target_pairs={{0,48},{4,52},{8,56},{12,60},{16,0},{20,4},{24,8},{28,12},{32,16},... | collective-permute-start | bytes 1966088 | tf_op jit(solution)/shard_map/ppermute | solution.py:319
  102.3 35.3 %copy-start.2 = (bf16[5,4,2,64,128]{4,3,2,1,0:T(8,128)(2,1)S(1)}, bf16[5,4,2,64,128]{4,3,2,1,0:T(8,128)(2,1)}, u32[]{:S(2)}) copy-start(bf16[5,4,2,64,128]{4,3,2,1,0:T(8,128)(2,1)} %copy-done.1) | copy-start | bytes 1966084
  102.3 35.3 %copy-start.5 = (s32[128,128]{1,0:T(8,128)S(1)}, s32[128,128]{1,0:T(8,128)}, u32[]{:S(2)}) copy-start(s32[128,128]{1,0:T(8,128)} %mask.3) | copy-start | bytes 196612
  161.5 20.4 %collective-permute-start.12 = (bf16[5,4,2,64,128]{4,3,2,1,0:T(8,128)(2,1)}, bf16[5,4,2,64,128]{4,3,2,1,0:T(8,128)(2,1)}, u32[]{:S(2)}, u32[]{:S(2)}) collective-permute-start(bf16[5,4,2,64,128]{4,3,2,1,0:T(8,128)(2,1)} %get-tuple-element.47), channel_id=1, source_target_pairs={{0,4},{4,8},{8,12},{12,16},{16,20},{20,24},{24,28},{28,32},{32,36}... | collective-permute-start | bytes 1966088 | tf_op jit(solution)/shard_map/ppermute | solution.py:319
  161.5 46.6 %collective-permute-start.13 = (bf16[5,4,2,64,128]{4,3,2,1,0:T(8,128)(2,1)}, bf16[5,4,2,64,128]{4,3,2,1,0:T(8,128)(2,1)}, u32[]{:S(2)}, u32[]{:S(2)}) collective-permute-start(bf16[5,4,2,64,128]{4,3,2,1,0:T(8,128)(2,1)} %get-tuple-element.46), channel_id=1, source_target_pairs={{0,60},{4,0},{8,4},{12,8},{16,12},{20,16},{24,20},{28,24},{32,28},... | collective-permute-start | bytes 1966088 | tf_op jit(solution)/shard_map/ppermute | solution.py:319
  166.2 8.8 %collective-permute-start.19 = (bf16[1,4,2,64,128]{4,3,2,1,0:T(8,128)(2,1)S(1)}, bf16[1,4,2,64,128]{4,3,2,1,0:T(8,128)(2,1)S(1)}, u32[]{:S(2)}, u32[]{:S(2)}) collective-permute-start(bf16[1,4,2,64,128]{4,3,2,1,0:T(8,128)(2,1)S(1)} %bitcast.14), channel_id=1, source_target_pairs={{0,128},{128,0},{64,192},{192,64},{1,129},{129,1},{65,193},{193,65... | collective-permute-start | bytes 393224 | tf_op jit(solution)/shard_map/ppermute | solution.py:309
  166.5 56.5 %collective-permute-start.18 = (bf16[6,4,2,64,128]{4,3,2,1,0:T(8,128)(2,1)S(1)}, bf16[6,4,2,64,128]{4,3,2,1,0:T(8,128)(2,1)S(1)}, u32[]{:S(2)}, u32[]{:S(2)}) collective-permute-start(bf16[6,4,2,64,128]{4,3,2,1,0:T(8,128)(2,1)S(1)} %pad_maximum_fusion.1.refs_11_.refs_7_), channel_id=1, source_target_pairs={{0,32},{4,36},{8,40},{12,44},{16,48},{20,52},{24,56},{28,60},{32,0... | collective-permute-start | bytes 2359304 | tf_op jit(solution)/shard_map/ppermute | solution.py:319
  167.0 41.1 %all-to-all-start.5 = ((bf16[4,2,64,128]{3,2,1,0:T(8,128)(2,1)}), bf16[4,2,64,128]{3,2,1,0:T(8,128)(2,1)S(1)}, u32[]{:S(2)}, u32[]{:S(2)}) async-start(bf16[4,2,64,128]{3,2,1,0:T(8,128)(2,1)} %get-tuple-element.22), calls=%async_computation.5 | async-start | bytes 262144 | tf_op jit(solution)/shard_map/all_to_all | solution.py:325
  175.0 46.3 %collective-permute-start.14 = (bf16[5,4,2,64,128]{4,3,2,1,0:T(8,128)(2,1)}, bf16[5,4,2,64,128]{4,3,2,1,0:T(8,128)(2,1)}, u32[]{:S(2)}, u32[]{:S(2)}) collective-permute-start(bf16[5,4,2,64,128]{4,3,2,1,0:T(8,128)(2,1)} %get-tuple-element.45), channel_id=1, source_target_pairs={{0,8},{4,12},{8,16},{12,20},{16,24},{20,28},{24,32},{28,36},{32,40... | collective-permute-start | bytes 1966088 | tf_op jit(solution)/shard_map/ppermute | solution.py:319
  175.0 33.1 %copy-start.3 = (bf16[1,4,2,64,128]{4,3,2,1,0:T(8,128)(2,1)}, bf16[1,4,2,64,128]{4,3,2,1,0:T(8,128)(2,1)S(1)}, u32[]{:S(2)}) copy-start(bf16[1,4,2,64,128]{4,3,2,1,0:T(8,128)(2,1)S(1)} %collective-permute-done.19.refs_10_) | copy-start | bytes 393220
  175.0 46.3 %collective-permute-start.15 = (bf16[5,4,2,64,128]{4,3,2,1,0:T(8,128)(2,1)}, bf16[5,4,2,64,128]{4,3,2,1,0:T(8,128)(2,1)}, u32[]{:S(2)}, u32[]{:S(2)}) collective-permute-start(bf16[5,4,2,64,128]{4,3,2,1,0:T(8,128)(2,1)} %get-tuple-element.44), channel_id=1, source_target_pairs={{0,56},{4,60},{8,0},{12,4},{16,8},{20,12},{24,16},{28,20},{32,24},... | collective-permute-start | bytes 1966088 | tf_op jit(solution)/shard_map/ppermute | solution.py:319
  181.9 41.1 %collective-permute-start.16 = (bf16[5,4,2,64,128]{4,3,2,1,0:T(8,128)(2,1)}, bf16[5,4,2,64,128]{4,3,2,1,0:T(8,128)(2,1)}, u32[]{:S(2)}, u32[]{:S(2)}) collective-permute-start(bf16[5,4,2,64,128]{4,3,2,1,0:T(8,128)(2,1)} %get-tuple-element.43), channel_id=1, source_target_pairs={{0,16},{4,20},{8,24},{12,28},{16,32},{20,36},{24,40},{28,44},{32,4... | collective-permute-start | bytes 1966088 | tf_op jit(solution)/shard_map/ppermute | solution.py:319
  208.1 14.9 %collective-permute-start.17 = (bf16[5,4,2,64,128]{4,3,2,1,0:T(8,128)(2,1)}, bf16[5,4,2,64,128]{4,3,2,1,0:T(8,128)(2,1)}, u32[]{:S(2)}, u32[]{:S(2)}) collective-permute-start(bf16[5,4,2,64,128]{4,3,2,1,0:T(8,128)(2,1)} %get-tuple-element.42), channel_id=1, source_target_pairs={{0,48},{4,52},{8,56},{12,60},{16,0},{20,4},{24,8},{28,12},{32,16},... | collective-permute-start | bytes 1966088 | tf_op jit(solution)/shard_map/ppermute | solution.py:319
  208.1 75.3 %all-to-all-start.4 = ((bf16[16,2,64,128]{3,2,1,0:T(8,128)(2,1)}), bf16[16,2,64,128]{3,2,1,0:T(8,128)(2,1)S(1)}, u32[]{:S(2)}, u32[]{:S(2)}) async-start(bf16[16,2,64,128]{3,2,1,0:T(8,128)(2,1)} %get-tuple-element.21), calls=%async_computation.4 | async-start | bytes 1048576 | tf_op jit(solution)/shard_map/all_to_all | solution.py:324
  261.3 1.2 copy-start
  262.5 0.9 copy-start.4
  290.9 22.8 %all-to-all-start.6 = ((bf16[16,2,64,128]{3,2,1,0:T(8,128)(2,1)}), bf16[16,2,64,128]{3,2,1,0:T(8,128)(2,1)S(1)}, u32[]{:S(2)}, u32[]{:S(2)}) async-start(bf16[16,2,64,128]{3,2,1,0:T(8,128)(2,1)} %get-tuple-element.26), calls=%async_computation.6 | async-start | bytes 1048576 | tf_op jit(solution)/shard_map/all_to_all | solution.py:324
Sparse Core Ops, SparseCore 0:
  159.3 101.8 all-gather.2

commit v2 on v1

v2 whole, which is shorter than its diff:
```python
import functools
import math

import jax
import jax.numpy as jnp
import numpy as np
from jax import lax
from jax.experimental import pallas as pl
from jax.experimental.pallas import tpu as pltpu
from jax.sharding import Mesh, PartitionSpec as P

ROT = 44
HALF = ROT // 2
BLK = 128
E = 128
TOK = 256
QTR = 64
GROUPS = 64
PLANE = 16
ZG = 4
UNITS = 5
NEG = -1e30
PARTS = 8
BASES = (0, 6, 12, 18, 24, 30, 36, 41)
OFFSETS = (0, 1, -1, 2, -2, 4, -4, 8, -8, 16, -16, 32, -32)
SLOTS = 46
SCALE = 1.0 / math.sqrt(E)
LOG2E = 1.4426950408889634
COEF = SCALE * LOG2E
F32 = jnp.float32
BF16 = jnp.bfloat16
ANY = pl.BlockSpec(memory_space=pl.ANY)
SMEM = pl.BlockSpec(memory_space=pltpu.SMEM)
VMEM = pl.BlockSpec(memory_space=pltpu.VMEM)

M_OUT = jax.ShapeDtypeStruct((16, 2, QTR, E), BF16)
X_OUT = jax.ShapeDtypeStruct((4, 2, QTR, E), BF16)
WIDE = jax.ShapeDtypeStruct((16, 2, 2, QTR, E), BF16)
SUMS = jax.ShapeDtypeStruct((UNITS, 2, TOK, E), F32)


def dot(a, b, ca, cb):
    return lax.dot_general(a, b, (((ca,), (cb,)), ((), ())), preferred_element_type=F32)


def turn(x, c, s1, s2):
    return x * c + pltpu.roll(x, HALF, x.ndim - 1) * s1 + pltpu.roll(x, E - HALF, x.ndim - 1) * s2


def pack_kernel(pos, tab, a_ref, b_ref, o_ref):
    t = tab[2 * pos[0] + pos[2] // 2]
    a = turn(a_ref[...].astype(F32), t[0:1][None], t[1:2][None], t[2:3][None]).astype(BF16)
    for n, val in ((0, a), (1, b_ref[...])):
        o_ref[:, 0, n] = val[:16]
        for i in range(4):
            o_ref[4 * i : 4 * i + 4, 1, n] = val[16:]


def pack(pos, tab, *tensors):
    return pl.pallas_call(
        pack_kernel,
        out_shape=WIDE,
        in_specs=[SMEM, VMEM, VMEM, VMEM],
        out_specs=VMEM,
        compiler_params=pltpu.CompilerParams(vmem_limit_bytes=40 * 2**20),
        name="pack",
    )(pos, tab, *[jnp.transpose(t, (1, 0, 2)) for t in tensors])


def unpack_kernel(m_ref, x_ref, a_ref, b_ref):
    for i, o in ((0, a_ref), (1, b_ref)):
        o[:16] = m_ref[:, i]
        o[16:] = x_ref[:, i]


def unpack(m, x):
    shape = jax.ShapeDtypeStruct((20, QTR, E), BF16)
    a, b = pl.pallas_call(
        unpack_kernel,
        out_shape=(shape, shape),
        in_specs=[VMEM, VMEM],
        out_specs=(VMEM, VMEM),
        compiler_params=pltpu.CompilerParams(vmem_limit_bytes=40 * 2**20),
        name="unpack",
    )(m, x)
    return jnp.transpose(a, (1, 0, 2)), jnp.transpose(b, (1, 0, 2))


def source(offset, unit, zh, p):
    is_x = unit == 4
    z = jnp.where(is_x, zh, unit)
    group = z * PLANE + p
    other = group - offset
    valid = (other >= 0) & (other < GROUPS)
    if local(offset):
        slot = jnp.clip(z - offset // PLANE, 0, ZG - 1)
    else:
        x = lax.rem(p, 4)
        up, down, eight, across, first, second, left, right = BASES
        base = {
            4: lambda: up,
            -4: lambda: down,
            8: lambda: eight,
            -8: lambda: eight,
            1: lambda: jnp.where(x == 0, first, left),
            -1: lambda: jnp.where(x == 3, first, right),
            2: lambda: jnp.where(x == 0, second, jnp.where(x == 1, first, across)),
            -2: lambda: jnp.where(x == 3, second, jnp.where(x == 2, first, across)),
        }[offset]()
        at = p - offset
        step = jnp.where(at < 0, -1, jnp.where(at >= PLANE, 1, 0))
        zz = jnp.clip(z + step, 0, ZG - 1)
        slot = base + jnp.where(is_x, 5 * step * step, 1 + zz)
    return group, jnp.clip(other, 0, GROUPS - 1), valid, slot


def local(offset):
    return offset == 0 or abs(offset) >= PLANE


def add_bias(st, bias):
    top = jnp.concatenate([st[:BLK, :BLK] + bias[0][0], st[:BLK, BLK:] + bias[0][1]], axis=1)
    low = jnp.concatenate([st[BLK:, :BLK] + bias[1][0], st[BLK:, BLK:] + bias[1][1]], axis=1)
    return jnp.concatenate([top, low], axis=0)


def bias_of(mask, q_group, k_group, valid):
    return [
        [
            jnp.where(valid & (mask[2 * q_group + qb, 2 * k_group + kb] != 0), 0.0, NEG)
            for qb in range(2)
        ]
        for kb in range(2)
    ]


def fetch(parts, pool, sems, first):
    at = 0
    copies = []
    for n, ref in enumerate(parts):
        copy = pltpu.make_async_copy(ref, pool.at[pl.ds(at, ref.shape[0])], sems.at[first + n])
        copy.start()
        copies.append(copy)
        at += ref.shape[0]
    return copies


def near(ref, z, unit, which):
    return ref[z, :, jnp.where(unit == 4, 1, 0), which].reshape(TOK, E)


def far(ref, slot, which):
    return ref[slot, :, which].reshape(TOK, E)


def unturn(x, tab, z):
    halves = []
    for blk in range(2):
        t = tab[2 * z + blk]
        halves.append(turn(x[blk * BLK : (blk + 1) * BLK], t[0:1], -t[1:2], -t[2:3]))
    return jnp.concatenate(halves, axis=0)


def put(unit, m_ref, x_ref, which, val):
    for b in range(4):
        piece = val[b * QTR : (b + 1) * QTR]

        @pl.when(unit < 4)
        def _():
            m_ref[unit * 4 + b, which] = piece

        @pl.when(unit == 4)
        def _():
            x_ref[b, which] = piece


def query_kernel(pos, mask, tab, kv, qg, *refs):
    parts = refs[:PARTS]
    m_ref, x_ref, stats, pool, sems, scores = refs[PARTS:]
    copies = fetch(parts, pool, sems, 0)
    for copy in copies:
        copy.wait()
    zh, p = pos[0], pos[1]

    def body(unit, carry):
        z = jnp.where(unit == 4, zh, unit)
        q = near(qg, z, unit, 0)
        g = near(qg, z, unit, 1)
        gt = jnp.transpose(g.astype(F32))
        slots = []
        top = jnp.full((1, TOK), NEG, F32)

        def take(n, which):
            if local(OFFSETS[n]):
                return near(kv, slots[n], unit, which)
            return far(pool, slots[n], which)

        for n, offset in enumerate(OFFSETS):
            group, other, valid, slot = source(offset, unit, zh, p)
            slots.append(slot)
            st = add_bias(dot(take(n, 0), q, 1, 1), bias_of(mask, group, other, valid))
            scores[n] = st
            top = jnp.maximum(top, jnp.max(st, axis=0, keepdims=True))
        top = top * COEF
        total = jnp.zeros((1, TOK), F32)
        out = jnp.zeros((E, TOK), F32)
        for n in range(len(OFFSETS)):
            w = jnp.exp2(scores[n] * COEF - top)
            scores[n] = w
            total = total + jnp.sum(w, axis=0, keepdims=True)
            out = out + dot(take(n, 1), w.astype(BF16), 0, 0)
        inv = 1.0 / total
        att = (out * inv).astype(BF16)
        delta = jnp.sum(gt * att.astype(F32), axis=0, keepdims=True)
        stats[pl.ds(2 * unit, 1), :] = top + jnp.log2(total)
        stats[pl.ds(2 * unit + 1, 1), :] = delta
        dq = jnp.zeros((E, TOK), F32)
        for n in range(len(OFFSETS)):
            dp = dot(take(n, 1), g, 1, 1)
            ds = (scores[n] * inv * (dp - delta)).astype(BF16)
            dq = dq + dot(take(n, 0), ds, 0, 0)
        put(unit, m_ref, x_ref, 0, jnp.transpose(att.astype(F32)).astype(BF16))
        put(unit, m_ref, x_ref, 1, unturn(jnp.transpose(dq * SCALE), tab, z).astype(BF16))
        return carry

    stats[...] = jnp.zeros_like(stats)
    lax.fori_loop(0, UNITS, body, 0)


def key_terms(offsets, zh, p, mask, unit, kv, take, dk, dv):
    is_x = unit == 4
    z = jnp.where(is_x, zh, unit)
    k = near(kv, z, unit, 0)
    v = near(kv, z, unit, 1)
    for offset in offsets:
        group, other, valid, slot = source(offset, unit, zh, p)
        row = 2 * (lax.div(other, PLANE) + jnp.where(is_x, ZG, 0))
        q, g, total, delta = take(offset, slot, lax.rem(other, PLANE), row)
        st = add_bias(dot(k, q, 1, 1), bias_of(mask, other, group, valid))
        w = jnp.exp2(st * COEF - total)
        ds = (w * (dot(v, g, 1, 1) - delta)).astype(BF16)
        dv = dv + dot(w.astype(BF16), g, 1, 0)
        dk = dk + dot(ds, q, 1, 0)
    return dk, dv


def near_key_kernel(pos, mask, kv, qg, stats, sums):
    zh, p = pos[0], pos[1]

    def body(unit, carry):
        def take(offset, z, at, row):
            total = stats[pl.ds(row, 1), :]
            return near(qg, z, unit, 0), near(qg, z, unit, 1), total, stats[pl.ds(row + 1, 1), :]

        zero = jnp.zeros((TOK, E), F32)
        offsets = [o for o in OFFSETS if local(o)]
        dk, dv = key_terms(offsets, zh, p, mask, unit, kv, take, zero, zero)
        sums[unit, 0] = dk
        sums[unit, 1] = dv
        return carry

    lax.fori_loop(0, UNITS, body, 0)


def far_key_kernel(pos, mask, tab, kv, sums, stats, *refs):
    m_ref, x_ref, pool, sems = refs[PARTS:]
    for copy in fetch(refs[:PARTS], pool, sems, 0):
        copy.wait()
    zh, p = pos[0], pos[1]

    def body(unit, carry):
        def take(offset, slot, at, row):
            total = stats[at, pl.ds(row, 1), :]
            return far(pool, slot, 0), far(pool, slot, 1), total, stats[at, pl.ds(row + 1, 1), :]

        offsets = [o for o in OFFSETS if not local(o)]
        dk, dv = key_terms(
            offsets, zh, p, mask, unit, kv, take, sums[unit, 0], sums[unit, 1]
        )
        z = jnp.where(unit == 4, zh, unit)
        put(unit, m_ref, x_ref, 0, unturn(dk * SCALE, tab, z).astype(BF16))
        put(unit, m_ref, x_ref, 1, dv.astype(BF16))
        return carry

    lax.fori_loop(0, UNITS, body, 0)


def cost(pairs, products):
    return pl.CostEstimate(
        flops=pairs * products * 2 * TOK * TOK * E,
        bytes_accessed=8 * 2**20,
        transcendentals=pairs * TOK * TOK,
    )


LIMIT = pltpu.CompilerParams(vmem_limit_bytes=40 * 2**20)


def query_side(pos, mask, tab, kv, qg, parts):
    return pl.pallas_call(
        query_kernel,
        out_shape=(M_OUT, X_OUT, jax.ShapeDtypeStruct((16, TOK), F32)),
        in_specs=[SMEM, SMEM, VMEM, VMEM, VMEM] + [ANY] * PARTS,
        out_specs=(VMEM, VMEM, VMEM),
        scratch_shapes=[
            pltpu.VMEM((SLOTS, 4, 2, QTR, E), BF16),
            pltpu.SemaphoreType.DMA((PARTS,)),
            pltpu.VMEM((len(OFFSETS), TOK, TOK), F32),
        ],
        compiler_params=LIMIT,
        cost_estimate=cost(65, 5),
        name="query_side",
    )(pos, mask, tab, kv, qg, *parts)


def near_key_side(pos, mask, kv, qg, stats):
    return pl.pallas_call(
        near_key_kernel,
        out_shape=SUMS,
        in_specs=[SMEM, SMEM, VMEM, VMEM, VMEM],
        out_specs=VMEM,
        compiler_params=LIMIT,
        cost_estimate=cost(25, 4),
        name="near_key_side",
    )(pos, mask, kv, qg, stats)


def far_key_side(pos, mask, tab, kv, sums, stats, parts):
    return pl.pallas_call(
        far_key_kernel,
        out_shape=(M_OUT, X_OUT),
        in_specs=[SMEM, SMEM, VMEM, VMEM, VMEM, VMEM] + [ANY] * PARTS,
        out_specs=(VMEM, VMEM),
        scratch_shapes=[
            pltpu.VMEM((SLOTS, 4, 2, QTR, E), BF16),
            pltpu.SemaphoreType.DMA((PARTS,)),
        ],
        compiler_params=LIMIT,
        cost_estimate=cost(40, 4),
        name="far_key_side",
    )(pos, mask, tab, kv, sums, stats, *parts)


def tables(block_frame, p):
    inv = np.zeros((E,), np.float32)
    inv[:HALF] = 10000.0 ** (-2.0 * np.arange(HALF, dtype=np.float32) / ROT)
    inv[HALF:ROT] = inv[:HALF]
    first = (np.arange(E) < HALF).astype(np.float32)
    second = ((np.arange(E) >= HALF) & (np.arange(E) < ROT)).astype(np.float32)
    frames = block_frame.reshape(ZG, PLANE, 2)
    frames = lax.dynamic_slice(frames, (0, p, 0), (ZG, 1, 2)).reshape(2 * ZG)
    angles = frames.astype(F32)[:, None] * inv[None]
    sine = jnp.sin(angles)
    zero = jnp.zeros_like(sine)
    return jnp.stack(
        [jnp.cos(angles), sine * second, -sine * first, zero, zero, zero, zero, zero], axis=1
    )


def move(value, rule):
    pairs = []
    for y in range(4):
        for x in range(4):
            to = rule(x, y)
            if to is not None:
                pairs.append((4 * y + x, 4 * (to[1] % 4) + to[0] % 4))
    return lax.ppermute(value, "p", pairs)


def start_exchange(own):
    across = move(own, lambda x, y: (x + 2, y))
    up = move(own, lambda x, y: (x, y + 1))
    down = move(own, lambda x, y: (x, y - 1))
    left = move(own[:5], lambda x, y: (x + 1, y) if x < 3 else None)
    right = move(own[:5], lambda x, y: (x - 1, y) if x > 0 else None)
    return up, down, across, left, right


def end_exchange(up, down, across, left, right, p):
    x = lax.rem(p, 4)
    turned = jnp.where(x < 2, down, up)
    eight = move(turned, lambda x, y: (x, y - 1) if x < 2 else (x, y + 1))
    first = move(
        jnp.where((x == 0) | (x == 3), turned, across),
        lambda x, y: ((3, y), (1, y + 1), (2, y - 1), (0, y))[x],
    )
    second = move(across, lambda x, y: ((0, y + 1), None, None, (3, y - 1))[x])
    return up, down, eight, across, first, second, left, right


def slots_of(m, x, zh, p):
    first = lax.dynamic_slice_in_dim(x, zh, 1, axis=0)
    wrap = jnp.clip(zh + jnp.where(p < 8, 1, -1), 0, ZG - 1)
    return jnp.concatenate([first, m, lax.dynamic_slice_in_dim(x, wrap, 1, axis=0)], axis=0)


def gather_heads(packed):
    wide = lax.all_to_all(packed, ("zh", "h"), 0, 0, tiled=True)
    return wide.reshape(4, 4, 2, 2, QTR, E)


def leave(m, x):
    m = lax.all_to_all(m, ("zh", "h"), 0, 0, tiled=True)
    x = lax.all_to_all(x, "h", 0, 0, tiled=True)
    return unpack(m, x)


def shards(queries, key_vectors, value_vectors, grad_output, block_mask, block_frame):
    zh, p, h = lax.axis_index("zh"), lax.axis_index("p"), lax.axis_index("h")
    pos = jnp.stack([zh, p, h]).astype(jnp.int32)
    tab = tables(block_frame, p)
    kv = gather_heads(pack(pos, tab, key_vectors, value_vectors))
    qg = gather_heads(pack(pos, tab, queries, grad_output))
    kv_first = start_exchange(slots_of(kv[:, :, 0], kv[:, :, 1], zh, p))
    kv_parts = end_exchange(*kv_first, p)
    qg_own = slots_of(qg[:, :, 0], qg[:, :, 1], zh, p)
    qg_own, kv_some = lax.optimization_barrier((qg_own, kv_first[:3]))
    qg_first = start_exchange(qg_own)
    am, ax, stats = query_side(pos, block_mask, tab, kv, qg, kv_parts)
    xs = jnp.broadcast_to(stats[None, 8:10], (4, 2, TOK))
    xs = lax.all_to_all(xs, "zh", 0, 0, tiled=True).reshape(8, TOK)
    stats = jnp.concatenate([stats[:8], xs], axis=0)
    every = lax.all_to_all(
        jnp.broadcast_to(stats[None], (PLANE, 16, TOK)), "p", 0, 0, tiled=True
    )
    qg_first, am = lax.optimization_barrier((qg_first, am))
    qg_parts = end_exchange(*qg_first, p)
    sums = near_key_side(pos, block_mask, kv, qg, stats)
    attended, grad_q = leave(am, ax)
    sums, attended, grad_q = lax.optimization_barrier((sums, attended, grad_q))
    bm, bx = far_key_side(pos, block_mask, tab, kv, sums, every, qg_parts)
    grad_k, grad_v = leave(bm, bx)
    return attended, grad_q, grad_k, grad_v


def solution(mesh):
    fine = Mesh(mesh.devices.reshape(ZG, PLANE, 4), ("zh", "p", "h"))
    tok = P(("zh", "p", "h"), None, None)
    return jax.shard_map(
        shards,
        mesh=fine,
        in_specs=(tok, tok, tok, tok, P(), P()),
        out_specs=(tok, tok, tok, tok),
        check_vma=False,
    )
```

time: 324 us -> 244 us (0.75)
  waiting for transfers between devices: 141 us -> 68 us
  starting transfers between devices: 88.1 us -> 58.9 us
  blocking collectives: 16.7 us -> 40.3 us
  between operations: 14.3 us -> 1.01 us
  other arithmetic: 1.57 us -> 9.46 us
    ppermute x20 -> x16, waiting for transfers between devices: 87 us -> 31.1 us  [move(): return lax.ppermute(value, 'p', pairs)]
    all_gather x1 -> x0, waiting for transfers between devices: 38.3 us -> none  [shards(): stats = lax.all_gather(stats, ('zh', 'p'), axis=0, tiled=False)]
    all_to_all x3, waiting for transfers between devices: 0.01 us -> 26.1 us  [the longest x2 26.1 us: gather_heads(): wide = lax.all_to_all(packed, ('zh', 'h'), 0, 0, tiled=True)]
    all_to_all x1 -> x2, blocking collectives: 9.21 us -> 35.2 us  [the longest x1 22.8 us: leave(): m = lax.all_to_all(m, ('zh', 'h'), 0, 0, tiled=True)]
    ppermute x20 -> x16, starting transfers between devices: 42.8 us -> 25.6 us  [move(): return lax.ppermute(value, 'p', pairs)]
    all_to_all x2 -> x1, starting transfers between devices: 18.6 us -> 4.58 us  [leave(): m = lax.all_to_all(m, ('zh', 'h'), 0, 0, tiled=True)]
    all_to_all x2 -> x1, waiting for transfers between devices: 15.4 us -> 7.27 us  [leave(): m = lax.all_to_all(m, ('zh', 'h'), 0, 0, tiled=True)]
    select_n x2, other arithmetic: 0.03 us -> 4.91 us  [end_exchange(): jnp.where((x == 0) | (x == 3), turned, across)]
  transfers between devices with their start and end apart: 27 -> 21, of which waited for: 11 -> 7; matrix products, arithmetic and copies ran while one was open for 2% -> 6% of each run, Pallas kernels for 7% -> 13%
where the time goes in v2:
time: 244 us; the launch traced here: 243 us
  waiting for transfers between devices  68 us (28%)
  starting transfers between devices  58.9 us (24%)
  Pallas kernels  48.9 us (20%)
  blocking collectives  40.3 us (17%)
  local copies, waits for them, and re-layouts  16.5 us (7%)
  other arithmetic  9.46 us (4%)
    ppermute x16, waiting for transfers between devices, move(): return lax.ppermute(value, 'p', pairs)  31.1 us
    all_to_all x2, waiting for transfers between devices, gather_heads(): wide = lax.all_to_all(packed, ('zh', 'h'), 0, 0, tiled=True)  26.1 us
    ppermute x16, starting transfers between devices, move(): return lax.ppermute(value, 'p', pairs)  25.6 us
    all_to_all x1, blocking collectives, leave(): m = lax.all_to_all(m, ('zh', 'h'), 0, 0, tiled=True)  22.8 us
    pallas_call x1, Pallas kernels, query_side(): pl.pallas_call(query_kernel, out_shape=(M_OUT, X_OUT, jax.ShapeDtypeStruc...  21.6 us
    pallas_call x1, Pallas kernels, far_key_side(): pl.pallas_call(far_key_kernel, out_shape=(M_OUT, X_OUT), in_specs=[SMEM,...  14.5 us
    all_to_all x2, starting transfers between devices, gather_heads(): wide = lax.all_to_all(packed, ('zh', 'h'), 0, 0, tiled=True)  13.7 us
    all_to_all x1, blocking collectives, shards(): xs = lax.all_to_all(xs, 'zh', 0, 0, tiled=True).reshape(8, TOK)  12.3 us
  transfers between devices with their start and end apart: 21, of which 7 were waited for; matrix products, arithmetic and copies ran while one was open for 6% of the time, Pallas kernels for 13%

profile of v2, /device:TPU:1, one launch (start us, length us, event | category | flops | bytes accessed | tf_op | source)
XLA Modules:
  0.0 243.1 jit_solution(4994887016159374188)
XLA Ops:
  2.6 1.0 copy-done.3
  3.6 1.0 copy-done.4
  4.6 1.8 pack.2
  6.4 10.1 %all-to-all-start = ((bf16[16,2,2,64,128]{4,3,2,1,0:T(8,128)(2,1)}), bf16[16,2,2,64,128]{4,3,2,1,0:T(8,128)(2,1)S(1)}, u32[]{:S(2)}, u32[]{:S(2)}) async-start(bf16[16,2,2,64,128]{4,3,2,1,0:T(8,128)(2,1)} %pack.2), calls=%async_computation | async-start | bytes 2097152 | tf_op jit(solution)/shard_map/all_to_all | solution.py:398
  16.5 1.8 pack.3
  18.4 26.1 %all-to-all-done = bf16[16,2,2,64,128]{4,3,2,1,0:T(8,128)(2,1)S(1)} async-done(((bf16[16,2,2,64,128]{4,3,2,1,0:T(8,128)(2,1)}), bf16[16,2,2,64,128]{4,3,2,1,0:T(8,128)(2,1)S(1)}, u32[]{:S(2)}, u32[]{:S(2)}) %all-to-all-start) | async-done | bytes 1048608 | tf_op jit(solution)/shard_map/all_to_all | solution.py:398
  44.4 3.6 %all-to-all-start.1 = ((bf16[16,2,2,64,128]{4,3,2,1,0:T(8,128)(2,1)}), bf16[16,2,2,64,128]{4,3,2,1,0:T(8,128)(2,1)S(1)}, u32[]{:S(2)}, u32[]{:S(2)}) async-start(bf16[16,2,2,64,128]{4,3,2,1,0:T(8,128)(2,1)} %pack.3), calls=%async_computation.1 | async-start | bytes 2097152 | tf_op jit(solution)/shard_map/all_to_all | solution.py:398
  48.9 1.0 pad_maximum_fusion
  49.9 1.3 collective-permute-start
  51.2 1.4 collective-permute-start.1
  52.6 2.7 %collective-permute-start.3 = (bf16[6,4,2,64,128]{4,3,2,1,0:T(8,128)(2,1)}, bf16[6,4,2,64,128]{4,3,2,1,0:T(8,128)(2,1)}, u32[]{:S(2)}, u32[]{:S(2)}) collective-permute-start(bf16[6,4,2,64,128]{4,3,2,1,0:T(8,128)(2,1)} %pad_maximum_fusion), channel_id=1, source_target_pairs={{0,8},{4,12},{8,0},{12,4},{16,24},{20,28},{24,16},{28,20},{32,40},... | collective-permute-start | bytes 2359304 | tf_op jit(solution)/shard_map/ppermute | solution.py:367
  55.3 15.3 %collective-permute-done.refs_0_ = bf16[6,4,2,64,128]{4,3,2,1,0:T(8,128)(2,1)S(1)} collective-permute-done((bf16[6,4,2,64,128]{4,3,2,1,0:T(8,128)(2,1)}, bf16[6,4,2,64,128]{4,3,2,1,0:T(8,128)(2,1)S(1)}, u32[]{:S(2)}, u32[]{:S(2)}) %collective-permute-start) | collective-permute-done | bytes 786464 | tf_op jit(solution)/shard_map/ppermute | solution.py:367
  70.6 2.3 collective-permute-done.3.refs_3_
  72.9 2.5 %broadcast_select_fusion.1 = (bf16[6,4,2,64,128]{4,3,2,1,0:T(8,128)(2,1)}, bf16[6,4,2,64,128]{4,3,2,1,0:T(8,128)(2,1)}) fusion(bf16[6,4,2,64,128]{4,3,2,1,0:T(8,128)(2,1)} %collective-permute-done.3.refs_3_, pred[]{:T(512)S(6)} %or.4, bf16[6,4,2,64,128]{4,3,2,1,0:T(8,128)(2,1)} %collective-permute-done.1.refs_1_, ...), kind=kLoop, calls=%fused_computation.3 | loop fusion | flops 786432 | bytes 3932162 | tf_op jit(solution)/shard_map/jit(_where)/select_n | solution.py:384
  75.4 1.4 collective-permute-start.2
  76.8 3.1 %collective-permute-start.5 = (bf16[6,4,2,64,128]{4,3,2,1,0:T(8,128)(2,1)}, bf16[6,4,2,64,128]{4,3,2,1,0:T(8,128)(2,1)}, u32[]{:S(2)}, u32[]{:S(2)}) collective-permute-start(bf16[6,4,2,64,128]{4,3,2,1,0:T(8,128)(2,1)} %collective-permute-done.3.refs_3_), channel_id=1, source_target_pairs={{0,16},{12,60},{16,32},{28,12},{32,48},{44,28},{48,0},{60,44},{1,1... | collective-permute-start | bytes 2359304 | tf_op jit(solution)/shard_map/ppermute | solution.py:367
  79.9 0.9 pad_maximum_fusion.2
  80.9 1.9 collective-permute-start.6
  82.8 1.3 collective-permute-start.7
  84.3 1.0 pad_maximum_fusion.1
  85.3 9.8 %collective-permute-done.6.refs_6_ = bf16[5,4,2,64,128]{4,3,2,1,0:T(8,128)(2,1)S(1)} collective-permute-done((bf16[5,4,2,64,128]{4,3,2,1,0:T(8,128)(2,1)}, bf16[5,4,2,64,128]{4,3,2,1,0:T(8,128)(2,1)S(1)}, u32[]{:S(2)}, u32[]{:S(2)}) %collective-permute-start.6) | collective-permute-done | bytes 655392 | tf_op jit(solution)/shard_map/ppermute | solution.py:367
  96.3 3.7 %collective-permute-done.7.refs_7_ = bf16[5,4,2,64,128]{4,3,2,1,0:T(8,128)(2,1)} collective-permute-done((bf16[5,4,2,64,128]{4,3,2,1,0:T(8,128)(2,1)}, bf16[5,4,2,64,128]{4,3,2,1,0:T(8,128)(2,1)}, u32[]{:S(2)}, u32[]{:S(2)}) %collective-permute-start.7) | collective-permute-done | bytes 655392 | tf_op jit(solution)/shard_map/ppermute | solution.py:367
  99.9 1.6 collective-permute-start.9
  101.5 1.8 collective-permute-start.10
  103.3 2.0 slice.31
  105.4 2.5 %collective-permute-start.11 = (bf16[5,4,2,64,128]{4,3,2,1,0:T(8,128)(2,1)}, bf16[5,4,2,64,128]{4,3,2,1,0:T(8,128)(2,1)}, u32[]{:S(2)}, u32[]{:S(2)}) collective-permute-start(bf16[5,4,2,64,128]{4,3,2,1,0:T(8,128)(2,1)} %slice.31), channel_id=1, source_target_pairs={{0,4},{4,8},{8,12},{16,20},{20,24},{24,28},{32,36},{36,40},{40,44}... | collective-permute-start | bytes 1966088 | tf_op jit(solution)/shard_map/ppermute | solution.py:367
  107.8 1.3 collective-permute-start.12
  109.2 21.6 %query_side.1 = (bf16[16,2,64,128]{3,2,1,0:T(8,128)(2,1)S(1)}, bf16[4,2,64,128]{3,2,1,0:T(8,128)(2,1)}, f32[16,256]{1,0:T(8,128)S(1)}) custom-call(s32[3]{0:T(128)S(1)} %pad_add_fusion.pos, s32[128,128]{1,0:T(8,128)S(1)} %copy-done.14, f32[8,8,128]{2,1,0:T(8,128)S(1)} %stack.26.tab, bf16[4,4,2,2,64,128]{5,4,3,2,1,0:T(8,128)(2,1)S(1)} %bitcast.28, ...), custom_call_target="tpu_custom_call" | custom-call | flops 5452595200 | bytes 8388608 | tf_op jit(solution)/shard_map/query_side/pallas_call | solution.py:300
  131.6 12.3 %all_to_all.40 = f32[4,2,256]{2,1,0:T(2,128)} all-to-all(f32[4,2,256]{2,1,0:T(2,128)S(1)} %broadcast_in_dim.4), channel_id=1, replica_groups=mesh['zh'=4,'p'=16,'h'=4] {'zh'}, dimensions={0} | all-to-all | bytes 16384 | tf_op jit(solution)/shard_map/all_to_all | solution.py:421
  143.9 9.3 %all-to-all-start.4 = ((bf16[4,2,64,128]{3,2,1,0:T(8,128)(2,1)}), bf16[4,2,64,128]{3,2,1,0:T(8,128)(2,1)S(1)}, u32[]{:S(2)}, u32[]{:S(2)}) async-start(bf16[4,2,64,128]{3,2,1,0:T(8,128)(2,1)} %get-tuple-element.27), calls=%async_computation.4 | async-start | bytes 262144 | tf_op jit(solution)/shard_map/all_to_all | solution.py:404
  153.2 3.6 %all-to-all-done.4.x_ref = bf16[4,2,64,128]{3,2,1,0:T(8,128)(2,1)S(1)} async-done(((bf16[4,2,64,128]{3,2,1,0:T(8,128)(2,1)}), bf16[4,2,64,128]{3,2,1,0:T(8,128)(2,1)S(1)}, u32[]{:S(2)}, u32[]{:S(2)}) %all-to-all-start.4) | async-done | bytes 131104 | tf_op jit(solution)/shard_map/all_to_all | solution.py:404
  156.8 4.6 %all-to-all-start.3 = ((bf16[16,2,64,128]{3,2,1,0:T(8,128)(2,1)}), bf16[16,2,64,128]{3,2,1,0:T(8,128)(2,1)S(1)}, u32[]{:S(2)}, u32[]{:S(2)}) async-start(bf16[16,2,64,128]{3,2,1,0:T(8,128)(2,1)} %copy-done.2), calls=%async_computation.3 | async-start | bytes 1048576 | tf_op jit(solution)/shard_map/all_to_all | solution.py:403
  161.4 2.4 %broadcast_select_fusion = (bf16[6,4,2,64,128]{4,3,2,1,0:T(8,128)(2,1)}, bf16[6,4,2,64,128]{4,3,2,1,0:T(8,128)(2,1)}) fusion(bf16[6,4,2,64,128]{4,3,2,1,0:T(8,128)(2,1)} %collective-permute-done.10.refs_3_, pred[]{:T(512)S(6)} %or.4, bf16[6,4,2,64,128]{4,3,2,1,0:T(8,128)(2,1)} %collective-permute-done.9.refs_1_, ...), kind=kLoop, calls=%fused_computation.2 | loop fusion | flops 786432 | bytes 3932162 | tf_op jit(solution)/shard_map/jit(_where)/select_n | solution.py:384
  163.8 2.9 %collective-permute-start.14 = (bf16[6,4,2,64,128]{4,3,2,1,0:T(8,128)(2,1)}, bf16[6,4,2,64,128]{4,3,2,1,0:T(8,128)(2,1)}, u32[]{:S(2)}, u32[]{:S(2)}) collective-permute-start(bf16[6,4,2,64,128]{4,3,2,1,0:T(8,128)(2,1)} %get-tuple-element.42), channel_id=1, source_target_pairs={{0,12},{4,20},{8,56},{12,0},{16,28},{20,36},{24,8},{28,16},{32,44}... | collective-permute-start | bytes 2359304 | tf_op jit(solution)/shard_map/ppermute | solution.py:367
  166.8 2.1 collective-permute-start.15
  169.5 1.3 reshape.216
  171.5 7.3 %all-to-all-done.3.m_ref = bf16[16,2,64,128]{3,2,1,0:T(8,128)(2,1)S(1)} async-done(((bf16[16,2,64,128]{3,2,1,0:T(8,128)(2,1)}), bf16[16,2,64,128]{3,2,1,0:T(8,128)(2,1)S(1)}, u32[]{:S(2)}, u32[]{:S(2)}) %all-to-all-start.3) | async-done | bytes 524320 | tf_op jit(solution)/shard_map/all_to_all | solution.py:403
  179.5 5.7 %all-to-all-start.5 = ((f32[16,16,256]{2,1,0:T(8,128)}), f32[16,16,256]{2,1,0:T(8,128)}, u32[]{:S(2)}, u32[]{:S(2)}) async-start(f32[16,16,256]{2,1,0:T(8,128)} %broadcast_in_dim.5), calls=%async_computation.5 | async-start | bytes 524288 | tf_op jit(solution)/shard_map/all_to_all | solution.py:423
  185.9 0.8 copy-done.15
  186.7 7.4 %near_key_side.1.sums = f32[5,2,256,128]{3,2,1,0:T(8,128)S(1)} custom-call(s32[3]{0:T(128)S(1)} %copy-done.10, s32[128,128]{1,0:T(8,128)S(1)} %copy-done.15, bf16[4,4,2,2,64,128]{5,4,3,2,1,0:T(8,128)(2,1)S(1)} %bitcast.29, bf16[4,4,2,2,64,128]{5,4,3,2,1,0:T(8,128)(2,1)S(1)} %bitcast.32, f32[16,256]{1,0:T(8,128)S(1)} %pad_maximum_fusion.3.stats), custom_call_target="tpu_custom_call" | custom-call | flops 1677721600 | bytes 8388608 | tf_op jit(solution)/shard_map/near_key_side/pallas_call | solution.py:317
  194.2 1.1 copy-done.17
  195.3 0.9 unpack.2
  197.6 0.8 copy-done.16
  198.4 1.3 copy-done.18
  199.7 14.5 %far_key_side.1 = (bf16[16,2,64,128]{3,2,1,0:T(8,128)(2,1)S(1)}, bf16[4,2,64,128]{3,2,1,0:T(8,128)(2,1)S(1)}) custom-call(s32[3]{0:T(128)S(1)} %copy-done.11, s32[128,128]{1,0:T(8,128)S(1)} %copy-done.16, f32[8,8,128]{2,1,0:T(8,128)S(1)} %copy-done.8, bf16[4,4,2,2,64,128]{5,4,3,2,1,0:T(8,128)(2,1)S(1)} %bitcast.30, f32[5,2,256,128]{3,2,1,0:T(8,128)S(1)} %copy-done.18, ...), custom_call_target="tpu_custom_call" | custom-call | flops 2684354560 | bytes 8388608 | tf_op jit(solution)/shard_map/far_key_side/pallas_call | solution.py:329
  214.3 5.2 %all_to_all.41.x_ref = bf16[4,2,64,128]{3,2,1,0:T(8,128)(2,1)S(1)} all-to-all(bf16[4,2,64,128]{3,2,1,0:T(8,128)(2,1)S(1)} %get-tuple-element.39), channel_id=1, replica_groups=mesh['zh'=4,'p'=16,'h'=4] {'h'}, dimensions={0} | all-to-all | bytes 262144 | tf_op jit(solution)/shard_map/all_to_all | solution.py:404
  219.4 22.8 %all_to_all.42.m_ref = bf16[16,2,64,128]{3,2,1,0:T(8,128)(2,1)S(1)} all-to-all(bf16[16,2,64,128]{3,2,1,0:T(8,128)(2,1)S(1)} %get-tuple-element.38), channel_id=1, replica_groups=mesh['zh'=4,'p'=16,'h'=4] {'zh','h'}, dimensions={0} | all-to-all | bytes 1048576 | tf_op jit(solution)/shard_map/all_to_all | solution.py:403
  242.2 0.9 unpack.3
  (73 shorter events, 9.1 us)
Async XLA Ops:
  1.6 107.5 %copy-start.9 = (s32[3]{0:T(128)}, s32[3]{0:T(128)S(1)}, u32[]{:S(2)}) copy-start(s32[3]{0:T(128)S(1)} %pad_add_fusion.pos) | copy-start | bytes 40
  2.6 106.5 %copy-start.7 = (f32[8,8,128]{2,1,0:T(8,128)}, f32[8,8,128]{2,1,0:T(8,128)S(1)}, u32[]{:S(2)}) copy-start(f32[8,8,128]{2,1,0:T(8,128)S(1)} %stack.26.tab) | copy-start | bytes 98308
  2.6 1.0 copy-start.3
  3.6 1.0 copy-start.4
  6.4 10.1 %copy-start.5 = (bf16[64,20,128]{2,0,1:T(8,128)(2,1)S(1)}, bf16[64,20,128]{2,0,1:T(8,128)(2,1)}, u32[]{:S(2)}) copy-start(bf16[64,20,128]{2,0,1:T(8,128)(2,1)} %param.9) | copy-start | bytes 983044
  6.4 10.1 %copy-start.6 = (bf16[64,20,128]{2,0,1:T(8,128)(2,1)S(1)}, bf16[64,20,128]{2,0,1:T(8,128)(2,1)}, u32[]{:S(2)}) copy-start(bf16[64,20,128]{2,0,1:T(8,128)(2,1)} %param.12) | copy-start | bytes 983044
  6.4 38.0 %all-to-all-start = ((bf16[16,2,2,64,128]{4,3,2,1,0:T(8,128)(2,1)}), bf16[16,2,2,64,128]{4,3,2,1,0:T(8,128)(2,1)S(1)}, u32[]{:S(2)}, u32[]{:S(2)}) async-start(bf16[16,2,2,64,128]{4,3,2,1,0:T(8,128)(2,1)} %pack.2), calls=%async_computation | async-start | bytes 2097152 | tf_op jit(solution)/shard_map/all_to_all | solution.py:398
  44.4 39.7 %all-to-all-start.1 = ((bf16[16,2,2,64,128]{4,3,2,1,0:T(8,128)(2,1)}), bf16[16,2,2,64,128]{4,3,2,1,0:T(8,128)(2,1)S(1)}, u32[]{:S(2)}, u32[]{:S(2)}) async-start(bf16[16,2,2,64,128]{4,3,2,1,0:T(8,128)(2,1)} %pack.3), calls=%async_computation.1 | async-start | bytes 2097152 | tf_op jit(solution)/shard_map/all_to_all | solution.py:398
  48.2 0.7 copy-start.19
  49.9 20.8 %collective-permute-start = (bf16[6,4,2,64,128]{4,3,2,1,0:T(8,128)(2,1)}, bf16[6,4,2,64,128]{4,3,2,1,0:T(8,128)(2,1)S(1)}, u32[]{:S(2)}, u32[]{:S(2)}) collective-permute-start(bf16[6,4,2,64,128]{4,3,2,1,0:T(8,128)(2,1)} %pad_maximum_fusion), channel_id=1, source_target_pairs={{0,16},{4,20},{8,24},{12,28},{16,32},{20,36},{24,40},{28,44},{32,4... | collective-permute-start | bytes 2359304 | tf_op jit(solution)/shard_map/ppermute | solution.py:367
  51.2 19.5 %collective-permute-start.1 = (bf16[6,4,2,64,128]{4,3,2,1,0:T(8,128)(2,1)}, bf16[6,4,2,64,128]{4,3,2,1,0:T(8,128)(2,1)}, u32[]{:S(2)}, u32[]{:S(2)}) collective-permute-start(bf16[6,4,2,64,128]{4,3,2,1,0:T(8,128)(2,1)} %pad_maximum_fusion), channel_id=1, source_target_pairs={{0,48},{4,52},{8,56},{12,60},{16,0},{20,4},{24,8},{28,12},{32,16},... | collective-permute-start | bytes 2359304 | tf_op jit(solution)/shard_map/ppermute | solution.py:367
  52.6 20.4 %collective-permute-start.3 = (bf16[6,4,2,64,128]{4,3,2,1,0:T(8,128)(2,1)}, bf16[6,4,2,64,128]{4,3,2,1,0:T(8,128)(2,1)}, u32[]{:S(2)}, u32[]{:S(2)}) collective-permute-start(bf16[6,4,2,64,128]{4,3,2,1,0:T(8,128)(2,1)} %pad_maximum_fusion), channel_id=1, source_target_pairs={{0,8},{4,12},{8,0},{12,4},{16,24},{20,28},{24,16},{28,20},{32,40},... | collective-permute-start | bytes 2359304 | tf_op jit(solution)/shard_map/ppermute | solution.py:367
  55.3 24.6 %copy-start.20 = (bf16[1,4,2,64,128]{4,3,2,1,0:T(8,128)(2,1)S(1)}, bf16[1,4,2,64,128]{4,3,2,1,0:T(8,128)(2,1)}, u32[]{:S(2)}) copy-start(bf16[1,4,2,64,128]{4,3,2,1,0:T(8,128)(2,1)} %copy-done.19) | copy-start | bytes 393220
  70.6 4.8 %copy-start = (bf16[6,4,2,64,128]{4,3,2,1,0:T(8,128)(2,1)}, bf16[6,4,2,64,128]{4,3,2,1,0:T(8,128)(2,1)S(1)}, u32[]{:S(2)}) copy-start(bf16[6,4,2,64,128]{4,3,2,1,0:T(8,128)(2,1)S(1)} %collective-permute-done.refs_0_) | copy-start | bytes 2359300
  75.4 26.1 %collective-permute-start.2 = (bf16[6,4,2,64,128]{4,3,2,1,0:T(8,128)(2,1)}, bf16[6,4,2,64,128]{4,3,2,1,0:T(8,128)(2,1)}, u32[]{:S(2)}, u32[]{:S(2)}) collective-permute-start(bf16[6,4,2,64,128]{4,3,2,1,0:T(8,128)(2,1)} %get-tuple-element.45), channel_id=1, source_target_pairs={{0,48},{4,52},{8,24},{12,28},{16,0},{20,4},{24,40},{28,44},{32,16}... | collective-permute-start | bytes 2359304 | tf_op jit(solution)/shard_map/ppermute | solution.py:367
  76.8 28.5 %collective-permute-start.4 = (bf16[6,4,2,64,128]{4,3,2,1,0:T(8,128)(2,1)}, bf16[6,4,2,64,128]{4,3,2,1,0:T(8,128)(2,1)}, u32[]{:S(2)}, u32[]{:S(2)}) collective-permute-start(bf16[6,4,2,64,128]{4,3,2,1,0:T(8,128)(2,1)} %get-tuple-element.44), channel_id=1, source_target_pairs={{0,12},{4,20},{8,56},{12,0},{16,28},{20,36},{24,8},{28,16},{32,44}... | collective-permute-start | bytes 2359304 | tf_op jit(solution)/shard_map/ppermute | solution.py:367
  76.8 31.0 %collective-permute-start.5 = (bf16[6,4,2,64,128]{4,3,2,1,0:T(8,128)(2,1)}, bf16[6,4,2,64,128]{4,3,2,1,0:T(8,128)(2,1)}, u32[]{:S(2)}, u32[]{:S(2)}) collective-permute-start(bf16[6,4,2,64,128]{4,3,2,1,0:T(8,128)(2,1)} %collective-permute-done.3.refs_3_), channel_id=1, source_target_pairs={{0,16},{12,60},{16,32},{28,12},{32,48},{44,28},{48,0},{60,44},{1,1... | collective-permute-start | bytes 2359304 | tf_op jit(solution)/shard_map/ppermute | solution.py:367
  80.9 14.2 %collective-permute-start.6 = (bf16[5,4,2,64,128]{4,3,2,1,0:T(8,128)(2,1)}, bf16[5,4,2,64,128]{4,3,2,1,0:T(8,128)(2,1)S(1)}, u32[]{:S(2)}, u32[]{:S(2)}) collective-permute-start(bf16[5,4,2,64,128]{4,3,2,1,0:T(8,128)(2,1)} %pad_maximum_fusion.2), channel_id=1, source_target_pairs={{0,4},{4,8},{8,12},{16,20},{20,24},{24,28},{32,36},{36,40},{40,44}... | collective-permute-start | bytes 1966088 | tf_op jit(solution)/shard_map/ppermute | solution.py:367
  82.8 17.1 %collective-permute-start.7 = (bf16[5,4,2,64,128]{4,3,2,1,0:T(8,128)(2,1)}, bf16[5,4,2,64,128]{4,3,2,1,0:T(8,128)(2,1)}, u32[]{:S(2)}, u32[]{:S(2)}) collective-permute-start(bf16[5,4,2,64,128]{4,3,2,1,0:T(8,128)(2,1)} %pad_maximum_fusion.2), channel_id=1, source_target_pairs={{4,0},{8,4},{12,8},{20,16},{24,20},{28,24},{36,32},{40,36},{44,40}... | collective-permute-start | bytes 1966088 | tf_op jit(solution)/shard_map/ppermute | solution.py:367
  84.3 24.8 %copy-start.1 = (bf16[6,4,2,64,128]{4,3,2,1,0:T(8,128)(2,1)S(1)}, bf16[6,4,2,64,128]{4,3,2,1,0:T(8,128)(2,1)}, u32[]{:S(2)}) copy-start(bf16[6,4,2,64,128]{4,3,2,1,0:T(8,128)(2,1)} %copy-done) | copy-start | bytes 2359300
  84.3 24.8 %copy-start.14 = (s32[128,128]{1,0:T(8,128)S(1)}, s32[128,128]{1,0:T(8,128)}, u32[]{:S(2)}) copy-start(s32[128,128]{1,0:T(8,128)} %mask.5) | copy-start | bytes 196612
  95.1 0.8 copy-start.12
  95.9 57.3 %collective-permute-start.8 = (bf16[6,4,2,64,128]{4,3,2,1,0:T(8,128)(2,1)}, bf16[6,4,2,64,128]{4,3,2,1,0:T(8,128)(2,1)S(1)}, u32[]{:S(2)}, u32[]{:S(2)}) collective-permute-start(bf16[6,4,2,64,128]{4,3,2,1,0:T(8,128)(2,1)} %pad_maximum_fusion.1), channel_id=1, source_target_pairs={{0,16},{4,20},{8,24},{12,28},{16,32},{20,36},{24,40},{28,44},{32,4... | collective-permute-start | bytes 2359304 | tf_op jit(solution)/shard_map/ppermute | solution.py:367
  96.3 12.9 %copy-start.13 = (bf16[5,4,2,64,128]{4,3,2,1,0:T(8,128)(2,1)S(1)}, bf16[5,4,2,64,128]{4,3,2,1,0:T(8,128)(2,1)}, u32[]{:S(2)}) copy-start(bf16[5,4,2,64,128]{4,3,2,1,0:T(8,128)(2,1)} %copy-done.12) | copy-start | bytes 1966084
  99.9 53.3 %collective-permute-start.9 = (bf16[6,4,2,64,128]{4,3,2,1,0:T(8,128)(2,1)}, bf16[6,4,2,64,128]{4,3,2,1,0:T(8,128)(2,1)}, u32[]{:S(2)}, u32[]{:S(2)}) collective-permute-start(bf16[6,4,2,64,128]{4,3,2,1,0:T(8,128)(2,1)} %pad_maximum_fusion.1), channel_id=1, source_target_pairs={{0,48},{4,52},{8,56},{12,60},{16,0},{20,4},{24,8},{28,12},{32,16},... | collective-permute-start | bytes 2359304 | tf_op jit(solution)/shard_map/ppermute | solution.py:367
  101.5 51.7 %collective-permute-start.10 = (bf16[6,4,2,64,128]{4,3,2,1,0:T(8,128)(2,1)}, bf16[6,4,2,64,128]{4,3,2,1,0:T(8,128)(2,1)}, u32[]{:S(2)}, u32[]{:S(2)}) collective-permute-start(bf16[6,4,2,64,128]{4,3,2,1,0:T(8,128)(2,1)} %pad_maximum_fusion.1), channel_id=1, source_target_pairs={{0,8},{4,12},{8,0},{12,4},{16,24},{20,28},{24,16},{28,20},{32,40},... | collective-permute-start | bytes 2359304 | tf_op jit(solution)/shard_map/ppermute | solution.py:367
  105.4 47.9 %collective-permute-start.11 = (bf16[5,4,2,64,128]{4,3,2,1,0:T(8,128)(2,1)}, bf16[5,4,2,64,128]{4,3,2,1,0:T(8,128)(2,1)}, u32[]{:S(2)}, u32[]{:S(2)}) collective-permute-start(bf16[5,4,2,64,128]{4,3,2,1,0:T(8,128)(2,1)} %slice.31), channel_id=1, source_target_pairs={{0,4},{4,8},{8,12},{16,20},{20,24},{24,28},{32,36},{36,40},{40,44}... | collective-permute-start | bytes 1966088 | tf_op jit(solution)/shard_map/ppermute | solution.py:367
  107.8 45.4 %collective-permute-start.12 = (bf16[5,4,2,64,128]{4,3,2,1,0:T(8,128)(2,1)}, bf16[5,4,2,64,128]{4,3,2,1,0:T(8,128)(2,1)}, u32[]{:S(2)}, u32[]{:S(2)}) collective-permute-start(bf16[5,4,2,64,128]{4,3,2,1,0:T(8,128)(2,1)} %slice.31), channel_id=1, source_target_pairs={{4,0},{8,4},{12,8},{20,16},{24,20},{28,24},{36,32},{40,36},{44,40}... | collective-permute-start | bytes 1966088 | tf_op jit(solution)/shard_map/ppermute | solution.py:367
  130.8 0.8 copy-start.2
  143.9 12.9 %all-to-all-start.4 = ((bf16[4,2,64,128]{3,2,1,0:T(8,128)(2,1)}), bf16[4,2,64,128]{3,2,1,0:T(8,128)(2,1)S(1)}, u32[]{:S(2)}, u32[]{:S(2)}) async-start(bf16[4,2,64,128]{3,2,1,0:T(8,128)(2,1)} %get-tuple-element.27), calls=%async_computation.4 | async-start | bytes 262144 | tf_op jit(solution)/shard_map/all_to_all | solution.py:404
  156.8 21.9 %all-to-all-start.3 = ((bf16[16,2,64,128]{3,2,1,0:T(8,128)(2,1)}), bf16[16,2,64,128]{3,2,1,0:T(8,128)(2,1)S(1)}, u32[]{:S(2)}, u32[]{:S(2)}) async-start(bf16[16,2,64,128]{3,2,1,0:T(8,128)(2,1)} %copy-done.2), calls=%async_computation.3 | async-start | bytes 1048576 | tf_op jit(solution)/shard_map/all_to_all | solution.py:403
  163.8 32.3 %collective-permute-start.13 = (bf16[6,4,2,64,128]{4,3,2,1,0:T(8,128)(2,1)}, bf16[6,4,2,64,128]{4,3,2,1,0:T(8,128)(2,1)}, u32[]{:S(2)}, u32[]{:S(2)}) collective-permute-start(bf16[6,4,2,64,128]{4,3,2,1,0:T(8,128)(2,1)} %get-tuple-element.43), channel_id=1, source_target_pairs={{0,48},{4,52},{8,24},{12,28},{16,0},{20,4},{24,40},{28,44},{32,16}... | collective-permute-start | bytes 2359304 | tf_op jit(solution)/shard_map/ppermute | solution.py:367
  163.8 32.3 %collective-permute-start.14 = (bf16[6,4,2,64,128]{4,3,2,1,0:T(8,128)(2,1)}, bf16[6,4,2,64,128]{4,3,2,1,0:T(8,128)(2,1)}, u32[]{:S(2)}, u32[]{:S(2)}) collective-permute-start(bf16[6,4,2,64,128]{4,3,2,1,0:T(8,128)(2,1)} %get-tuple-element.42), channel_id=1, source_target_pairs={{0,12},{4,20},{8,56},{12,0},{16,28},{20,36},{24,8},{28,16},{32,44}... | collective-permute-start | bytes 2359304 | tf_op jit(solution)/shard_map/ppermute | solution.py:367
  166.8 29.4 %collective-permute-start.15 = (bf16[6,4,2,64,128]{4,3,2,1,0:T(8,128)(2,1)}, bf16[6,4,2,64,128]{4,3,2,1,0:T(8,128)(2,1)}, u32[]{:S(2)}, u32[]{:S(2)}) collective-permute-start(bf16[6,4,2,64,128]{4,3,2,1,0:T(8,128)(2,1)} %collective-permute-done.10.refs_3_), channel_id=1, source_target_pairs={{0,16},{12,60},{16,32},{28,12},{32,48},{44,28},{48,0},{60,44},{1,1... | collective-permute-start | bytes 2359304 | tf_op jit(solution)/shard_map/ppermute | solution.py:367
  179.5 16.7 %all-to-all-start.5 = ((f32[16,16,256]{2,1,0:T(8,128)}), f32[16,16,256]{2,1,0:T(8,128)}, u32[]{:S(2)}, u32[]{:S(2)}) async-start(f32[16,16,256]{2,1,0:T(8,128)} %broadcast_in_dim.5), calls=%async_computation.5 | async-start | bytes 524288 | tf_op jit(solution)/shard_map/all_to_all | solution.py:423
  185.2 0.7 copy-start.10
  185.9 0.8 copy-start.15
  194.1 1.1 copy-start.17
  196.2 0.8 copy-start.8
  196.9 0.7 copy-start.11
  197.6 0.8 copy-start.16
  198.4 1.3 copy-start.18

commit v3 on v2

v3 whole, which is shorter than its diff:
```python
import functools
import math

import jax
import jax.numpy as jnp
import numpy as np
from jax import lax
from jax.experimental import pallas as pl
from jax.experimental.pallas import tpu as pltpu
from jax.sharding import Mesh, PartitionSpec as P

ROT = 44
HALF = ROT // 2
BLK = 128
E = 128
TOK = 256
QTR = 64
GROUPS = 64
PLANE = 16
ZG = 4
UNITS = 5
SROWS = 24
NEG = -1e30
PARTS = 8
OFFSETS = (0, 1, -1, 2, -2, 4, -4, 8, -8, 16, -16, 32, -32)
SLOTS = 46
SCALE = 1.0 / math.sqrt(E)
LOG2E = 1.4426950408889634
COEF = SCALE * LOG2E
F32 = jnp.float32
BF16 = jnp.bfloat16
HBM = pl.BlockSpec(memory_space=pltpu.HBM)
SMEM = pl.BlockSpec(memory_space=pltpu.SMEM)
VMEM = pl.BlockSpec(memory_space=pltpu.VMEM)

WIDE = jax.ShapeDtypeStruct((16, 2, 2, QTR, E), BF16)


def dot(a, b, ca, cb):
    return lax.dot_general(a, b, (((ca,), (cb,)), ((), ())), preferred_element_type=F32)


def turn(x, c, s1, s2):
    return x * c + pltpu.roll(x, HALF, x.ndim - 1) * s1 + pltpu.roll(x, E - HALF, x.ndim - 1) * s2


def pack_kernel(pos, frames, rates, a_hbm, b_hbm, o_ref, a_ref, b_ref, sems):
    copies = [
        pltpu.make_async_copy(a_hbm, a_ref, sems.at[0]),
        pltpu.make_async_copy(b_hbm, b_ref, sems.at[1]),
    ]
    for copy in copies:
        copy.start()
    block = 2 * (pos[0] * PLANE + pos[1]) + pos[2] // 2
    rows = [r[None] for r in turn_rows(frames, rates, block)]
    copies[0].wait()
    a = turn(a_ref[...].astype(F32), *rows).astype(BF16)
    copies[1].wait()
    for n, val in ((0, a), (1, b_ref[...])):
        o_ref[:, 0, n] = val[:16]
        for i in range(4):
            o_ref[4 * i : 4 * i + 4, 1, n] = val[16:]


def pack(pos, frames, rates, *tensors):
    return pl.pallas_call(
        pack_kernel,
        out_shape=WIDE,
        in_specs=[SMEM, SMEM, VMEM, HBM, HBM],
        out_specs=VMEM,
        scratch_shapes=[
            pltpu.VMEM((20, QTR, E), BF16),
            pltpu.VMEM((20, QTR, E), BF16),
            pltpu.SemaphoreType.DMA((2,)),
        ],
        compiler_params=LIMIT,
        name="pack",
    )(pos, frames, rates, *[jnp.transpose(t, (1, 0, 2)) for t in tensors])


def unpack_kernel(pos, a_ref, b_ref, *refs):
    pieces, outs = refs[:4], refs[4:]
    for i, o in enumerate(outs):
        o[:16] = (a_ref, b_ref)[i // 2][:, i % 2]
        for n, piece in enumerate(pieces):
            o[16 + lax.rem(pos[2] - n + 4, 4)] = piece[i]


def unpack(pos, a, b, pieces):
    shape = jax.ShapeDtypeStruct((20, QTR, E), BF16)
    outs = pl.pallas_call(
        unpack_kernel,
        out_shape=(shape,) * 4,
        in_specs=[SMEM] + [VMEM] * 6,
        out_specs=(VMEM,) * 4,
        compiler_params=LIMIT,
        name="unpack",
    )(pos, a, b, *pieces)
    return tuple(jnp.transpose(o, (1, 0, 2)) for o in outs)


def source(offset, unit, zh, p):
    is_x = unit == 4
    z = jnp.where(is_x, zh, unit)
    group = z * PLANE + p
    other = group - offset
    valid = (other >= 0) & (other < GROUPS)
    if local(offset):
        slot = jnp.clip(z - offset // PLANE, 0, ZG - 1)
    else:
        x = lax.rem(p, 4)
        low = x < 2
        base = {
            4: lambda: 0,
            -4: lambda: 6,
            8: lambda: 12,
            -8: lambda: 12,
            1: lambda: jnp.where(x == 0, 30, 36),
            -1: lambda: jnp.where(x == 3, 30, 41),
            2: lambda: jnp.where(low, 24, 18),
            -2: lambda: jnp.where(low, 18, 24),
        }[offset]()
        at = p - offset
        step = jnp.where(at < 0, -1, jnp.where(at >= PLANE, 1, 0))
        zz = jnp.clip(z + step, 0, ZG - 1)
        slot = base + jnp.where(is_x, 5 * step * step, 1 + zz)
    return group, jnp.clip(other, 0, GROUPS - 1), valid, slot


def local(offset):
    return offset == 0 or abs(offset) >= PLANE


def add_bias(st, bias):
    top = jnp.concatenate([st[:BLK, :BLK] + bias[0][0], st[:BLK, BLK:] + bias[0][1]], axis=1)
    low = jnp.concatenate([st[BLK:, :BLK] + bias[1][0], st[BLK:, BLK:] + bias[1][1]], axis=1)
    return jnp.concatenate([top, low], axis=0)


def bias_of(mask, q_group, k_group, valid):
    return [
        [
            jnp.where(valid & (mask[2 * q_group + qb, 2 * k_group + kb] != 0), 0.0, NEG)
            for qb in range(2)
        ]
        for kb in range(2)
    ]


def fetch(parts, pool, sems, wholes=(), only_x=False):
    copies = []
    at = 0
    for n, ref in enumerate(parts):
        size = ref.shape[0]
        for first, count in (((0, 1), (5, 1)) if only_x else ((0, size),)):
            if first < size:
                copies.append(
                    pltpu.make_async_copy(
                        ref.at[pl.ds(first, count)],
                        pool.at[pl.ds(at + first, count)],
                        sems.at[2 * n + (first > 0)],
                    )
                )
        at += size
    for n, (whole, target) in enumerate(wholes):
        copies.append(pltpu.make_async_copy(whole, target, sems.at[2 * PARTS + n]))
    for copy in copies:
        copy.start()
    for copy in copies:
        copy.wait()


def near(ref, z, unit, which):
    return ref[z, :, jnp.where(unit == 4, 1, 0), which].reshape(TOK, E)


def far(ref, slot, which):
    return ref[slot, :, which].reshape(TOK, E)


def turn_rows(frames, rates, block):
    angles = frames[block].astype(F32) * rates[0:1]
    sine = jnp.sin(angles)
    return jnp.cos(angles), sine * rates[1:2], sine * rates[2:3]


def unturn(x, frames, rates, group):
    halves = []
    for blk in range(2):
        c, s1, s2 = turn_rows(frames, rates, 2 * group + blk)
        halves.append(turn(x[blk * BLK : (blk + 1) * BLK], c, -s1, -s2))
    return jnp.concatenate(halves, axis=0)


def put(ref, at, which, val):
    for b in range(4):
        ref[at, b, which] = val[b * QTR : (b + 1) * QTR]


def read_stats(ref, unit, *at):
    rows = [ref[(*at, pl.ds(4 * unit + n, 1), slice(None))] for n in range(4)]
    return jnp.concatenate(rows[:2], axis=1), jnp.concatenate(rows[2:], axis=1)


def pool_rows(offset, slot, unit, near_ref, pool, which):
    if local(offset):
        return near(near_ref, slot, unit, which)
    return far(pool, slot, which)


def forward_kernel(pos, *refs):
    parts, wholes, rest = refs[:PARTS], refs[PARTS : PARTS + 3], refs[PARTS + 3 :]
    att_ref, stats, pool, sems, mask, kv, qg, scores = rest
    fetch(parts, pool, sems, zip(wholes, (mask, kv, qg)))
    zh, p = pos[0], pos[1]

    def body(unit, carry):
        z = jnp.where(unit == 4, zh, unit)
        q = near(qg, z, unit, 0)
        slots = []
        top = jnp.full((1, TOK), NEG, F32)
        for n, offset in enumerate(OFFSETS):
            group, other, valid, slot = source(offset, unit, zh, p)
            slots.append(slot)
            k = pool_rows(offset, slot, unit, kv, pool, 0)
            st = add_bias(dot(k, q, 1, 1), bias_of(mask, group, other, valid))
            scores[n] = st
            top = jnp.maximum(top, jnp.max(st, axis=0, keepdims=True))
        top = top * COEF
        total = jnp.zeros((1, TOK), F32)
        out = jnp.zeros((E, TOK), F32)
        for n, offset in enumerate(OFFSETS):
            w = jnp.exp2(scores[n] * COEF - top)
            total = total + jnp.sum(w, axis=0, keepdims=True)
            v = pool_rows(offset, slots[n], unit, kv, pool, 1)
            out = out + dot(v, w.astype(BF16), 0, 0)
        att = jnp.transpose(out * (1.0 / total)).astype(BF16)
        put(att_ref, unit, 0, att)
        g = near(qg, z, unit, 1).astype(F32)
        delta = jnp.sum(jnp.transpose(g * att.astype(F32)), axis=0, keepdims=True)
        for n, row in enumerate((top + jnp.log2(total), delta)):
            stats[pl.ds(4 * unit + 2 * n, 1), :] = row[:, :BLK]
            stats[pl.ds(4 * unit + 2 * n + 1, 1), :] = row[:, BLK:]
        return carry

    stats[...] = jnp.zeros_like(stats)
    lax.fori_loop(0, UNITS, body, 0)


def query_kernel(pos, frames, rates, *refs):
    parts, wholes, rest = refs[:PARTS], refs[PARTS : PARTS + 5], refs[PARTS + 5 :]
    o_ref, pool, sems, mask, kv, qg, att, stats = rest
    fetch(parts, pool, sems, zip(wholes, (mask, kv, qg, att, stats)))
    zh, p = pos[0], pos[1]

    def body(unit, carry):
        z = jnp.where(unit == 4, zh, unit)
        q = near(qg, z, unit, 0)
        g = near(qg, z, unit, 1)
        total, delta = read_stats(stats, unit)
        dq = jnp.zeros((E, TOK), F32)
        for offset in OFFSETS:
            group, other, valid, slot = source(offset, unit, zh, p)
            k = pool_rows(offset, slot, unit, kv, pool, 0)
            v = pool_rows(offset, slot, unit, kv, pool, 1)
            st = add_bias(dot(k, q, 1, 1), bias_of(mask, group, other, valid))
            w = jnp.exp2(st * COEF - total)
            ds = (w * (dot(v, g, 1, 1) - delta)).astype(BF16)
            dq = dq + dot(k, ds, 0, 0)
        o_ref[unit, :, 0] = att[unit, :, 0]
        dq = unturn(jnp.transpose(dq * SCALE), frames, rates, z * PLANE + p)
        put(o_ref, unit, 1, dq.astype(BF16))
        return carry

    lax.fori_loop(0, UNITS, body, 0)


def key_terms(unit, zh, p, mask, kv, qg, pool, stats_of):
    z = jnp.where(unit == 4, zh, unit)
    k = near(kv, z, unit, 0)
    v = near(kv, z, unit, 1)
    dk = jnp.zeros((TOK, E), F32)
    dv = jnp.zeros((TOK, E), F32)
    for offset in OFFSETS:
        group, other, valid, slot = source(offset, unit, zh, p)
        total, delta = stats_of(other)
        q = pool_rows(offset, slot, unit, qg, pool, 0)
        g = pool_rows(offset, slot, unit, qg, pool, 1)
        st = add_bias(dot(k, q, 1, 1), bias_of(mask, other, group, valid))
        w = jnp.exp2(st * COEF - total)
        ds = (w * (dot(v, g, 1, 1) - delta)).astype(BF16)
        dv = dv + dot(w.astype(BF16), g, 1, 0)
        dk = dk + dot(ds, q, 1, 0)
    return dk, dv


def key_kernel(pos, frames, rates, *refs):
    parts, wholes, rest = refs[:PARTS], refs[PARTS : PARTS + 4], refs[PARTS + 4 :]
    o_ref, pool, sems, mask, kv, qg, stats = rest
    fetch(parts, pool, sems, zip(wholes, (mask, kv, qg, stats)))
    zh, p = pos[0], pos[1]

    def stats_of(other):
        return read_stats(stats, lax.div(other, PLANE), zh * PLANE + lax.rem(other, PLANE))

    def body(unit, carry):
        dk, dv = key_terms(unit, zh, p, mask, kv, qg, pool, stats_of)
        dk = unturn(dk * SCALE, frames, rates, unit * PLANE + p)
        put(o_ref, unit, 0, dk.astype(BF16))
        put(o_ref, unit, 1, dv.astype(BF16))
        return carry

    lax.fori_loop(0, ZG, body, 0)


def extra_key_kernel(pos, frames, rates, *refs):
    parts, wholes, rest = refs[:PARTS], refs[PARTS : PARTS + 5], refs[PARTS + 5 :]
    o_ref, pool, sems, mask, kv, qg, stats, done = rest
    fetch(parts, pool, sems, zip(wholes, (mask, kv, qg, stats, done)), only_x=True)
    zh, p, h = pos[0], pos[1], pos[2]

    def stats_of(other):
        return read_stats(stats, 4, other)

    dk, dv = key_terms(jnp.int32(4), zh, p, mask, kv, qg, pool, stats_of)
    dk = unturn(dk * SCALE, frames, rates, zh * PLANE + p).astype(BF16)
    dv = dv.astype(BF16)
    for b in range(4):
        to = lax.rem(b - h + 4, 4)
        o_ref[to, 0] = done[b, 0]
        o_ref[to, 1] = done[b, 1]
        o_ref[to, 2] = dk[b * QTR : (b + 1) * QTR]
        o_ref[to, 3] = dv[b * QTR : (b + 1) * QTR]


def cost(pairs, products):
    return pl.CostEstimate(
        flops=pairs * products * 2 * TOK * TOK * E,
        bytes_accessed=8 * 2**20,
        transcendentals=pairs * TOK * TOK,
    )


LIMIT = pltpu.CompilerParams(vmem_limit_bytes=60 * 2**20)


POOL = [
    pltpu.VMEM((SLOTS, 4, 2, QTR, E), BF16),
    pltpu.SemaphoreType.DMA((2 * PARTS + 5,)),
    pltpu.SMEM((2 * GROUPS, 2 * GROUPS), jnp.int32),
    pltpu.VMEM((4, 4, 2, 2, QTR, E), BF16),
    pltpu.VMEM((4, 4, 2, 2, QTR, E), BF16),
]
EVERY = pltpu.VMEM((GROUPS, SROWS, E), F32)


def side(kernel, out_shape, scratch, pairs, products, scalars, arrays):
    outs = out_shape if isinstance(out_shape, tuple) else (out_shape,)
    specs = [SMEM, SMEM, VMEM][: len(scalars)]
    return pl.pallas_call(
        kernel,
        out_shape=out_shape,
        in_specs=specs + [HBM] * len(arrays),
        out_specs=(VMEM,) * len(outs) if isinstance(out_shape, tuple) else VMEM,
        scratch_shapes=POOL + scratch,
        compiler_params=LIMIT,
        cost_estimate=cost(pairs, products),
        name=kernel.__name__,
    )(*scalars, *arrays)


def blocks(units, tensors):
    return jax.ShapeDtypeStruct((units, 4, tensors, QTR, E), BF16)


def forward_side(pos, mask, kv, qg, parts):
    shapes = (blocks(UNITS, 1), jax.ShapeDtypeStruct((SROWS, E), F32))
    scratch = [pltpu.VMEM((len(OFFSETS), TOK, TOK), F32)]
    return side(forward_kernel, shapes, scratch, 65, 2, (pos,), (*parts, mask, kv, qg))


def query_side(scalars, mask, kv, qg, att, stats, parts):
    scratch = [pltpu.VMEM((UNITS, 4, 1, QTR, E), BF16), pltpu.VMEM((SROWS, E), F32)]
    arrays = (*parts, mask, kv, qg, att, stats)
    return side(query_kernel, blocks(UNITS, 2), scratch, 65, 3, scalars, arrays)


def key_side(scalars, mask, kv, qg, stats, parts):
    return side(
        key_kernel, blocks(ZG, 2), [EVERY], 52, 4, scalars, (*parts, mask, kv, qg, stats)
    )


def extra_key_side(scalars, mask, kv, qg, stats, done, parts):
    shape = jax.ShapeDtypeStruct((4, 4, QTR, E), BF16)
    scratch = [EVERY, pltpu.VMEM((4, 2, QTR, E), BF16)]
    arrays = (*parts, mask, kv, qg, stats, done)
    return side(extra_key_kernel, shape, scratch, 13, 4, scalars, arrays)


def turn_rates():
    rates = np.zeros((8, E), np.float32)
    rates[0, :HALF] = 10000.0 ** (-2.0 * np.arange(HALF, dtype=np.float32) / ROT)
    rates[0, HALF:ROT] = rates[0, :HALF]
    rates[1, HALF:ROT] = 1.0
    rates[2, :HALF] = -1.0
    return rates


def move(value, rule):
    pairs = []
    for y in range(4):
        for x in range(4):
            to = rule(x, y)
            if to is not None:
                pairs.append((4 * y + x, 4 * (to[1] % 4) + to[0] % 4))
    return lax.ppermute(value, "p", pairs)


def start_exchange(own):
    across = move(own, lambda x, y: (x + 2, y))
    up = move(own, lambda x, y: (x, y + 1))
    down = move(own, lambda x, y: (x, y - 1))
    return up, down, across


def end_exchange(own5, up, down, across, turned):
    eight = move(turned, lambda x, y: (x, y - 1) if x < 2 else (x, y + 1))
    aslant = move(across, lambda x, y: (x, y + 1) if x < 2 else (x, y - 1))
    wrap = move(turned, lambda x, y: (3 - x, y) if x in (0, 3) else None)
    left = move(own5, lambda x, y: (x + 1, y) if x < 3 else None)
    right = move(own5, lambda x, y: (x - 1, y) if x > 0 else None)
    return up, down, eight, across, aslant, wrap, left, right


def slots_of(m, x, zh, p):
    first = lax.dynamic_slice_in_dim(x, zh, 1, axis=0)
    wrap = jnp.clip(zh + jnp.where(p < 8, 1, -1), 0, ZG - 1)
    return jnp.concatenate([first, m, lax.dynamic_slice_in_dim(x, wrap, 1, axis=0)], axis=0)


def gather_heads(packed):
    wide = lax.all_to_all(packed, ("zh", "h"), 0, 0, tiled=True)
    return wide.reshape(4, 4, 2, 2, QTR, E)


def shards(queries, key_vectors, value_vectors, grad_output, block_mask, block_frame):
    zh, p, h = lax.axis_index("zh"), lax.axis_index("p"), lax.axis_index("h")
    pos = jnp.stack([zh, p, h]).astype(jnp.int32)
    rates = turn_rates()
    low = lax.rem(p, 4) < 2
    kv = gather_heads(pack(pos, block_frame, rates, key_vectors, value_vectors))
    qg = pack(pos, block_frame, rates, queries, grad_output)
    kv_own = slots_of(kv[:, :, 0], kv[:, :, 1], zh, p)
    up, down, across = start_exchange(kv_own)
    qg, up, down, across = lax.optimization_barrier((qg, up, down, across))
    kv_parts = end_exchange(kv_own[:5], up, down, across, jnp.where(low, down, up))
    qg = gather_heads(qg)
    qg_own = slots_of(qg[:, :, 0], qg[:, :, 1], zh, p)
    qg_own, kv_some = lax.optimization_barrier((qg_own, kv_parts[2:6]))
    kv_parts = kv_parts[:2] + tuple(kv_some) + kv_parts[6:]
    up, down, across = start_exchange(qg_own)
    att, stats = forward_side(pos, block_mask, kv, qg, kv_parts)
    turned = jnp.where(low, down, up)
    own5, turned, across, att, stats = lax.optimization_barrier(
        (qg_own[:5], turned, across, att, stats)
    )
    qg_parts = end_exchange(own5, up, down, across, turned)
    every = lax.all_to_all(
        jnp.broadcast_to(stats[None], (GROUPS, SROWS, E)), ("zh", "p"), 0, 0, tiled=True
    )
    scalars = (pos, block_frame, rates)
    am = query_side(scalars, block_mask, kv, qg, att, stats, kv_parts)
    am, every, qg_parts = lax.optimization_barrier((am, every, qg_parts))
    bm = key_side(scalars, block_mask, kv, qg, every, qg_parts)
    out = lax.all_to_all(am[:4].reshape(16, 2, QTR, E), ("zh", "h"), 0, 0, tiled=True)
    out, bm = lax.optimization_barrier((out, bm))
    x = extra_key_side(scalars, block_mask, kv, qg, every, am[4], qg_parts)
    pieces = [x[0]] + [
        lax.ppermute(x[n], "h", [(i, (i + n) % 4) for i in range(4)]) for n in range(1, 4)
    ]
    bm = lax.all_to_all(bm.reshape(16, 2, QTR, E), ("zh", "h"), 0, 0, tiled=True)
    return unpack(pos, out, bm, pieces)


def solution(mesh):
    fine = Mesh(mesh.devices.reshape(ZG, PLANE, 4), ("zh", "p", "h"))
    tok = P(("zh", "p", "h"), None, None)
    return jax.shard_map(
        shards,
        mesh=fine,
        in_specs=(tok, tok, tok, tok, P(), P()),
        out_specs=(tok, tok, tok, tok),
        check_vma=False,
    )
```

time: 244 us -> 222 us (0.910)
  blocking collectives: 40.3 us -> 0 us
  Pallas kernels: 48.9 us -> 66.1 us
  starting transfers between devices: 58.9 us -> 70.6 us
  other arithmetic: 9.46 us -> 3.77 us
  local copies, waits for them, and re-layouts: 16.5 us -> 11.3 us
    all_to_all x3 -> x0, blocking collectives: 40.3 us -> none  [the longest x1 22.8 us: leave(): m = lax.all_to_all(m, ('zh', 'h'), 0, 0, tiled=True)]
    all_to_all x2, waiting for transfers between devices: 26.1 us -> 43.5 us  [gather_heads(): wide = lax.all_to_all(packed, ('zh', 'h'), 0, 0, tiled=True)]
    pallas_call x7, Pallas kernels: 48.9 us -> 66.1 us  [the longest x4 57.8 us: side(): pl.pallas_call(kernel, out_shape=out_shape, in_specs=specs + [HBM] * len(...]
    ppermute x16, waiting for transfers between devices: 31.1 us -> 20.9 us  [move(): return lax.ppermute(value, 'p', pairs)]
    all_to_all x3, waiting for transfers between devices: 10.8 us -> 1.33 us  [the longest x1 1.33 us: shards(): lax.all_to_all(bm.reshape(16, 2, QTR, E), ('zh', 'h'), 0, 0, tiled=True)]
    unnamed x42 -> x36, local copies, waits for them, and re-layouts: 10.4 us -> 3.7 us
    ppermute x16, starting transfers between devices: 25.6 us -> 31.9 us  [move(): return lax.ppermute(value, 'p', pairs)]
    ppermute x0 -> x3, starting transfers between devices: none -> 3.41 us  [shards(): lax.ppermute(x[n], 'h', [(i, (i + n) % 4) for i in range(4)])]
  transfers between devices with their start and end apart: 21 -> 24, of which waited for: 7 -> 9; matrix products, arithmetic and copies ran while one was open for 6% -> 3% of each run, Pallas kernels for 13% -> 28%
where the time goes in v3:
time: 222 us; the launch traced here: 221 us
  starting transfers between devices  70.6 us (32%)
  waiting for transfers between devices  68.1 us (31%)
  Pallas kernels  66.1 us (30%)
  local copies, waits for them, and re-layouts  11.3 us (5%)
  other arithmetic  3.77 us (2%)
    pallas_call x4, Pallas kernels, side(): pl.pallas_call(kernel, out_shape=out_shape, in_specs=specs + [HBM] * len(...  57.8 us
    all_to_all x2, waiting for transfers between devices, gather_heads(): wide = lax.all_to_all(packed, ('zh', 'h'), 0, 0, tiled=True)  43.5 us
    ppermute x16, starting transfers between devices, move(): return lax.ppermute(value, 'p', pairs)  31.9 us
    ppermute x16, waiting for transfers between devices, move(): return lax.ppermute(value, 'p', pairs)  20.9 us
    all_to_all x2, starting transfers between devices, gather_heads(): wide = lax.all_to_all(packed, ('zh', 'h'), 0, 0, tiled=True)  13.8 us
    all_to_all x1, starting transfers between devices, shards(): lax.all_to_all(am[:4].reshape(16, 2, QTR, E), ('zh', 'h'), 0, 0, tiled=True)  9.59 us
    all_to_all x1, starting transfers between devices, shards(): lax.all_to_all(bm.reshape(16, 2, QTR, E), ('zh', 'h'), 0, 0, tiled=True)  7.23 us
    pallas_call x2, Pallas kernels, pack(): pl.pallas_call(pack_kernel, out_shape=WIDE, in_specs=[SMEM, SMEM, VMEM, H...  6.04 us
  transfers between devices with their start and end apart: 24, of which 9 were waited for; matrix products, arithmetic and copies ran while one was open for 3% of the time, Pallas kernels for 28%

profile of v3, /device:TPU:1, one launch (start us, length us, event | category | flops | bytes accessed | tf_op | source)
XLA Modules:
  0.0 220.9 jit_solution(3669707100668311281)
XLA Ops:
  0.6 0.6 pad_add_fusion.pos
  1.3 3.0 %pack.3 = bf16[16,2,2,64,128]{4,3,2,1,0:T(8,128)(2,1)} custom-call(s32[3]{0:T(128)} %pad_add_fusion.pos, s32[128]{0:T(128)} %frames.9, f32[8,128]{1,0:T(8,128)} %constant.36.clone.rates, bf16[20,64,128]{2,1,0:T(8,128)(2,1)} %bitcast.49, bf16[20,64,128]{2,1,0:T(8,128)(2,1)} %bitcast.50), custom_call_target="tpu_custom_call" | custom-call | tf_op jit(solution)/shard_map/pack/pallas_call | solution.py:66
  4.3 10.0 %all-to-all-start = ((bf16[16,2,2,64,128]{4,3,2,1,0:T(8,128)(2,1)}), bf16[16,2,2,64,128]{4,3,2,1,0:T(8,128)(2,1)S(1)}, u32[]{:S(2)}, u32[]{:S(2)}) async-start(bf16[16,2,2,64,128]{4,3,2,1,0:T(8,128)(2,1)} %pack.3), calls=%async_computation | async-start | bytes 2097152 | tf_op jit(solution)/shard_map/all_to_all | solution.py:443
  14.3 27.9 %all-to-all-done = bf16[16,2,2,64,128]{4,3,2,1,0:T(8,128)(2,1)S(1)} async-done(((bf16[16,2,2,64,128]{4,3,2,1,0:T(8,128)(2,1)}), bf16[16,2,2,64,128]{4,3,2,1,0:T(8,128)(2,1)S(1)}, u32[]{:S(2)}, u32[]{:S(2)}) %all-to-all-start) | async-done | bytes 1048608 | tf_op jit(solution)/shard_map/all_to_all | solution.py:443
  42.4 0.9 copy-done
  43.5 2.8 %collective-permute-start.2 = (bf16[6,4,2,64,128]{4,3,2,1,0:T(8,128)(2,1)S(1)}, bf16[6,4,2,64,128]{4,3,2,1,0:T(8,128)(2,1)}, u32[]{:S(2)}, u32[]{:S(2)}) collective-permute-start(bf16[6,4,2,64,128]{4,3,2,1,0:T(8,128)(2,1)S(1)} %pad_maximum_fusion), channel_id=1, source_target_pairs={{0,8},{4,12},{8,0},{12,4},{16,24},{20,28},{24,16},{28,20},{32,40},... | collective-permute-start | bytes 2359304 | tf_op jit(solution)/shard_map/ppermute | solution.py:417
  46.3 2.7 %collective-permute-start.1 = (bf16[6,4,2,64,128]{4,3,2,1,0:T(8,128)(2,1)S(1)}, bf16[6,4,2,64,128]{4,3,2,1,0:T(8,128)(2,1)S(1)}, u32[]{:S(2)}, u32[]{:S(2)}) collective-permute-start(bf16[6,4,2,64,128]{4,3,2,1,0:T(8,128)(2,1)S(1)} %pad_maximum_fusion), channel_id=1, source_target_pairs={{0,48},{4,52},{8,56},{12,60},{16,0},{20,4},{24,8},{28,12},{32,16},... | collective-permute-start | bytes 2359304 | tf_op jit(solution)/shard_map/ppermute | solution.py:417
  49.1 3.0 %pack.2 = bf16[16,2,2,64,128]{4,3,2,1,0:T(8,128)(2,1)} custom-call(s32[3]{0:T(128)} %pad_add_fusion.pos, s32[128]{0:T(128)} %frames.9, f32[8,128]{1,0:T(8,128)} %constant.36.clone.rates, bf16[20,64,128]{2,1,0:T(8,128)(2,1)} %bitcast.51, bf16[20,64,128]{2,1,0:T(8,128)(2,1)} %bitcast.52), custom_call_target="tpu_custom_call" | custom-call | tf_op jit(solution)/shard_map/pack/pallas_call | solution.py:66
  52.1 11.7 %collective-permute-done.2.refs_3_ = bf16[6,4,2,64,128]{4,3,2,1,0:T(8,128)(2,1)} collective-permute-done((bf16[6,4,2,64,128]{4,3,2,1,0:T(8,128)(2,1)S(1)}, bf16[6,4,2,64,128]{4,3,2,1,0:T(8,128)(2,1)}, u32[]{:S(2)}, u32[]{:S(2)}) %collective-permute-start.2) | collective-permute-done | bytes 786464 | tf_op jit(solution)/shard_map/ppermute | solution.py:417
  63.7 2.2 %collective-permute-done.1.refs_1_ = bf16[6,4,2,64,128]{4,3,2,1,0:T(8,128)(2,1)S(1)} collective-permute-done((bf16[6,4,2,64,128]{4,3,2,1,0:T(8,128)(2,1)S(1)}, bf16[6,4,2,64,128]{4,3,2,1,0:T(8,128)(2,1)S(1)}, u32[]{:S(2)}, u32[]{:S(2)}) %collective-permute-start.1) | collective-permute-done | bytes 786464 | tf_op jit(solution)/shard_map/ppermute | solution.py:417
  66.0 3.5 %collective-permute-done.refs_0_ = bf16[6,4,2,64,128]{4,3,2,1,0:T(8,128)(2,1)S(1)} collective-permute-done((bf16[6,4,2,64,128]{4,3,2,1,0:T(8,128)(2,1)S(1)}, bf16[6,4,2,64,128]{4,3,2,1,0:T(8,128)(2,1)S(1)}, u32[]{:S(2)}, u32[]{:S(2)}) %collective-permute-start) | collective-permute-done | bytes 786464 | tf_op jit(solution)/shard_map/ppermute | solution.py:417
  69.5 3.8 %all-to-all-start.1 = ((bf16[16,2,2,64,128]{4,3,2,1,0:T(8,128)(2,1)}), bf16[16,2,2,64,128]{4,3,2,1,0:T(8,128)(2,1)S(1)}, u32[]{:S(2)}, u32[]{:S(2)}) async-start(bf16[16,2,2,64,128]{4,3,2,1,0:T(8,128)(2,1)} %pack.2), calls=%async_computation.1 | async-start | bytes 2097152 | tf_op jit(solution)/shard_map/all_to_all | solution.py:443
  73.4 1.0 broadcast_select_fusion.1
  74.3 2.8 %collective-permute-start.5 = (bf16[6,4,2,64,128]{4,3,2,1,0:T(8,128)(2,1)}, bf16[6,4,2,64,128]{4,3,2,1,0:T(8,128)(2,1)S(1)}, u32[]{:S(2)}, u32[]{:S(2)}) collective-permute-start(bf16[6,4,2,64,128]{4,3,2,1,0:T(8,128)(2,1)} %broadcast_select_fusion.1), channel_id=1, source_target_pairs={{0,12},{12,0},{16,28},{28,16},{32,44},{44,32},{48,60},{60,48},{1,1... | collective-permute-start | bytes 2359304 | tf_op jit(solution)/shard_map/ppermute | solution.py:417
  77.2 1.4 collective-permute-start.4
  78.7 0.9 pad_maximum_fusion.2
  79.6 1.3 collective-permute-start.7
  80.9 4.9 %collective-permute-start.6 = (bf16[5,4,2,64,128]{4,3,2,1,0:T(8,128)(2,1)}, bf16[5,4,2,64,128]{4,3,2,1,0:T(8,128)(2,1)}, u32[]{:S(2)}, u32[]{:S(2)}) collective-permute-start(bf16[5,4,2,64,128]{4,3,2,1,0:T(8,128)(2,1)} %pad_maximum_fusion.2), channel_id=1, source_target_pairs={{0,4},{4,8},{8,12},{16,20},{20,24},{24,28},{32,36},{36,40},{40,44}... | collective-permute-start | bytes 1966088 | tf_op jit(solution)/shard_map/ppermute | solution.py:417
  85.7 15.6 %all-to-all-done.1 = bf16[16,2,2,64,128]{4,3,2,1,0:T(8,128)(2,1)S(1)} async-done(((bf16[16,2,2,64,128]{4,3,2,1,0:T(8,128)(2,1)}), bf16[16,2,2,64,128]{4,3,2,1,0:T(8,128)(2,1)S(1)}, u32[]{:S(2)}, u32[]{:S(2)}) %all-to-all-start.1) | async-done | bytes 1048608 | tf_op jit(solution)/shard_map/all_to_all | solution.py:443
  101.5 0.9 copy-done.1
  102.6 2.7 %collective-permute-start.8 = (bf16[6,4,2,64,128]{4,3,2,1,0:T(8,128)(2,1)S(1)}, bf16[6,4,2,64,128]{4,3,2,1,0:T(8,128)(2,1)S(1)}, u32[]{:S(2)}, u32[]{:S(2)}) collective-permute-start(bf16[6,4,2,64,128]{4,3,2,1,0:T(8,128)(2,1)S(1)} %pad_maximum_fusion.1), channel_id=1, source_target_pairs={{0,48},{4,52},{8,56},{12,60},{16,0},{20,4},{24,8},{28,12},{32,16},... | collective-permute-start | bytes 2359304 | tf_op jit(solution)/shard_map/ppermute | solution.py:417
  105.5 0.9 slice.39
  106.4 14.9 %forward_kernel.1 = (bf16[5,4,1,64,128]{4,3,2,1,0:T(8,128)(2,1)}, f32[24,128]{1,0:T(8,128)}) custom-call(s32[3]{0:T(128)} %pad_add_fusion.pos, bf16[6,4,2,64,128]{4,3,2,1,0:T(8,128)(2,1)} %copy-done.3, bf16[6,4,2,64,128]{4,3,2,1,0:T(8,128)(2,1)} %copy-done.2, bf16[6,4,2,64,128]{4,3,2,1,0:T(8,128)(2,1)} %copy-done.10, ...), custom_call_target="tpu_custom_call" | custom-call | flops 2181038080 | bytes 8388608 | tf_op jit(solution)/shard_map/forward_kernel/pallas_call | solution.py:360
  121.3 1.4 collective-permute-done.9.refs_0_
  122.8 1.1 broadcast_select_fusion
  123.9 0.3 copy-done.5
  124.2 2.0 collective-permute-done.10.refs_3_
  126.2 0.9 broadcast_in_dim.2
  127.1 4.6 %all-to-all-start.2 = ((f32[64,24,128]{2,1,0:T(8,128)}), f32[64,24,128]{2,1,0:T(8,128)S(1)}, u32[]{:S(2)}, u32[]{:S(2)}) async-start(f32[64,24,128]{2,1,0:T(8,128)} %broadcast_in_dim.2), calls=%async_computation.2 | async-start | bytes 1572864 | tf_op jit(solution)/shard_map/all_to_all | solution.py:469
  131.8 4.0 %collective-permute-start.13 = (bf16[6,4,2,64,128]{4,3,2,1,0:T(8,128)(2,1)}, bf16[6,4,2,64,128]{4,3,2,1,0:T(8,128)(2,1)S(1)}, u32[]{:S(2)}, u32[]{:S(2)}) collective-permute-start(bf16[6,4,2,64,128]{4,3,2,1,0:T(8,128)(2,1)} %broadcast_select_fusion), channel_id=1, source_target_pairs={{0,12},{12,0},{16,28},{28,16},{32,44},{44,32},{48,60},{60,48},{1,1... | collective-permute-start | bytes 2359304 | tf_op jit(solution)/shard_map/ppermute | solution.py:417
  135.8 2.7 %collective-permute-start.11 = (bf16[6,4,2,64,128]{4,3,2,1,0:T(8,128)(2,1)}, bf16[6,4,2,64,128]{4,3,2,1,0:T(8,128)(2,1)S(1)}, u32[]{:S(2)}, u32[]{:S(2)}) collective-permute-start(bf16[6,4,2,64,128]{4,3,2,1,0:T(8,128)(2,1)} %broadcast_select_fusion), channel_id=1, source_target_pairs={{0,48},{4,52},{8,24},{12,28},{16,0},{20,4},{24,40},{28,44},{32,16}... | collective-permute-start | bytes 2359304 | tf_op jit(solution)/shard_map/ppermute | solution.py:417
  138.5 1.3 collective-permute-start.15
  139.8 4.9 %collective-permute-start.14 = (bf16[5,4,2,64,128]{4,3,2,1,0:T(8,128)(2,1)}, bf16[5,4,2,64,128]{4,3,2,1,0:T(8,128)(2,1)}, u32[]{:S(2)}, u32[]{:S(2)}) collective-permute-start(bf16[5,4,2,64,128]{4,3,2,1,0:T(8,128)(2,1)} %slice.39), channel_id=1, source_target_pairs={{0,4},{4,8},{8,12},{16,20},{20,24},{24,28},{32,36},{36,40},{40,44}... | collective-permute-start | bytes 1966088 | tf_op jit(solution)/shard_map/ppermute | solution.py:417
  144.7 18.4 %query_kernel.1 = bf16[5,4,2,64,128]{4,3,2,1,0:T(8,128)(2,1)} custom-call(s32[3]{0:T(128)} %pad_add_fusion.pos, s32[128]{0:T(128)} %frames.9, f32[8,128]{1,0:T(8,128)} %constant.36.clone.rates, bf16[6,4,2,64,128]{4,3,2,1,0:T(8,128)(2,1)} %copy-done.3, bf16[6,4,2,64,128]{4,3,2,1,0:T(8,128)(2,1)} %copy-done.2, bf16[6,4,2,64,128]{4,3,2,1,0:T(8,128)(2,1)} %copy-done.10, ...), custom_call_target="tpu_custom_call" | custom-call | flops 3271557120 | bytes 8388608 | tf_op jit(solution)/shard_map/query_kernel/pallas_call | solution.py:360
  163.2 2.3 %slice.40 = bf16[4,4,2,64,128]{4,3,2,1,0:T(8,128)(2,1)} slice(bf16[5,4,2,64,128]{4,3,2,1,0:T(8,128)(2,1)} %query_kernel.1), slice={[0:4], [0:4], [0:2], [0:64], [0:128]} | slice | bytes 1048576 | tf_op jit(solution)/shard_map/slice | solution.py:476
  165.5 9.6 %all-to-all-start.3 = ((bf16[16,2,64,128]{3,2,1,0:T(8,128)(2,1)}), bf16[16,2,64,128]{3,2,1,0:T(8,128)(2,1)S(1)}, u32[]{:S(2)}, u32[]{:S(2)}) async-start(bf16[16,2,64,128]{3,2,1,0:T(8,128)(2,1)} %bitcast.16), calls=%async_computation.3 | async-start | bytes 1048576 | tf_op jit(solution)/shard_map/all_to_all | solution.py:476
  175.1 17.3 %key_kernel.1 = bf16[4,4,2,64,128]{4,3,2,1,0:T(8,128)(2,1)} custom-call(s32[3]{0:T(128)} %pad_add_fusion.pos, s32[128]{0:T(128)} %frames.9, f32[8,128]{1,0:T(8,128)} %constant.36.clone.rates, bf16[6,4,2,64,128]{4,3,2,1,0:T(8,128)(2,1)} %copy-done.4, bf16[6,4,2,64,128]{4,3,2,1,0:T(8,128)(2,1)} %copy-done.5, bf16[6,4,2,64,128]{4,3,2,1,0:T(8,128)(2,1)} %copy-done.12, ...), custom_call_target="tpu_custom_call" | custom-call | flops 3489660928 | bytes 8388608 | tf_op jit(solution)/shard_map/key_kernel/pallas_call | solution.py:360
  192.4 0.8 copy-done.7
  193.2 7.2 %all-to-all-start.4 = ((bf16[16,2,64,128]{3,2,1,0:T(8,128)(2,1)}), bf16[16,2,64,128]{3,2,1,0:T(8,128)(2,1)S(1)}, u32[]{:S(2)}, u32[]{:S(2)}) async-start(bf16[16,2,64,128]{3,2,1,0:T(8,128)(2,1)} %bitcast.48), calls=%async_computation.4 | async-start | bytes 1048576 | tf_op jit(solution)/shard_map/all_to_all | solution.py:482
  200.4 1.6 slice_bitcast_fusion.2.refs_12_
  202.0 7.1 %extra_key_kernel.1 = bf16[4,4,64,128]{3,2,1,0:T(8,128)(2,1)} custom-call(s32[3]{0:T(128)} %pad_add_fusion.pos, s32[128]{0:T(128)} %frames.9, f32[8,128]{1,0:T(8,128)} %constant.36.clone.rates, bf16[6,4,2,64,128]{4,3,2,1,0:T(8,128)(2,1)} %copy-done.4, bf16[6,4,2,64,128]{4,3,2,1,0:T(8,128)(2,1)} %copy-done.5, bf16[6,4,2,64,128]{4,3,2,1,0:T(8,128)(2,1)} %copy-done.12, ...), custom_call_target="tpu_custom_call" | custom-call | flops 872415232 | bytes 8388608 | tf_op jit(solution)/shard_map/extra_key_kernel/pallas_call | solution.py:360
  209.2 1.6 slice_bitcast_fusion.3
  210.8 1.7 collective-permute-start.17
  212.5 1.6 collective-permute-start.16
  214.1 2.3 %collective-permute-done.18.refs_3_ = bf16[4,64,128]{2,1,0:T(8,128)(2,1)S(1)} collective-permute-done((bf16[4,64,128]{2,1,0:T(8,128)(2,1)S(1)}, bf16[4,64,128]{2,1,0:T(8,128)(2,1)S(1)}, u32[]{:S(2)}, u32[]{:S(2)}) %collective-permute-start.18) | collective-permute-done | bytes 65568 | tf_op jit(solution)/shard_map/ppermute | solution.py:480
  216.5 1.3 all-to-all-done.4.b_ref
  217.8 0.8 copy-done.8
  218.6 2.3 %unpack.1 = (bf16[20,64,128]{2,1,0:T(8,128)(2,1)}, bf16[20,64,128]{2,1,0:T(8,128)(2,1)}, bf16[20,64,128]{2,1,0:T(8,128)(2,1)}, bf16[20,64,128]{2,1,0:T(8,128)(2,1)}) custom-call(s32[3]{0:T(128)} %pad_add_fusion.pos, bf16[16,2,64,128]{3,2,1,0:T(8,128)(2,1)} %copy-done.7, bf16[16,2,64,128]{3,2,1,0:T(8,128)(2,1)} %copy-done.8, ...), custom_call_target="tpu_custom_call" | custom-call | tf_op jit(solution)/shard_map/unpack/pallas_call | solution.py:91
  (59 shorter events, 1.2 us)
Async XLA Ops:
  4.3 37.9 %all-to-all-start = ((bf16[16,2,2,64,128]{4,3,2,1,0:T(8,128)(2,1)}), bf16[16,2,2,64,128]{4,3,2,1,0:T(8,128)(2,1)S(1)}, u32[]{:S(2)}, u32[]{:S(2)}) async-start(bf16[16,2,2,64,128]{4,3,2,1,0:T(8,128)(2,1)} %pack.3), calls=%async_computation | async-start | bytes 2097152 | tf_op jit(solution)/shard_map/all_to_all | solution.py:443
  42.2 1.0 copy-start
  43.5 20.2 %collective-permute-start.2 = (bf16[6,4,2,64,128]{4,3,2,1,0:T(8,128)(2,1)S(1)}, bf16[6,4,2,64,128]{4,3,2,1,0:T(8,128)(2,1)}, u32[]{:S(2)}, u32[]{:S(2)}) collective-permute-start(bf16[6,4,2,64,128]{4,3,2,1,0:T(8,128)(2,1)S(1)} %pad_maximum_fusion), channel_id=1, source_target_pairs={{0,8},{4,12},{8,0},{12,4},{16,24},{20,28},{24,16},{28,20},{32,40},... | collective-permute-start | bytes 2359304 | tf_op jit(solution)/shard_map/ppermute | solution.py:417
  46.3 19.7 %collective-permute-start.1 = (bf16[6,4,2,64,128]{4,3,2,1,0:T(8,128)(2,1)S(1)}, bf16[6,4,2,64,128]{4,3,2,1,0:T(8,128)(2,1)S(1)}, u32[]{:S(2)}, u32[]{:S(2)}) collective-permute-start(bf16[6,4,2,64,128]{4,3,2,1,0:T(8,128)(2,1)S(1)} %pad_maximum_fusion), channel_id=1, source_target_pairs={{0,48},{4,52},{8,56},{12,60},{16,0},{20,4},{24,8},{28,12},{32,16},... | collective-permute-start | bytes 2359304 | tf_op jit(solution)/shard_map/ppermute | solution.py:417
  49.1 20.5 %collective-permute-start = (bf16[6,4,2,64,128]{4,3,2,1,0:T(8,128)(2,1)S(1)}, bf16[6,4,2,64,128]{4,3,2,1,0:T(8,128)(2,1)S(1)}, u32[]{:S(2)}, u32[]{:S(2)}) collective-permute-start(bf16[6,4,2,64,128]{4,3,2,1,0:T(8,128)(2,1)S(1)} %pad_maximum_fusion), channel_id=1, source_target_pairs={{0,16},{4,20},{8,24},{12,28},{16,32},{20,36},{24,40},{28,44},{32,4... | collective-permute-start | bytes 2359304 | tf_op jit(solution)/shard_map/ppermute | solution.py:417
  66.0 7.4 %copy-start.2 = (bf16[6,4,2,64,128]{4,3,2,1,0:T(8,128)(2,1)}, bf16[6,4,2,64,128]{4,3,2,1,0:T(8,128)(2,1)S(1)}, u32[]{:S(2)}) copy-start(bf16[6,4,2,64,128]{4,3,2,1,0:T(8,128)(2,1)S(1)} %collective-permute-done.1.refs_1_) | copy-start | bytes 2359300
  69.5 3.8 %copy-start.3 = (bf16[6,4,2,64,128]{4,3,2,1,0:T(8,128)(2,1)}, bf16[6,4,2,64,128]{4,3,2,1,0:T(8,128)(2,1)S(1)}, u32[]{:S(2)}) copy-start(bf16[6,4,2,64,128]{4,3,2,1,0:T(8,128)(2,1)S(1)} %collective-permute-done.refs_0_) | copy-start | bytes 2359300
  69.5 31.8 %all-to-all-start.1 = ((bf16[16,2,2,64,128]{4,3,2,1,0:T(8,128)(2,1)}), bf16[16,2,2,64,128]{4,3,2,1,0:T(8,128)(2,1)S(1)}, u32[]{:S(2)}, u32[]{:S(2)}) async-start(bf16[16,2,2,64,128]{4,3,2,1,0:T(8,128)(2,1)} %pack.2), calls=%async_computation.1 | async-start | bytes 2097152 | tf_op jit(solution)/shard_map/all_to_all | solution.py:443
  74.3 28.1 %collective-permute-start.5 = (bf16[6,4,2,64,128]{4,3,2,1,0:T(8,128)(2,1)}, bf16[6,4,2,64,128]{4,3,2,1,0:T(8,128)(2,1)S(1)}, u32[]{:S(2)}, u32[]{:S(2)}) collective-permute-start(bf16[6,4,2,64,128]{4,3,2,1,0:T(8,128)(2,1)} %broadcast_select_fusion.1), channel_id=1, source_target_pairs={{0,12},{12,0},{16,28},{28,16},{32,44},{44,32},{48,60},{60,48},{1,1... | collective-permute-start | bytes 2359304 | tf_op jit(solution)/shard_map/ppermute | solution.py:417
  77.1 25.4 %collective-permute-start.3 = (bf16[6,4,2,64,128]{4,3,2,1,0:T(8,128)(2,1)}, bf16[6,4,2,64,128]{4,3,2,1,0:T(8,128)(2,1)S(1)}, u32[]{:S(2)}, u32[]{:S(2)}) collective-permute-start(bf16[6,4,2,64,128]{4,3,2,1,0:T(8,128)(2,1)} %broadcast_select_fusion.1), channel_id=1, source_target_pairs={{0,48},{4,52},{8,24},{12,28},{16,0},{20,4},{24,40},{28,44},{32,16}... | collective-permute-start | bytes 2359304 | tf_op jit(solution)/shard_map/ppermute | solution.py:417
  77.2 25.3 %collective-permute-start.4 = (bf16[6,4,2,64,128]{4,3,2,1,0:T(8,128)(2,1)}, bf16[6,4,2,64,128]{4,3,2,1,0:T(8,128)(2,1)}, u32[]{:S(2)}, u32[]{:S(2)}) collective-permute-start(bf16[6,4,2,64,128]{4,3,2,1,0:T(8,128)(2,1)} %collective-permute-done.2.refs_3_), channel_id=1, source_target_pairs={{0,16},{4,20},{8,56},{12,60},{16,32},{20,36},{24,8},{28,12},{32,48... | collective-permute-start | bytes 2359304 | tf_op jit(solution)/shard_map/ppermute | solution.py:417
  79.6 26.8 %collective-permute-start.7 = (bf16[5,4,2,64,128]{4,3,2,1,0:T(8,128)(2,1)}, bf16[5,4,2,64,128]{4,3,2,1,0:T(8,128)(2,1)}, u32[]{:S(2)}, u32[]{:S(2)}) collective-permute-start(bf16[5,4,2,64,128]{4,3,2,1,0:T(8,128)(2,1)} %pad_maximum_fusion.2), channel_id=1, source_target_pairs={{4,0},{8,4},{12,8},{20,16},{24,20},{28,24},{36,32},{40,36},{44,40}... | collective-permute-start | bytes 1966088 | tf_op jit(solution)/shard_map/ppermute | solution.py:417
  80.9 25.5 %collective-permute-start.6 = (bf16[5,4,2,64,128]{4,3,2,1,0:T(8,128)(2,1)}, bf16[5,4,2,64,128]{4,3,2,1,0:T(8,128)(2,1)}, u32[]{:S(2)}, u32[]{:S(2)}) collective-permute-start(bf16[5,4,2,64,128]{4,3,2,1,0:T(8,128)(2,1)} %pad_maximum_fusion.2), channel_id=1, source_target_pairs={{0,4},{4,8},{8,12},{16,20},{20,24},{24,28},{32,36},{36,40},{40,44}... | collective-permute-start | bytes 1966088 | tf_op jit(solution)/shard_map/ppermute | solution.py:417
  101.3 1.0 copy-start.1
  102.5 3.9 %copy-start.9 = (bf16[6,4,2,64,128]{4,3,2,1,0:T(8,128)(2,1)}, bf16[6,4,2,64,128]{4,3,2,1,0:T(8,128)(2,1)S(1)}, u32[]{:S(2)}) copy-start(bf16[6,4,2,64,128]{4,3,2,1,0:T(8,128)(2,1)S(1)} %collective-permute-done.5.refs_5_) | copy-start | bytes 2359300
  102.5 3.9 %copy-start.10 = (bf16[6,4,2,64,128]{4,3,2,1,0:T(8,128)(2,1)}, bf16[6,4,2,64,128]{4,3,2,1,0:T(8,128)(2,1)S(1)}, u32[]{:S(2)}) copy-start(bf16[6,4,2,64,128]{4,3,2,1,0:T(8,128)(2,1)S(1)} %collective-permute-done.3.refs_2_) | copy-start | bytes 2359300
  102.5 20.3 %collective-permute-start.9 = (bf16[6,4,2,64,128]{4,3,2,1,0:T(8,128)(2,1)S(1)}, bf16[6,4,2,64,128]{4,3,2,1,0:T(8,128)(2,1)S(1)}, u32[]{:S(2)}, u32[]{:S(2)}) collective-permute-start(bf16[6,4,2,64,128]{4,3,2,1,0:T(8,128)(2,1)S(1)} %pad_maximum_fusion.1), channel_id=1, source_target_pairs={{0,16},{4,20},{8,24},{12,28},{16,32},{20,36},{24,40},{28,44},{32,4... | collective-permute-start | bytes 2359304 | tf_op jit(solution)/shard_map/ppermute | solution.py:417
  102.6 20.2 %collective-permute-start.8 = (bf16[6,4,2,64,128]{4,3,2,1,0:T(8,128)(2,1)S(1)}, bf16[6,4,2,64,128]{4,3,2,1,0:T(8,128)(2,1)S(1)}, u32[]{:S(2)}, u32[]{:S(2)}) collective-permute-start(bf16[6,4,2,64,128]{4,3,2,1,0:T(8,128)(2,1)S(1)} %pad_maximum_fusion.1), channel_id=1, source_target_pairs={{0,48},{4,52},{8,56},{12,60},{16,0},{20,4},{24,8},{28,12},{32,16},... | collective-permute-start | bytes 2359304 | tf_op jit(solution)/shard_map/ppermute | solution.py:417
  105.3 20.9 %collective-permute-start.10 = (bf16[6,4,2,64,128]{4,3,2,1,0:T(8,128)(2,1)S(1)}, bf16[6,4,2,64,128]{4,3,2,1,0:T(8,128)(2,1)}, u32[]{:S(2)}, u32[]{:S(2)}) collective-permute-start(bf16[6,4,2,64,128]{4,3,2,1,0:T(8,128)(2,1)S(1)} %pad_maximum_fusion.1), channel_id=1, source_target_pairs={{0,8},{4,12},{8,0},{12,4},{16,24},{20,28},{24,16},{28,20},{32,40},... | collective-permute-start | bytes 2359304 | tf_op jit(solution)/shard_map/ppermute | solution.py:417
  122.8 1.1 copy-start.4
  122.8 1.4 copy-start.5
  122.8 3.4 %copy-start.17 = (f32[24,128]{1,0:T(8,128)S(1)}, f32[24,128]{1,0:T(8,128)}, u32[]{:S(2)}) copy-start(f32[24,128]{1,0:T(8,128)} %get-tuple-element.48.refs_12_) | copy-start | bytes 36868
  127.1 36.1 %all-to-all-start.2 = ((f32[64,24,128]{2,1,0:T(8,128)}), f32[64,24,128]{2,1,0:T(8,128)S(1)}, u32[]{:S(2)}, u32[]{:S(2)}) async-start(f32[64,24,128]{2,1,0:T(8,128)} %broadcast_in_dim.2), calls=%async_computation.2 | async-start | bytes 1572864 | tf_op jit(solution)/shard_map/all_to_all | solution.py:469
  131.8 31.4 %collective-permute-start.13 = (bf16[6,4,2,64,128]{4,3,2,1,0:T(8,128)(2,1)}, bf16[6,4,2,64,128]{4,3,2,1,0:T(8,128)(2,1)S(1)}, u32[]{:S(2)}, u32[]{:S(2)}) collective-permute-start(bf16[6,4,2,64,128]{4,3,2,1,0:T(8,128)(2,1)} %broadcast_select_fusion), channel_id=1, source_target_pairs={{0,12},{12,0},{16,28},{28,16},{32,44},{44,32},{48,60},{60,48},{1,1... | collective-permute-start | bytes 2359304 | tf_op jit(solution)/shard_map/ppermute | solution.py:417
  135.8 27.4 %collective-permute-start.11 = (bf16[6,4,2,64,128]{4,3,2,1,0:T(8,128)(2,1)}, bf16[6,4,2,64,128]{4,3,2,1,0:T(8,128)(2,1)S(1)}, u32[]{:S(2)}, u32[]{:S(2)}) collective-permute-start(bf16[6,4,2,64,128]{4,3,2,1,0:T(8,128)(2,1)} %broadcast_select_fusion), channel_id=1, source_target_pairs={{0,48},{4,52},{8,24},{12,28},{16,0},{20,4},{24,40},{28,44},{32,16}... | collective-permute-start | bytes 2359304 | tf_op jit(solution)/shard_map/ppermute | solution.py:417
  138.5 24.7 %collective-permute-start.12 = (bf16[6,4,2,64,128]{4,3,2,1,0:T(8,128)(2,1)}, bf16[6,4,2,64,128]{4,3,2,1,0:T(8,128)(2,1)}, u32[]{:S(2)}, u32[]{:S(2)}) collective-permute-start(bf16[6,4,2,64,128]{4,3,2,1,0:T(8,128)(2,1)} %collective-permute-done.10.refs_3_), channel_id=1, source_target_pairs={{0,16},{4,20},{8,56},{12,60},{16,32},{20,36},{24,8},{28,12},{32,48... | collective-permute-start | bytes 2359304 | tf_op jit(solution)/shard_map/ppermute | solution.py:417
  138.5 24.6 %collective-permute-start.15 = (bf16[5,4,2,64,128]{4,3,2,1,0:T(8,128)(2,1)}, bf16[5,4,2,64,128]{4,3,2,1,0:T(8,128)(2,1)S(1)}, u32[]{:S(2)}, u32[]{:S(2)}) collective-permute-start(bf16[5,4,2,64,128]{4,3,2,1,0:T(8,128)(2,1)} %slice.39), channel_id=1, source_target_pairs={{4,0},{8,4},{12,8},{20,16},{24,20},{28,24},{36,32},{40,36},{44,40}... | collective-permute-start | bytes 1966088 | tf_op jit(solution)/shard_map/ppermute | solution.py:417
  139.8 23.3 %collective-permute-start.14 = (bf16[5,4,2,64,128]{4,3,2,1,0:T(8,128)(2,1)}, bf16[5,4,2,64,128]{4,3,2,1,0:T(8,128)(2,1)}, u32[]{:S(2)}, u32[]{:S(2)}) collective-permute-start(bf16[5,4,2,64,128]{4,3,2,1,0:T(8,128)(2,1)} %slice.39), channel_id=1, source_target_pairs={{0,4},{4,8},{8,12},{16,20},{20,24},{24,28},{32,36},{36,40},{40,44}... | collective-permute-start | bytes 1966088 | tf_op jit(solution)/shard_map/ppermute | solution.py:417
  163.2 12.0 %copy-start.13 = (bf16[5,4,2,64,128]{4,3,2,1,0:T(8,128)(2,1)}, bf16[5,4,2,64,128]{4,3,2,1,0:T(8,128)(2,1)S(1)}, u32[]{:S(2)}) copy-start(bf16[5,4,2,64,128]{4,3,2,1,0:T(8,128)(2,1)S(1)} %collective-permute-done.15.refs_7_) | copy-start | bytes 1966084
  163.2 2.3 %copy-start.11 = (bf16[6,4,2,64,128]{4,3,2,1,0:T(8,128)(2,1)}, bf16[6,4,2,64,128]{4,3,2,1,0:T(8,128)(2,1)S(1)}, u32[]{:S(2)}) copy-start(bf16[6,4,2,64,128]{4,3,2,1,0:T(8,128)(2,1)S(1)} %collective-permute-done.13.refs_5_) | copy-start | bytes 2359300
  163.2 11.9 %copy-start.12 = (bf16[6,4,2,64,128]{4,3,2,1,0:T(8,128)(2,1)}, bf16[6,4,2,64,128]{4,3,2,1,0:T(8,128)(2,1)S(1)}, u32[]{:S(2)}) copy-start(bf16[6,4,2,64,128]{4,3,2,1,0:T(8,128)(2,1)S(1)} %collective-permute-done.11.refs_2_) | copy-start | bytes 2359300
  163.2 2.3 %copy-start.6 = (f32[64,24,128]{2,1,0:T(8,128)}, f32[64,24,128]{2,1,0:T(8,128)S(1)}, u32[]{:S(2)}) copy-start(f32[64,24,128]{2,1,0:T(8,128)S(1)} %all-to-all-done.2.refs_11_) | copy-start | bytes 2359300
  165.5 26.9 %all-to-all-start.3 = ((bf16[16,2,64,128]{3,2,1,0:T(8,128)(2,1)}), bf16[16,2,64,128]{3,2,1,0:T(8,128)(2,1)S(1)}, u32[]{:S(2)}, u32[]{:S(2)}) async-start(bf16[16,2,64,128]{3,2,1,0:T(8,128)(2,1)} %bitcast.16), calls=%async_computation.3 | async-start | bytes 1048576 | tf_op jit(solution)/shard_map/all_to_all | solution.py:476
  192.4 0.8 copy-start.7
  193.2 24.6 %all-to-all-start.4 = ((bf16[16,2,64,128]{3,2,1,0:T(8,128)(2,1)}), bf16[16,2,64,128]{3,2,1,0:T(8,128)(2,1)S(1)}, u32[]{:S(2)}, u32[]{:S(2)}) async-start(bf16[16,2,64,128]{3,2,1,0:T(8,128)(2,1)} %bitcast.48), calls=%async_computation.4 | async-start | bytes 1048576 | tf_op jit(solution)/shard_map/all_to_all | solution.py:482
  210.7 5.7 %collective-permute-start.18 = (bf16[4,64,128]{2,1,0:T(8,128)(2,1)S(1)}, bf16[4,64,128]{2,1,0:T(8,128)(2,1)S(1)}, u32[]{:S(2)}, u32[]{:S(2)}) collective-permute-start(bf16[4,64,128]{2,1,0:T(8,128)(2,1)S(1)} %get-tuple-element.76), channel_id=1, source_target_pairs={{0,3},{1,0},{2,1},{3,2},{4,7},{5,4},{6,5},{7,6},{8,11},{9,8},{10,9... | collective-permute-start | bytes 196616 | tf_op jit(solution)/shard_map/ppermute | solution.py:480
  210.8 5.6 %collective-permute-start.17 = (bf16[4,64,128]{2,1,0:T(8,128)(2,1)S(1)}, bf16[4,64,128]{2,1,0:T(8,128)(2,1)S(1)}, u32[]{:S(2)}, u32[]{:S(2)}) collective-permute-start(bf16[4,64,128]{2,1,0:T(8,128)(2,1)S(1)} %get-tuple-element.77), channel_id=1, source_target_pairs={{0,2},{1,3},{2,0},{3,1},{4,6},{5,7},{6,4},{7,5},{8,10},{9,11},{10,... | collective-permute-start | bytes 196616 | tf_op jit(solution)/shard_map/ppermute | solution.py:480
  212.5 3.9 %collective-permute-start.16 = (bf16[4,64,128]{2,1,0:T(8,128)(2,1)S(1)}, bf16[4,64,128]{2,1,0:T(8,128)(2,1)S(1)}, u32[]{:S(2)}, u32[]{:S(2)}) collective-permute-start(bf16[4,64,128]{2,1,0:T(8,128)(2,1)S(1)} %get-tuple-element.78), channel_id=1, source_target_pairs={{0,1},{1,2},{2,3},{3,0},{4,5},{5,6},{6,7},{7,4},{8,9},{9,10},{10,1... | collective-permute-start | bytes 196616 | tf_op jit(solution)/shard_map/ppermute | solution.py:480
  216.4 1.4 copy-start.14
  216.4 1.4 copy-start.15
  216.5 1.3 copy-start.16
  217.8 0.8 copy-start.8

commit v4 on v3

--- a/solution.py
+++ b/solution.py
@@ -22,7 +22,8 @@
 SROWS = 24
 NEG = -1e30
 PARTS = 8
-OFFSETS = (0, 1, -1, 2, -2, 4, -4, 8, -8, 16, -16, 32, -32)
+OFFSETS = (0, 16, -16, 32, -32, 4, -4, 8, -8, 1, -1, 2, -2)
+FIRST_FAR = 4
 SLOTS = 46
 SCALE = 1.0 / math.sqrt(E)
 LOG2E = 1.4426950408889634
@@ -164,10 +165,17 @@
         at += size
     for n, (whole, target) in enumerate(wholes):
         copies.append(pltpu.make_async_copy(whole, target, sems.at[2 * PARTS + n]))
-    for copy in copies:
+    far_count = len(copies) - len(wholes)
+    for copy in copies[far_count:] + copies[:far_count]:
         copy.start()
-    for copy in copies:
+    for copy in copies[far_count:]:
         copy.wait()
+
+    def rest():
+        for copy in copies[:far_count]:
+            copy.wait()
+
+    return rest
 
 
 def near(ref, z, unit, which):
@@ -209,9 +217,9 @@
 
 
 def forward_kernel(pos, *refs):
-    parts, wholes, rest = refs[:PARTS], refs[PARTS : PARTS + 3], refs[PARTS + 3 :]
-    att_ref, stats, pool, sems, mask, kv, qg, scores = rest
-    fetch(parts, pool, sems, zip(wholes, (mask, kv, qg)))
+    parts, wholes, others = refs[:PARTS], refs[PARTS : PARTS + 3], refs[PARTS + 3 :]
+    att_ref, stats, pool, sems, mask, kv, qg, scores, weights, values = others
+    rest = fetch(parts, pool, sems, list(zip(wholes, (mask, kv, qg))))
     zh, p = pos[0], pos[1]
 
     def body(unit, carry):
@@ -220,6 +228,8 @@
         slots = []
         top = jnp.full((1, TOK), NEG, F32)
         for n, offset in enumerate(OFFSETS):
+            if offset == FIRST_FAR:
+                pl.when(unit == 0)(rest)
             group, other, valid, slot = source(offset, unit, zh, p)
             slots.append(slot)
             k = pool_rows(offset, slot, unit, kv, pool, 0)
@@ -228,12 +238,13 @@
             top = jnp.maximum(top, jnp.max(st, axis=0, keepdims=True))
         top = top * COEF
         total = jnp.zeros((1, TOK), F32)
-        out = jnp.zeros((E, TOK), F32)
         for n, offset in enumerate(OFFSETS):
             w = jnp.exp2(scores[n] * COEF - top)
             total = total + jnp.sum(w, axis=0, keepdims=True)
-            v = pool_rows(offset, slots[n], unit, kv, pool, 1)
-            out = out + dot(v, w.astype(BF16), 0, 0)
+            rows = slice(n * TOK, (n + 1) * TOK)
+            weights[rows] = w.astype(BF16)
+            values[rows] = pool_rows(offset, slots[n], unit, kv, pool, 1)
+        out = dot(values[...], weights[...], 0, 0)
         att = jnp.transpose(out * (1.0 / total)).astype(BF16)
         put(att_ref, unit, 0, att)
         g = near(qg, z, unit, 1).astype(F32)
@@ -248,9 +259,9 @@
 
 
 def query_kernel(pos, frames, rates, *refs):
-    parts, wholes, rest = refs[:PARTS], refs[PARTS : PARTS + 5], refs[PARTS + 5 :]
-    o_ref, pool, sems, mask, kv, qg, att, stats = rest
-    fetch(parts, pool, sems, zip(wholes, (mask, kv, qg, att, stats)))
+    parts, wholes, others = refs[:PARTS], refs[PARTS : PARTS + 5], refs[PARTS + 5 :]
+    m_ref, x_ref, pool, sems, mask, kv, qg, att, stats, dscores, keys, values, scores, products = others
+    rest = fetch(parts, pool, sems, list(zip(wholes, (mask, kv, qg, att, stats))))
     zh, p = pos[0], pos[1]
 
     def body(unit, carry):
@@ -258,53 +269,73 @@
         q = near(qg, z, unit, 0)
         g = near(qg, z, unit, 1)
         total, delta = read_stats(stats, unit)
-        dq = jnp.zeros((E, TOK), F32)
-        for offset in OFFSETS:
-            group, other, valid, slot = source(offset, unit, zh, p)
-            k = pool_rows(offset, slot, unit, kv, pool, 0)
-            v = pool_rows(offset, slot, unit, kv, pool, 1)
-            st = add_bias(dot(k, q, 1, 1), bias_of(mask, group, other, valid))
+        for n, offset in enumerate(OFFSETS):
+            if offset == FIRST_FAR:
+                pl.when(unit == 0)(rest)
+            slot = source(offset, unit, zh, p)[3]
+            keys[n * TOK : (n + 1) * TOK] = pool_rows(offset, slot, unit, kv, pool, 0)
+            values[n * TOK : (n + 1) * TOK] = pool_rows(offset, slot, unit, kv, pool, 1)
+        scores[...] = dot(keys[...], q, 1, 1)
+        products[...] = dot(values[...], g, 1, 1)
+        for n, offset in enumerate(OFFSETS):
+            group, other, valid, _ = source(offset, unit, zh, p)
+            rows = slice(n * TOK, (n + 1) * TOK)
+            st = add_bias(scores[rows], bias_of(mask, group, other, valid))
             w = jnp.exp2(st * COEF - total)
-            ds = (w * (dot(v, g, 1, 1) - delta)).astype(BF16)
-            dq = dq + dot(k, ds, 0, 0)
-        o_ref[unit, :, 0] = att[unit, :, 0]
-        dq = unturn(jnp.transpose(dq * SCALE), frames, rates, z * PLANE + p)
-        put(o_ref, unit, 1, dq.astype(BF16))
+            dscores[rows] = (w * (products[rows] - delta)).astype(BF16)
+        dq = dot(keys[...], dscores[...], 0, 0)
+        dq = unturn(jnp.transpose(dq * SCALE), frames, rates, z * PLANE + p).astype(BF16)
+
+        @pl.when(unit < 4)
+        def _():
+            m_ref[unit, :, 0] = att[unit, :, 0]
+            put(m_ref, unit, 1, dq)
+
+        @pl.when(unit == 4)
+        def _():
+            x_ref[0, :, 0] = att[4, :, 0]
+            put(x_ref, 0, 1, dq)
+
         return carry
 
     lax.fori_loop(0, UNITS, body, 0)
 
 
-def key_terms(unit, zh, p, mask, kv, qg, pool, stats_of):
+def key_terms(unit, zh, p, mask, kv, qg, pool, stats_of, rest, big):
     z = jnp.where(unit == 4, zh, unit)
     k = near(kv, z, unit, 0)
     v = near(kv, z, unit, 1)
-    dk = jnp.zeros((TOK, E), F32)
-    dv = jnp.zeros((TOK, E), F32)
-    for offset in OFFSETS:
+    weights, dscores, queries, grads = big
+    for n, offset in enumerate(OFFSETS):
+        if offset == FIRST_FAR:
+            rest()
         group, other, valid, slot = source(offset, unit, zh, p)
         total, delta = stats_of(other)
         q = pool_rows(offset, slot, unit, qg, pool, 0)
         g = pool_rows(offset, slot, unit, qg, pool, 1)
         st = add_bias(dot(k, q, 1, 1), bias_of(mask, other, group, valid))
         w = jnp.exp2(st * COEF - total)
-        ds = (w * (dot(v, g, 1, 1) - delta)).astype(BF16)
-        dv = dv + dot(w.astype(BF16), g, 1, 0)
-        dk = dk + dot(ds, q, 1, 0)
-    return dk, dv
+        cols = slice(n * TOK, (n + 1) * TOK)
+        weights[:, cols] = w.astype(BF16)
+        dscores[:, cols] = (w * (dot(v, g, 1, 1) - delta)).astype(BF16)
+        queries[cols] = q
+        grads[cols] = g
+    return dot(dscores[...], queries[...], 1, 0), dot(weights[...], grads[...], 1, 0)
 
 
 def key_kernel(pos, frames, rates, *refs):
-    parts, wholes, rest = refs[:PARTS], refs[PARTS : PARTS + 4], refs[PARTS + 4 :]
-    o_ref, pool, sems, mask, kv, qg, stats = rest
-    fetch(parts, pool, sems, zip(wholes, (mask, kv, qg, stats)))
+    parts, wholes, others = refs[:PARTS], refs[PARTS : PARTS + 4], refs[PARTS + 4 :]
+    o_ref, pool, sems, mask, kv, qg, stats, *big = others
+    rest = fetch(parts, pool, sems, list(zip(wholes, (mask, kv, qg, stats))))
     zh, p = pos[0], pos[1]
 
     def stats_of(other):
         return read_stats(stats, lax.div(other, PLANE), zh * PLANE + lax.rem(other, PLANE))
 
     def body(unit, carry):
-        dk, dv = key_terms(unit, zh, p, mask, kv, qg, pool, stats_of)
+        dk, dv = key_terms(
+            unit, zh, p, mask, kv, qg, pool, stats_of, lambda: pl.when(unit == 0)(rest), big
+        )
         dk = unturn(dk * SCALE, frames, rates, unit * PLANE + p)
         put(o_ref, unit, 0, dk.astype(BF16))
         put(o_ref, unit, 1, dv.astype(BF16))
@@ -314,23 +345,23 @@
 
 
 def extra_key_kernel(pos, frames, rates, *refs):
-    parts, wholes, rest = refs[:PARTS], refs[PARTS : PARTS + 5], refs[PARTS + 5 :]
-    o_ref, pool, sems, mask, kv, qg, stats, done = rest
-    fetch(parts, pool, sems, zip(wholes, (mask, kv, qg, stats, done)), only_x=True)
+    parts, wholes, others = refs[:PARTS], refs[PARTS : PARTS + 5], refs[PARTS + 5 :]
+    *pieces, pool, sems, mask, kv, qg, stats, done, c0, c1, c2, c3, sums = others
+    big = (c0, c1, c2, c3)
+    rest = fetch(parts, pool, sems, list(zip(wholes, (mask, kv, qg, stats, done))), only_x=True)
     zh, p, h = pos[0], pos[1], pos[2]
 
     def stats_of(other):
         return read_stats(stats, 4, other)
 
-    dk, dv = key_terms(jnp.int32(4), zh, p, mask, kv, qg, pool, stats_of)
-    dk = unturn(dk * SCALE, frames, rates, zh * PLANE + p).astype(BF16)
-    dv = dv.astype(BF16)
-    for b in range(4):
-        to = lax.rem(b - h + 4, 4)
-        o_ref[to, 0] = done[b, 0]
-        o_ref[to, 1] = done[b, 1]
-        o_ref[to, 2] = dk[b * QTR : (b + 1) * QTR]
-        o_ref[to, 3] = dv[b * QTR : (b + 1) * QTR]
+    dk, dv = key_terms(jnp.int32(4), zh, p, mask, kv, qg, pool, stats_of, rest, big)
+    put(sums, 0, 0, unturn(dk * SCALE, frames, rates, zh * PLANE + p).astype(BF16))
+    put(sums, 0, 1, dv.astype(BF16))
+    for n, piece in enumerate(pieces):
+        to = lax.rem(h + n, 4)
+        for i in range(2):
+            piece[i] = done[0, to, i]
+            piece[2 + i] = sums[0, to, i]
 
 
 def cost(pairs, products):
@@ -351,6 +382,11 @@
     pltpu.VMEM((4, 4, 2, 2, QTR, E), BF16),
     pltpu.VMEM((4, 4, 2, 2, QTR, E), BF16),
 ]
+ALL_SUMS = pltpu.VMEM((len(OFFSETS) * TOK, TOK), F32)
+ALL_PAIRS = pltpu.VMEM((len(OFFSETS) * TOK, TOK), BF16)
+ALL_ROWS = pltpu.VMEM((len(OFFSETS) * TOK, E), BF16)
+ALL_COLUMNS = pltpu.VMEM((TOK, len(OFFSETS) * TOK), BF16)
+BIG = [ALL_COLUMNS, ALL_COLUMNS, ALL_ROWS, ALL_ROWS]
 EVERY = pltpu.VMEM((GROUPS, SROWS, E), F32)
 
 
@@ -375,27 +411,28 @@
 
 def forward_side(pos, mask, kv, qg, parts):
     shapes = (blocks(UNITS, 1), jax.ShapeDtypeStruct((SROWS, E), F32))
-    scratch = [pltpu.VMEM((len(OFFSETS), TOK, TOK), F32)]
+    scratch = [pltpu.VMEM((len(OFFSETS), TOK, TOK), F32), ALL_PAIRS, ALL_ROWS]
     return side(forward_kernel, shapes, scratch, 65, 2, (pos,), (*parts, mask, kv, qg))
 
 
 def query_side(scalars, mask, kv, qg, att, stats, parts):
     scratch = [pltpu.VMEM((UNITS, 4, 1, QTR, E), BF16), pltpu.VMEM((SROWS, E), F32)]
+    scratch += [ALL_PAIRS, ALL_ROWS, ALL_ROWS, ALL_SUMS, ALL_SUMS]
     arrays = (*parts, mask, kv, qg, att, stats)
-    return side(query_kernel, blocks(UNITS, 2), scratch, 65, 3, scalars, arrays)
+    return side(query_kernel, (blocks(ZG, 2), blocks(1, 2)), scratch, 65, 3, scalars, arrays)
 
 
 def key_side(scalars, mask, kv, qg, stats, parts):
     return side(
-        key_kernel, blocks(ZG, 2), [EVERY], 52, 4, scalars, (*parts, mask, kv, qg, stats)
+        key_kernel, blocks(ZG, 2), [EVERY] + BIG, 52, 4, scalars, (*parts, mask, kv, qg, stats)
     )
 
 
 def extra_key_side(scalars, mask, kv, qg, stats, done, parts):
-    shape = jax.ShapeDtypeStruct((4, 4, QTR, E), BF16)
-    scratch = [EVERY, pltpu.VMEM((4, 2, QTR, E), BF16)]
+    pieces = (jax.ShapeDtypeStruct((4, QTR, E), BF16),) * 4
+    pair = pltpu.VMEM((1, 4, 2, QTR, E), BF16)
     arrays = (*parts, mask, kv, qg, stats, done)
-    return side(extra_key_kernel, shape, scratch, 13, 4, scalars, arrays)
+    return side(extra_key_kernel, pieces, [EVERY, pair] + BIG + [pair], 13, 4, scalars, arrays)
 
 
 def turn_rates():
@@ -470,15 +507,14 @@
         jnp.broadcast_to(stats[None], (GROUPS, SROWS, E)), ("zh", "p"), 0, 0, tiled=True
     )
     scalars = (pos, block_frame, rates)
-    am = query_side(scalars, block_mask, kv, qg, att, stats, kv_parts)
-    am, every, qg_parts = lax.optimization_barrier((am, every, qg_parts))
+    am, ax = query_side(scalars, block_mask, kv, qg, att, stats, kv_parts)
+    am, ax, every, qg_parts = lax.optimization_barrier((am, ax, every, qg_parts))
     bm = key_side(scalars, block_mask, kv, qg, every, qg_parts)
-    out = lax.all_to_all(am[:4].reshape(16, 2, QTR, E), ("zh", "h"), 0, 0, tiled=True)
+    out = lax.all_to_all(am.reshape(16, 2, QTR, E), ("zh", "h"), 0, 0, tiled=True)
     out, bm = lax.optimization_barrier((out, bm))
-    x = extra_key_side(scalars, block_mask, kv, qg, every, am[4], qg_parts)
-    pieces = [x[0]] + [
-        lax.ppermute(x[n], "h", [(i, (i + n) % 4) for i in range(4)]) for n in range(1, 4)
-    ]
+    pieces = list(extra_key_side(scalars, block_mask, kv, qg, every, ax, qg_parts))
+    for n in range(1, 4):
+        pieces[n] = lax.ppermute(pieces[n], "h", [(i, (i + n) % 4) for i in range(4)])
     bm = lax.all_to_all(bm.reshape(16, 2, QTR, E), ("zh", "h"), 0, 0, tiled=True)
     return unpack(pos, out, bm, pieces)
 

time: 222 us -> 215 us (0.968)
  waiting for transfers between devices: 68.1 us -> 83.7 us
  Pallas kernels: 66.1 us -> 54.8 us
  starting transfers between devices: 70.6 us -> 64.5 us
  local copies, waits for them, and re-layouts: 11.3 us -> 5.94 us
    pallas_call x4, Pallas kernels: 57.8 us -> 46.4 us  [side(): pl.pallas_call(kernel, out_shape=out_shape, in_specs=specs + [HBM] * len(...]
    ppermute x3, waiting for transfers between devices: 2.3 us -> 8.8 us  [shards(): lax.ppermute(pieces[n], 'h', [(i, (i + n) % 4) for i in range(4)])]
    ppermute x16, waiting for transfers between devices: 20.9 us -> 26.8 us  [move(): return lax.ppermute(value, 'p', pairs)]
    all_to_all x1, waiting for transfers between devices: 0.01 us -> 3.87 us  [shards(): lax.all_to_all(am.reshape(16, 2, QTR, E), ('zh', 'h'), 0, 0, tiled=True)]
    all_to_all x1, starting transfers between devices: 7.23 us -> 3.47 us  [shards(): lax.all_to_all(bm.reshape(16, 2, QTR, E), ('zh', 'h'), 0, 0, tiled=True)]
    squeeze x2 -> x0, local copies, waits for them, and re-layouts: 3.15 us -> none  [the longest x1 1.58 us: shards(): x[n]]
    slice x1 -> x0, local copies, waits for them, and re-layouts: 2.27 us -> none  [shards(): am[:4].reshape(16, 2, QTR, E)]
  transfers between devices with their start and end apart: 24 -> 24, of which waited for: 9 -> 15; matrix products, arithmetic and copies ran while one was open for 3% -> 2% of each run, Pallas kernels for 28% -> 23%
where the time goes in v4:
time: 215 us; the launch traced here: 214 us
  waiting for transfers between devices  83.7 us (39%)
  starting transfers between devices  64.5 us (30%)
  Pallas kernels  54.8 us (25%)
  local copies, waits for them, and re-layouts  5.94 us (3%)
  other arithmetic  3.69 us (2%)
    pallas_call x4, Pallas kernels, side(): pl.pallas_call(kernel, out_shape=out_shape, in_specs=specs + [HBM] * len(...  46.4 us
    all_to_all x2, waiting for transfers between devices, gather_heads(): wide = lax.all_to_all(packed, ('zh', 'h'), 0, 0, tiled=True)  43.5 us
    ppermute x16, starting transfers between devices, move(): return lax.ppermute(value, 'p', pairs)  31.7 us
    ppermute x16, waiting for transfers between devices, move(): return lax.ppermute(value, 'p', pairs)  26.8 us
    all_to_all x2, starting transfers between devices, gather_heads(): wide = lax.all_to_all(packed, ('zh', 'h'), 0, 0, tiled=True)  13.8 us
    ppermute x3, waiting for transfers between devices, shards(): lax.ppermute(pieces[n], 'h', [(i, (i + n) % 4) for i in range(4)])  8.8 us
    all_to_all x1, starting transfers between devices, shards(): lax.all_to_all(am.reshape(16, 2, QTR, E), ('zh', 'h'), 0, 0, tiled=True)  8.73 us
    pallas_call x2, Pallas kernels, pack(): pl.pallas_call(pack_kernel, out_shape=WIDE, in_specs=[SMEM, SMEM, VMEM, H...  6.04 us
  transfers between devices with their start and end apart: 24, of which 15 were waited for; matrix products, arithmetic and copies ran while one was open for 2% of the time, Pallas kernels for 23%

profile of v4, /device:TPU:1, one launch (start us, length us, event | category | flops | bytes accessed | tf_op | source)
XLA Modules:
  0.0 213.6 jit_solution(18145318232257651206)
XLA Ops:
  0.6 0.6 pad_add_fusion.pos
  1.2 3.0 %pack.3 = bf16[16,2,2,64,128]{4,3,2,1,0:T(8,128)(2,1)} custom-call(s32[3]{0:T(128)} %pad_add_fusion.pos, s32[128]{0:T(128)} %frames.9, f32[8,128]{1,0:T(8,128)} %constant.36.clone.rates, bf16[20,64,128]{2,1,0:T(8,128)(2,1)} %bitcast.40, bf16[20,64,128]{2,1,0:T(8,128)(2,1)} %bitcast.41), custom_call_target="tpu_custom_call" | custom-call | tf_op jit(solution)/shard_map/pack/pallas_call | solution.py:67
  4.2 10.0 %all-to-all-start = ((bf16[16,2,2,64,128]{4,3,2,1,0:T(8,128)(2,1)}), bf16[16,2,2,64,128]{4,3,2,1,0:T(8,128)(2,1)S(1)}, u32[]{:S(2)}, u32[]{:S(2)}) async-start(bf16[16,2,2,64,128]{4,3,2,1,0:T(8,128)(2,1)} %pack.3), calls=%async_computation | async-start | bytes 2097152 | tf_op jit(solution)/shard_map/all_to_all | solution.py:480
  14.2 27.9 %all-to-all-done = bf16[16,2,2,64,128]{4,3,2,1,0:T(8,128)(2,1)S(1)} async-done(((bf16[16,2,2,64,128]{4,3,2,1,0:T(8,128)(2,1)}), bf16[16,2,2,64,128]{4,3,2,1,0:T(8,128)(2,1)S(1)}, u32[]{:S(2)}, u32[]{:S(2)}) %all-to-all-start) | async-done | bytes 1048608 | tf_op jit(solution)/shard_map/all_to_all | solution.py:480
  42.3 0.9 copy-done
  43.4 2.8 %collective-permute-start.2 = (bf16[6,4,2,64,128]{4,3,2,1,0:T(8,128)(2,1)S(1)}, bf16[6,4,2,64,128]{4,3,2,1,0:T(8,128)(2,1)}, u32[]{:S(2)}, u32[]{:S(2)}) collective-permute-start(bf16[6,4,2,64,128]{4,3,2,1,0:T(8,128)(2,1)S(1)} %pad_maximum_fusion), channel_id=1, source_target_pairs={{0,8},{4,12},{8,0},{12,4},{16,24},{20,28},{24,16},{28,20},{32,40},... | collective-permute-start | bytes 2359304 | tf_op jit(solution)/shard_map/ppermute | solution.py:454
  46.2 2.7 %collective-permute-start.1 = (bf16[6,4,2,64,128]{4,3,2,1,0:T(8,128)(2,1)S(1)}, bf16[6,4,2,64,128]{4,3,2,1,0:T(8,128)(2,1)S(1)}, u32[]{:S(2)}, u32[]{:S(2)}) collective-permute-start(bf16[6,4,2,64,128]{4,3,2,1,0:T(8,128)(2,1)S(1)} %pad_maximum_fusion), channel_id=1, source_target_pairs={{0,48},{4,52},{8,56},{12,60},{16,0},{20,4},{24,8},{28,12},{32,16},... | collective-permute-start | bytes 2359304 | tf_op jit(solution)/shard_map/ppermute | solution.py:454
  49.0 3.0 %pack.2 = bf16[16,2,2,64,128]{4,3,2,1,0:T(8,128)(2,1)} custom-call(s32[3]{0:T(128)} %pad_add_fusion.pos, s32[128]{0:T(128)} %frames.9, f32[8,128]{1,0:T(8,128)} %constant.36.clone.rates, bf16[20,64,128]{2,1,0:T(8,128)(2,1)} %bitcast.42, bf16[20,64,128]{2,1,0:T(8,128)(2,1)} %bitcast.43), custom_call_target="tpu_custom_call" | custom-call | tf_op jit(solution)/shard_map/pack/pallas_call | solution.py:67
  52.0 11.7 %collective-permute-done.2.refs_3_ = bf16[6,4,2,64,128]{4,3,2,1,0:T(8,128)(2,1)} collective-permute-done((bf16[6,4,2,64,128]{4,3,2,1,0:T(8,128)(2,1)S(1)}, bf16[6,4,2,64,128]{4,3,2,1,0:T(8,128)(2,1)}, u32[]{:S(2)}, u32[]{:S(2)}) %collective-permute-start.2) | collective-permute-done | bytes 786464 | tf_op jit(solution)/shard_map/ppermute | solution.py:454
  63.6 2.2 %collective-permute-done.1.refs_1_ = bf16[6,4,2,64,128]{4,3,2,1,0:T(8,128)(2,1)S(1)} collective-permute-done((bf16[6,4,2,64,128]{4,3,2,1,0:T(8,128)(2,1)S(1)}, bf16[6,4,2,64,128]{4,3,2,1,0:T(8,128)(2,1)S(1)}, u32[]{:S(2)}, u32[]{:S(2)}) %collective-permute-start.1) | collective-permute-done | bytes 786464 | tf_op jit(solution)/shard_map/ppermute | solution.py:454
  65.9 3.5 %collective-permute-done.refs_0_ = bf16[6,4,2,64,128]{4,3,2,1,0:T(8,128)(2,1)S(1)} collective-permute-done((bf16[6,4,2,64,128]{4,3,2,1,0:T(8,128)(2,1)S(1)}, bf16[6,4,2,64,128]{4,3,2,1,0:T(8,128)(2,1)S(1)}, u32[]{:S(2)}, u32[]{:S(2)}) %collective-permute-start) | collective-permute-done | bytes 786464 | tf_op jit(solution)/shard_map/ppermute | solution.py:454
  69.4 3.8 %all-to-all-start.1 = ((bf16[16,2,2,64,128]{4,3,2,1,0:T(8,128)(2,1)}), bf16[16,2,2,64,128]{4,3,2,1,0:T(8,128)(2,1)S(1)}, u32[]{:S(2)}, u32[]{:S(2)}) async-start(bf16[16,2,2,64,128]{4,3,2,1,0:T(8,128)(2,1)} %pack.2), calls=%async_computation.1 | async-start | bytes 2097152 | tf_op jit(solution)/shard_map/all_to_all | solution.py:480
  73.3 1.0 broadcast_select_fusion.1
  74.3 2.8 %collective-permute-start.5 = (bf16[6,4,2,64,128]{4,3,2,1,0:T(8,128)(2,1)}, bf16[6,4,2,64,128]{4,3,2,1,0:T(8,128)(2,1)S(1)}, u32[]{:S(2)}, u32[]{:S(2)}) collective-permute-start(bf16[6,4,2,64,128]{4,3,2,1,0:T(8,128)(2,1)} %broadcast_select_fusion.1), channel_id=1, source_target_pairs={{0,12},{12,0},{16,28},{28,16},{32,44},{44,32},{48,60},{60,48},{1,1... | collective-permute-start | bytes 2359304 | tf_op jit(solution)/shard_map/ppermute | solution.py:454
  77.1 1.4 collective-permute-start.4
  78.6 0.9 pad_maximum_fusion.2
  79.5 1.3 collective-permute-start.7
  80.8 4.9 %collective-permute-start.6 = (bf16[5,4,2,64,128]{4,3,2,1,0:T(8,128)(2,1)}, bf16[5,4,2,64,128]{4,3,2,1,0:T(8,128)(2,1)}, u32[]{:S(2)}, u32[]{:S(2)}) collective-permute-start(bf16[5,4,2,64,128]{4,3,2,1,0:T(8,128)(2,1)} %pad_maximum_fusion.2), channel_id=1, source_target_pairs={{0,4},{4,8},{8,12},{16,20},{20,24},{24,28},{32,36},{36,40},{40,44}... | collective-permute-start | bytes 1966088 | tf_op jit(solution)/shard_map/ppermute | solution.py:454
  85.6 15.6 %all-to-all-done.1 = bf16[16,2,2,64,128]{4,3,2,1,0:T(8,128)(2,1)S(1)} async-done(((bf16[16,2,2,64,128]{4,3,2,1,0:T(8,128)(2,1)}), bf16[16,2,2,64,128]{4,3,2,1,0:T(8,128)(2,1)S(1)}, u32[]{:S(2)}, u32[]{:S(2)}) %all-to-all-start.1) | async-done | bytes 1048608 | tf_op jit(solution)/shard_map/all_to_all | solution.py:480
  101.4 0.9 copy-done.1
  102.5 2.7 %collective-permute-start.8 = (bf16[6,4,2,64,128]{4,3,2,1,0:T(8,128)(2,1)S(1)}, bf16[6,4,2,64,128]{4,3,2,1,0:T(8,128)(2,1)S(1)}, u32[]{:S(2)}, u32[]{:S(2)}) collective-permute-start(bf16[6,4,2,64,128]{4,3,2,1,0:T(8,128)(2,1)S(1)} %pad_maximum_fusion.1), channel_id=1, source_target_pairs={{0,48},{4,52},{8,56},{12,60},{16,0},{20,4},{24,8},{28,12},{32,16},... | collective-permute-start | bytes 2359304 | tf_op jit(solution)/shard_map/ppermute | solution.py:454
  105.4 0.9 slice.21
  106.3 13.9 %forward_kernel.1 = (bf16[5,4,1,64,128]{4,3,2,1,0:T(8,128)(2,1)}, f32[24,128]{1,0:T(8,128)}) custom-call(s32[3]{0:T(128)} %pad_add_fusion.pos, bf16[6,4,2,64,128]{4,3,2,1,0:T(8,128)(2,1)} %copy-done.3, bf16[6,4,2,64,128]{4,3,2,1,0:T(8,128)(2,1)} %copy-done.2, bf16[6,4,2,64,128]{4,3,2,1,0:T(8,128)(2,1)} %collective-permute-done.3.refs_2_, ...), custom_call_target="tpu_custom_call" | custom-call | flops 2181038080 | bytes 8388608 | tf_op jit(solution)/shard_map/forward_kernel/pallas_call | solution.py:396
  120.2 2.5 %collective-permute-done.9.refs_0_ = bf16[6,4,2,64,128]{4,3,2,1,0:T(8,128)(2,1)S(1)} collective-permute-done((bf16[6,4,2,64,128]{4,3,2,1,0:T(8,128)(2,1)S(1)}, bf16[6,4,2,64,128]{4,3,2,1,0:T(8,128)(2,1)S(1)}, u32[]{:S(2)}, u32[]{:S(2)}) %collective-permute-start.9) | collective-permute-done | bytes 786464 | tf_op jit(solution)/shard_map/ppermute | solution.py:454
  122.7 1.1 broadcast_select_fusion
  124.1 2.0 collective-permute-done.10.refs_3_
  126.1 0.9 broadcast_in_dim.2
  127.0 4.6 %all-to-all-start.2 = ((f32[64,24,128]{2,1,0:T(8,128)}), f32[64,24,128]{2,1,0:T(8,128)S(1)}, u32[]{:S(2)}, u32[]{:S(2)}) async-start(f32[64,24,128]{2,1,0:T(8,128)} %broadcast_in_dim.2), calls=%async_computation.2 | async-start | bytes 1572864 | tf_op jit(solution)/shard_map/all_to_all | solution.py:506
  131.7 4.0 %collective-permute-start.13 = (bf16[6,4,2,64,128]{4,3,2,1,0:T(8,128)(2,1)}, bf16[6,4,2,64,128]{4,3,2,1,0:T(8,128)(2,1)S(1)}, u32[]{:S(2)}, u32[]{:S(2)}) collective-permute-start(bf16[6,4,2,64,128]{4,3,2,1,0:T(8,128)(2,1)} %broadcast_select_fusion), channel_id=1, source_target_pairs={{0,12},{12,0},{16,28},{28,16},{32,44},{44,32},{48,60},{60,48},{1,1... | collective-permute-start | bytes 2359304 | tf_op jit(solution)/shard_map/ppermute | solution.py:454
  135.7 2.6 %collective-permute-start.11 = (bf16[6,4,2,64,128]{4,3,2,1,0:T(8,128)(2,1)}, bf16[6,4,2,64,128]{4,3,2,1,0:T(8,128)(2,1)S(1)}, u32[]{:S(2)}, u32[]{:S(2)}) collective-permute-start(bf16[6,4,2,64,128]{4,3,2,1,0:T(8,128)(2,1)} %broadcast_select_fusion), channel_id=1, source_target_pairs={{0,48},{4,52},{8,24},{12,28},{16,0},{20,4},{24,40},{28,44},{32,16}... | collective-permute-start | bytes 2359304 | tf_op jit(solution)/shard_map/ppermute | solution.py:454
  138.3 1.3 collective-permute-start.15
  139.5 4.9 %collective-permute-start.14 = (bf16[5,4,2,64,128]{4,3,2,1,0:T(8,128)(2,1)}, bf16[5,4,2,64,128]{4,3,2,1,0:T(8,128)(2,1)}, u32[]{:S(2)}, u32[]{:S(2)}) collective-permute-start(bf16[5,4,2,64,128]{4,3,2,1,0:T(8,128)(2,1)} %slice.21), channel_id=1, source_target_pairs={{0,4},{4,8},{8,12},{16,20},{20,24},{24,28},{32,36},{36,40},{40,44}... | collective-permute-start | bytes 1966088 | tf_op jit(solution)/shard_map/ppermute | solution.py:454
  144.4 13.6 %query_kernel.1 = (bf16[4,4,2,64,128]{4,3,2,1,0:T(8,128)(2,1)}, bf16[1,4,2,64,128]{4,3,2,1,0:T(8,128)(2,1)}) custom-call(s32[3]{0:T(128)} %pad_add_fusion.pos, s32[128]{0:T(128)} %frames.9, f32[8,128]{1,0:T(8,128)} %constant.36.clone.rates, bf16[6,4,2,64,128]{4,3,2,1,0:T(8,128)(2,1)} %copy-done.3, bf16[6,4,2,64,128]{4,3,2,1,0:T(8,128)(2,1)} %copy-done.2, ...), custom_call_target="tpu_custom_call" | custom-call | flops 3271557120 | bytes 8388608 | tf_op jit(solution)/shard_map/query_kernel/pallas_call | solution.py:396
  158.0 2.9 %collective-permute-done.15.refs_7_ = bf16[5,4,2,64,128]{4,3,2,1,0:T(8,128)(2,1)S(1)} collective-permute-done((bf16[5,4,2,64,128]{4,3,2,1,0:T(8,128)(2,1)}, bf16[5,4,2,64,128]{4,3,2,1,0:T(8,128)(2,1)S(1)}, u32[]{:S(2)}, u32[]{:S(2)}) %collective-permute-start.15) | collective-permute-done | bytes 655392 | tf_op jit(solution)/shard_map/ppermute | solution.py:454
  161.1 1.8 collective-permute-done.12.refs_4_
  162.9 8.7 %all-to-all-start.3 = ((bf16[16,2,64,128]{3,2,1,0:T(8,128)(2,1)}), bf16[16,2,64,128]{3,2,1,0:T(8,128)(2,1)S(1)}, u32[]{:S(2)}, u32[]{:S(2)}) async-start(bf16[16,2,64,128]{3,2,1,0:T(8,128)(2,1)} %bitcast.39), calls=%async_computation.3 | async-start | bytes 1048576 | tf_op jit(solution)/shard_map/all_to_all | solution.py:513
  171.7 13.4 %key_kernel.1 = bf16[4,4,2,64,128]{4,3,2,1,0:T(8,128)(2,1)} custom-call(s32[3]{0:T(128)} %pad_add_fusion.pos, s32[128]{0:T(128)} %frames.9, f32[8,128]{1,0:T(8,128)} %constant.36.clone.rates, bf16[6,4,2,64,128]{4,3,2,1,0:T(8,128)(2,1)} %copy-done.4, bf16[6,4,2,64,128]{4,3,2,1,0:T(8,128)(2,1)} %copy-done.5, bf16[6,4,2,64,128]{4,3,2,1,0:T(8,128)(2,1)} %copy-done.11, ...), custom_call_target="tpu_custom_call" | custom-call | flops 3489660928 | bytes 8388608 | tf_op jit(solution)/shard_map/key_kernel/pallas_call | solution.py:396
  185.1 3.9 %all-to-all-done.3.a_ref = bf16[16,2,64,128]{3,2,1,0:T(8,128)(2,1)S(1)} async-done(((bf16[16,2,64,128]{3,2,1,0:T(8,128)(2,1)}), bf16[16,2,64,128]{3,2,1,0:T(8,128)(2,1)S(1)}, u32[]{:S(2)}, u32[]{:S(2)}) %all-to-all-start.3) | async-done | bytes 524320 | tf_op jit(solution)/shard_map/all_to_all | solution.py:513
  188.9 0.8 copy-done.7
  189.8 3.5 %all-to-all-start.4 = ((bf16[16,2,64,128]{3,2,1,0:T(8,128)(2,1)}), bf16[16,2,64,128]{3,2,1,0:T(8,128)(2,1)S(1)}, u32[]{:S(2)}, u32[]{:S(2)}) async-start(bf16[16,2,64,128]{3,2,1,0:T(8,128)(2,1)} %bitcast.38), calls=%async_computation.4 | async-start | bytes 1048576 | tf_op jit(solution)/shard_map/all_to_all | solution.py:518
  193.3 5.6 %extra_key_kernel.1 = (bf16[4,64,128]{2,1,0:T(8,128)(2,1)}, bf16[4,64,128]{2,1,0:T(8,128)(2,1)}, bf16[4,64,128]{2,1,0:T(8,128)(2,1)}, bf16[4,64,128]{2,1,0:T(8,128)(2,1)}) custom-call(s32[3]{0:T(128)} %pad_add_fusion.pos, s32[128]{0:T(128)} %frames.9, f32[8,128]{1,0:T(8,128)} %constant.36.clone.rates, bf16[6,4,2,64,128]{4,3,2,1,0:T(8,128)(2,1)} %copy-done.4, ...), custom_call_target="tpu_custom_call" | custom-call | flops 872415232 | bytes 8388608 | tf_op jit(solution)/shard_map/extra_key_kernel/pallas_call | solution.py:396
  198.8 1.6 collective-permute-start.16
  200.4 0.5 collective-permute-start.18
  201.0 4.3 %collective-permute-done.16.refs_1_ = bf16[4,64,128]{2,1,0:T(8,128)(2,1)S(1)} collective-permute-done((bf16[4,64,128]{2,1,0:T(8,128)(2,1)}, bf16[4,64,128]{2,1,0:T(8,128)(2,1)S(1)}, u32[]{:S(2)}, u32[]{:S(2)}) %collective-permute-start.16) | collective-permute-done | bytes 65568 | tf_op jit(solution)/shard_map/ppermute | solution.py:517
  205.3 4.0 %collective-permute-done.17.refs_2_ = bf16[4,64,128]{2,1,0:T(8,128)(2,1)S(1)} collective-permute-done((bf16[4,64,128]{2,1,0:T(8,128)(2,1)}, bf16[4,64,128]{2,1,0:T(8,128)(2,1)S(1)}, u32[]{:S(2)}, u32[]{:S(2)}) %collective-permute-start.17) | collective-permute-done | bytes 65568 | tf_op jit(solution)/shard_map/ppermute | solution.py:517
  209.8 0.7 all-to-all-done.4.b_ref
  210.5 0.8 copy-done.8
  211.3 2.3 %unpack.1 = (bf16[20,64,128]{2,1,0:T(8,128)(2,1)}, bf16[20,64,128]{2,1,0:T(8,128)(2,1)}, bf16[20,64,128]{2,1,0:T(8,128)(2,1)}, bf16[20,64,128]{2,1,0:T(8,128)(2,1)}) custom-call(s32[3]{0:T(128)} %pad_add_fusion.pos, bf16[16,2,64,128]{3,2,1,0:T(8,128)(2,1)} %copy-done.7, bf16[16,2,64,128]{3,2,1,0:T(8,128)(2,1)} %copy-done.8, ...), custom_call_target="tpu_custom_call" | custom-call | tf_op jit(solution)/shard_map/unpack/pallas_call | solution.py:92
  (54 shorter events, 2.0 us)
Async XLA Ops:
  4.2 37.9 %all-to-all-start = ((bf16[16,2,2,64,128]{4,3,2,1,0:T(8,128)(2,1)}), bf16[16,2,2,64,128]{4,3,2,1,0:T(8,128)(2,1)S(1)}, u32[]{:S(2)}, u32[]{:S(2)}) async-start(bf16[16,2,2,64,128]{4,3,2,1,0:T(8,128)(2,1)} %pack.3), calls=%async_computation | async-start | bytes 2097152 | tf_op jit(solution)/shard_map/all_to_all | solution.py:480
  42.2 1.0 copy-start
  43.4 20.2 %collective-permute-start.2 = (bf16[6,4,2,64,128]{4,3,2,1,0:T(8,128)(2,1)S(1)}, bf16[6,4,2,64,128]{4,3,2,1,0:T(8,128)(2,1)}, u32[]{:S(2)}, u32[]{:S(2)}) collective-permute-start(bf16[6,4,2,64,128]{4,3,2,1,0:T(8,128)(2,1)S(1)} %pad_maximum_fusion), channel_id=1, source_target_pairs={{0,8},{4,12},{8,0},{12,4},{16,24},{20,28},{24,16},{28,20},{32,40},... | collective-permute-start | bytes 2359304 | tf_op jit(solution)/shard_map/ppermute | solution.py:454
  46.2 19.7 %collective-permute-start.1 = (bf16[6,4,2,64,128]{4,3,2,1,0:T(8,128)(2,1)S(1)}, bf16[6,4,2,64,128]{4,3,2,1,0:T(8,128)(2,1)S(1)}, u32[]{:S(2)}, u32[]{:S(2)}) collective-permute-start(bf16[6,4,2,64,128]{4,3,2,1,0:T(8,128)(2,1)S(1)} %pad_maximum_fusion), channel_id=1, source_target_pairs={{0,48},{4,52},{8,56},{12,60},{16,0},{20,4},{24,8},{28,12},{32,16},... | collective-permute-start | bytes 2359304 | tf_op jit(solution)/shard_map/ppermute | solution.py:454
  49.0 20.5 %collective-permute-start = (bf16[6,4,2,64,128]{4,3,2,1,0:T(8,128)(2,1)S(1)}, bf16[6,4,2,64,128]{4,3,2,1,0:T(8,128)(2,1)S(1)}, u32[]{:S(2)}, u32[]{:S(2)}) collective-permute-start(bf16[6,4,2,64,128]{4,3,2,1,0:T(8,128)(2,1)S(1)} %pad_maximum_fusion), channel_id=1, source_target_pairs={{0,16},{4,20},{8,24},{12,28},{16,32},{20,36},{24,40},{28,44},{32,4... | collective-permute-start | bytes 2359304 | tf_op jit(solution)/shard_map/ppermute | solution.py:454
  65.9 7.4 %copy-start.2 = (bf16[6,4,2,64,128]{4,3,2,1,0:T(8,128)(2,1)}, bf16[6,4,2,64,128]{4,3,2,1,0:T(8,128)(2,1)S(1)}, u32[]{:S(2)}) copy-start(bf16[6,4,2,64,128]{4,3,2,1,0:T(8,128)(2,1)S(1)} %collective-permute-done.1.refs_1_) | copy-start | bytes 2359300
  69.4 3.8 %copy-start.3 = (bf16[6,4,2,64,128]{4,3,2,1,0:T(8,128)(2,1)}, bf16[6,4,2,64,128]{4,3,2,1,0:T(8,128)(2,1)S(1)}, u32[]{:S(2)}) copy-start(bf16[6,4,2,64,128]{4,3,2,1,0:T(8,128)(2,1)S(1)} %collective-permute-done.refs_0_) | copy-start | bytes 2359300
  69.4 31.8 %all-to-all-start.1 = ((bf16[16,2,2,64,128]{4,3,2,1,0:T(8,128)(2,1)}), bf16[16,2,2,64,128]{4,3,2,1,0:T(8,128)(2,1)S(1)}, u32[]{:S(2)}, u32[]{:S(2)}) async-start(bf16[16,2,2,64,128]{4,3,2,1,0:T(8,128)(2,1)} %pack.2), calls=%async_computation.1 | async-start | bytes 2097152 | tf_op jit(solution)/shard_map/all_to_all | solution.py:480
  74.3 28.1 %collective-permute-start.5 = (bf16[6,4,2,64,128]{4,3,2,1,0:T(8,128)(2,1)}, bf16[6,4,2,64,128]{4,3,2,1,0:T(8,128)(2,1)S(1)}, u32[]{:S(2)}, u32[]{:S(2)}) collective-permute-start(bf16[6,4,2,64,128]{4,3,2,1,0:T(8,128)(2,1)} %broadcast_select_fusion.1), channel_id=1, source_target_pairs={{0,12},{12,0},{16,28},{28,16},{32,44},{44,32},{48,60},{60,48},{1,1... | collective-permute-start | bytes 2359304 | tf_op jit(solution)/shard_map/ppermute | solution.py:454
  77.0 25.4 %collective-permute-start.3 = (bf16[6,4,2,64,128]{4,3,2,1,0:T(8,128)(2,1)}, bf16[6,4,2,64,128]{4,3,2,1,0:T(8,128)(2,1)}, u32[]{:S(2)}, u32[]{:S(2)}) collective-permute-start(bf16[6,4,2,64,128]{4,3,2,1,0:T(8,128)(2,1)} %broadcast_select_fusion.1), channel_id=1, source_target_pairs={{0,48},{4,52},{8,24},{12,28},{16,0},{20,4},{24,40},{28,44},{32,16}... | collective-permute-start | bytes 2359304 | tf_op jit(solution)/shard_map/ppermute | solution.py:454
  77.1 25.3 %collective-permute-start.4 = (bf16[6,4,2,64,128]{4,3,2,1,0:T(8,128)(2,1)}, bf16[6,4,2,64,128]{4,3,2,1,0:T(8,128)(2,1)}, u32[]{:S(2)}, u32[]{:S(2)}) collective-permute-start(bf16[6,4,2,64,128]{4,3,2,1,0:T(8,128)(2,1)} %collective-permute-done.2.refs_3_), channel_id=1, source_target_pairs={{0,16},{4,20},{8,56},{12,60},{16,32},{20,36},{24,8},{28,12},{32,48... | collective-permute-start | bytes 2359304 | tf_op jit(solution)/shard_map/ppermute | solution.py:454
  79.5 26.8 %collective-permute-start.7 = (bf16[5,4,2,64,128]{4,3,2,1,0:T(8,128)(2,1)}, bf16[5,4,2,64,128]{4,3,2,1,0:T(8,128)(2,1)}, u32[]{:S(2)}, u32[]{:S(2)}) collective-permute-start(bf16[5,4,2,64,128]{4,3,2,1,0:T(8,128)(2,1)} %pad_maximum_fusion.2), channel_id=1, source_target_pairs={{4,0},{8,4},{12,8},{20,16},{24,20},{28,24},{36,32},{40,36},{44,40}... | collective-permute-start | bytes 1966088 | tf_op jit(solution)/shard_map/ppermute | solution.py:454
  80.8 25.5 %collective-permute-start.6 = (bf16[5,4,2,64,128]{4,3,2,1,0:T(8,128)(2,1)}, bf16[5,4,2,64,128]{4,3,2,1,0:T(8,128)(2,1)}, u32[]{:S(2)}, u32[]{:S(2)}) collective-permute-start(bf16[5,4,2,64,128]{4,3,2,1,0:T(8,128)(2,1)} %pad_maximum_fusion.2), channel_id=1, source_target_pairs={{0,4},{4,8},{8,12},{16,20},{20,24},{24,28},{32,36},{36,40},{40,44}... | collective-permute-start | bytes 1966088 | tf_op jit(solution)/shard_map/ppermute | solution.py:454
  101.2 1.0 copy-start.1
  102.4 3.9 %copy-start.9 = (bf16[6,4,2,64,128]{4,3,2,1,0:T(8,128)(2,1)}, bf16[6,4,2,64,128]{4,3,2,1,0:T(8,128)(2,1)S(1)}, u32[]{:S(2)}) copy-start(bf16[6,4,2,64,128]{4,3,2,1,0:T(8,128)(2,1)S(1)} %collective-permute-done.5.refs_5_) | copy-start | bytes 2359300
  102.4 20.3 %collective-permute-start.9 = (bf16[6,4,2,64,128]{4,3,2,1,0:T(8,128)(2,1)S(1)}, bf16[6,4,2,64,128]{4,3,2,1,0:T(8,128)(2,1)S(1)}, u32[]{:S(2)}, u32[]{:S(2)}) collective-permute-start(bf16[6,4,2,64,128]{4,3,2,1,0:T(8,128)(2,1)S(1)} %pad_maximum_fusion.1), channel_id=1, source_target_pairs={{0,16},{4,20},{8,24},{12,28},{16,32},{20,36},{24,40},{28,44},{32,4... | collective-permute-start | bytes 2359304 | tf_op jit(solution)/shard_map/ppermute | solution.py:454
  102.5 20.2 %collective-permute-start.8 = (bf16[6,4,2,64,128]{4,3,2,1,0:T(8,128)(2,1)S(1)}, bf16[6,4,2,64,128]{4,3,2,1,0:T(8,128)(2,1)S(1)}, u32[]{:S(2)}, u32[]{:S(2)}) collective-permute-start(bf16[6,4,2,64,128]{4,3,2,1,0:T(8,128)(2,1)S(1)} %pad_maximum_fusion.1), channel_id=1, source_target_pairs={{0,48},{4,52},{8,56},{12,60},{16,0},{20,4},{24,8},{28,12},{32,16},... | collective-permute-start | bytes 2359304 | tf_op jit(solution)/shard_map/ppermute | solution.py:454
  105.2 20.9 %collective-permute-start.10 = (bf16[6,4,2,64,128]{4,3,2,1,0:T(8,128)(2,1)S(1)}, bf16[6,4,2,64,128]{4,3,2,1,0:T(8,128)(2,1)}, u32[]{:S(2)}, u32[]{:S(2)}) collective-permute-start(bf16[6,4,2,64,128]{4,3,2,1,0:T(8,128)(2,1)S(1)} %pad_maximum_fusion.1), channel_id=1, source_target_pairs={{0,8},{4,12},{8,0},{12,4},{16,24},{20,28},{24,16},{28,20},{32,40},... | collective-permute-start | bytes 2359304 | tf_op jit(solution)/shard_map/ppermute | solution.py:454
  122.7 1.1 copy-start.4
  122.7 1.4 copy-start.5
  122.7 3.4 %copy-start.16 = (f32[24,128]{1,0:T(8,128)S(1)}, f32[24,128]{1,0:T(8,128)}, u32[]{:S(2)}) copy-start(f32[24,128]{1,0:T(8,128)} %get-tuple-element.55.refs_12_) | copy-start | bytes 36868
  127.0 35.9 %all-to-all-start.2 = ((f32[64,24,128]{2,1,0:T(8,128)}), f32[64,24,128]{2,1,0:T(8,128)S(1)}, u32[]{:S(2)}, u32[]{:S(2)}) async-start(f32[64,24,128]{2,1,0:T(8,128)} %broadcast_in_dim.2), calls=%async_computation.2 | async-start | bytes 1572864 | tf_op jit(solution)/shard_map/all_to_all | solution.py:506
  131.7 29.4 %collective-permute-start.13 = (bf16[6,4,2,64,128]{4,3,2,1,0:T(8,128)(2,1)}, bf16[6,4,2,64,128]{4,3,2,1,0:T(8,128)(2,1)S(1)}, u32[]{:S(2)}, u32[]{:S(2)}) collective-permute-start(bf16[6,4,2,64,128]{4,3,2,1,0:T(8,128)(2,1)} %broadcast_select_fusion), channel_id=1, source_target_pairs={{0,12},{12,0},{16,28},{28,16},{32,44},{44,32},{48,60},{60,48},{1,1... | collective-permute-start | bytes 2359304 | tf_op jit(solution)/shard_map/ppermute | solution.py:454
  135.7 25.4 %collective-permute-start.11 = (bf16[6,4,2,64,128]{4,3,2,1,0:T(8,128)(2,1)}, bf16[6,4,2,64,128]{4,3,2,1,0:T(8,128)(2,1)S(1)}, u32[]{:S(2)}, u32[]{:S(2)}) collective-permute-start(bf16[6,4,2,64,128]{4,3,2,1,0:T(8,128)(2,1)} %broadcast_select_fusion), channel_id=1, source_target_pairs={{0,48},{4,52},{8,24},{12,28},{16,0},{20,4},{24,40},{28,44},{32,16}... | collective-permute-start | bytes 2359304 | tf_op jit(solution)/shard_map/ppermute | solution.py:454
  138.3 24.6 %collective-permute-start.12 = (bf16[6,4,2,64,128]{4,3,2,1,0:T(8,128)(2,1)}, bf16[6,4,2,64,128]{4,3,2,1,0:T(8,128)(2,1)}, u32[]{:S(2)}, u32[]{:S(2)}) collective-permute-start(bf16[6,4,2,64,128]{4,3,2,1,0:T(8,128)(2,1)} %collective-permute-done.10.refs_3_), channel_id=1, source_target_pairs={{0,16},{4,20},{8,56},{12,60},{16,32},{20,36},{24,8},{28,12},{32,48... | collective-permute-start | bytes 2359304 | tf_op jit(solution)/shard_map/ppermute | solution.py:454
  138.3 22.7 %collective-permute-start.15 = (bf16[5,4,2,64,128]{4,3,2,1,0:T(8,128)(2,1)}, bf16[5,4,2,64,128]{4,3,2,1,0:T(8,128)(2,1)S(1)}, u32[]{:S(2)}, u32[]{:S(2)}) collective-permute-start(bf16[5,4,2,64,128]{4,3,2,1,0:T(8,128)(2,1)} %slice.21), channel_id=1, source_target_pairs={{4,0},{8,4},{12,8},{20,16},{24,20},{28,24},{36,32},{40,36},{44,40}... | collective-permute-start | bytes 1966088 | tf_op jit(solution)/shard_map/ppermute | solution.py:454
  139.5 21.5 %collective-permute-start.14 = (bf16[5,4,2,64,128]{4,3,2,1,0:T(8,128)(2,1)}, bf16[5,4,2,64,128]{4,3,2,1,0:T(8,128)(2,1)}, u32[]{:S(2)}, u32[]{:S(2)}) collective-permute-start(bf16[5,4,2,64,128]{4,3,2,1,0:T(8,128)(2,1)} %slice.21), channel_id=1, source_target_pairs={{0,4},{4,8},{8,12},{16,20},{20,24},{24,28},{32,36},{36,40},{40,44}... | collective-permute-start | bytes 1966088 | tf_op jit(solution)/shard_map/ppermute | solution.py:454
  160.9 10.7 %copy-start.12 = (bf16[5,4,2,64,128]{4,3,2,1,0:T(8,128)(2,1)}, bf16[5,4,2,64,128]{4,3,2,1,0:T(8,128)(2,1)S(1)}, u32[]{:S(2)}) copy-start(bf16[5,4,2,64,128]{4,3,2,1,0:T(8,128)(2,1)S(1)} %collective-permute-done.15.refs_7_) | copy-start | bytes 1966084
  161.1 10.6 %copy-start.10 = (bf16[6,4,2,64,128]{4,3,2,1,0:T(8,128)(2,1)}, bf16[6,4,2,64,128]{4,3,2,1,0:T(8,128)(2,1)S(1)}, u32[]{:S(2)}) copy-start(bf16[6,4,2,64,128]{4,3,2,1,0:T(8,128)(2,1)S(1)} %collective-permute-done.13.refs_5_) | copy-start | bytes 2359300
  161.1 10.6 %copy-start.11 = (bf16[6,4,2,64,128]{4,3,2,1,0:T(8,128)(2,1)}, bf16[6,4,2,64,128]{4,3,2,1,0:T(8,128)(2,1)S(1)}, u32[]{:S(2)}) copy-start(bf16[6,4,2,64,128]{4,3,2,1,0:T(8,128)(2,1)S(1)} %collective-permute-done.11.refs_2_) | copy-start | bytes 2359300
  162.9 8.8 %copy-start.6 = (f32[64,24,128]{2,1,0:T(8,128)}, f32[64,24,128]{2,1,0:T(8,128)S(1)}, u32[]{:S(2)}) copy-start(f32[64,24,128]{2,1,0:T(8,128)S(1)} %all-to-all-done.2.refs_11_) | copy-start | bytes 2359300
  162.9 26.1 %all-to-all-start.3 = ((bf16[16,2,64,128]{3,2,1,0:T(8,128)(2,1)}), bf16[16,2,64,128]{3,2,1,0:T(8,128)(2,1)S(1)}, u32[]{:S(2)}, u32[]{:S(2)}) async-start(bf16[16,2,64,128]{3,2,1,0:T(8,128)(2,1)} %bitcast.39), calls=%async_computation.3 | async-start | bytes 1048576 | tf_op jit(solution)/shard_map/all_to_all | solution.py:513
  188.9 0.8 copy-start.7
  189.8 20.7 %all-to-all-start.4 = ((bf16[16,2,64,128]{3,2,1,0:T(8,128)(2,1)}), bf16[16,2,64,128]{3,2,1,0:T(8,128)(2,1)S(1)}, u32[]{:S(2)}, u32[]{:S(2)}) async-start(bf16[16,2,64,128]{3,2,1,0:T(8,128)(2,1)} %bitcast.38), calls=%async_computation.4 | async-start | bytes 1048576 | tf_op jit(solution)/shard_map/all_to_all | solution.py:518
  198.8 6.5 %collective-permute-start.16 = (bf16[4,64,128]{2,1,0:T(8,128)(2,1)}, bf16[4,64,128]{2,1,0:T(8,128)(2,1)S(1)}, u32[]{:S(2)}, u32[]{:S(2)}) collective-permute-start(bf16[4,64,128]{2,1,0:T(8,128)(2,1)} %get-tuple-element.75), channel_id=1, source_target_pairs={{0,1},{1,2},{2,3},{3,0},{4,5},{5,6},{6,7},{7,4},{8,9},{9,10},{10,1... | collective-permute-start | bytes 196616 | tf_op jit(solution)/shard_map/ppermute | solution.py:517
  200.4 8.9 %collective-permute-start.17 = (bf16[4,64,128]{2,1,0:T(8,128)(2,1)}, bf16[4,64,128]{2,1,0:T(8,128)(2,1)S(1)}, u32[]{:S(2)}, u32[]{:S(2)}) collective-permute-start(bf16[4,64,128]{2,1,0:T(8,128)(2,1)} %get-tuple-element.76), channel_id=1, source_target_pairs={{0,2},{1,3},{2,0},{3,1},{4,6},{5,7},{6,4},{7,5},{8,10},{9,11},{10,... | collective-permute-start | bytes 196616 | tf_op jit(solution)/shard_map/ppermute | solution.py:517
  200.4 9.3 %collective-permute-start.18 = (bf16[4,64,128]{2,1,0:T(8,128)(2,1)}, bf16[4,64,128]{2,1,0:T(8,128)(2,1)S(1)}, u32[]{:S(2)}, u32[]{:S(2)}) collective-permute-start(bf16[4,64,128]{2,1,0:T(8,128)(2,1)} %get-tuple-element.77), channel_id=1, source_target_pairs={{0,3},{1,0},{2,1},{3,2},{4,7},{5,4},{6,5},{7,6},{8,11},{9,8},{10,9... | collective-permute-start | bytes 196616 | tf_op jit(solution)/shard_map/ppermute | solution.py:517
  205.3 5.2 %copy-start.13 = (bf16[4,64,128]{2,1,0:T(8,128)(2,1)}, bf16[4,64,128]{2,1,0:T(8,128)(2,1)S(1)}, u32[]{:S(2)}) copy-start(bf16[4,64,128]{2,1,0:T(8,128)(2,1)S(1)} %collective-permute-done.16.refs_1_) | copy-start | bytes 196612
  209.3 1.2 copy-start.14
  209.8 0.7 copy-start.15
  210.5 0.8 copy-start.8

commit v5 on v4

--- a/solution.py
+++ b/solution.py
@@ -24,7 +24,7 @@
 PARTS = 8
 OFFSETS = (0, 16, -16, 32, -32, 4, -4, 8, -8, 1, -1, 2, -2)
 FIRST_FAR = 4
-SLOTS = 46
+SLOTS = 48
 SCALE = 1.0 / math.sqrt(E)
 LOG2E = 1.4426950408889634
 COEF = SCALE * LOG2E
@@ -117,7 +117,7 @@
             8: lambda: 12,
             -8: lambda: 12,
             1: lambda: jnp.where(x == 0, 30, 36),
-            -1: lambda: jnp.where(x == 3, 30, 41),
+            -1: lambda: jnp.where(x == 3, 30, 42),
             2: lambda: jnp.where(low, 24, 18),
             -2: lambda: jnp.where(low, 18, 24),
         }[offset]()
@@ -150,8 +150,8 @@
 
 def fetch(parts, pool, sems, wholes=(), only_x=False):
     copies = []
-    at = 0
     for n, ref in enumerate(parts):
+        at = 6 * n
         size = ref.shape[0]
         for first, count in (((0, 1), (5, 1)) if only_x else ((0, size),)):
             if first < size:
@@ -162,7 +162,6 @@
                         sems.at[2 * n + (first > 0)],
                     )
                 )
-        at += size
     for n, (whole, target) in enumerate(wholes):
         copies.append(pltpu.make_async_copy(whole, target, sems.at[2 * PARTS + n]))
     far_count = len(copies) - len(wholes)
@@ -455,18 +454,18 @@
 
 
 def start_exchange(own):
-    across = move(own, lambda x, y: (x + 2, y))
     up = move(own, lambda x, y: (x, y + 1))
     down = move(own, lambda x, y: (x, y - 1))
+    across = move(own, lambda x, y: (x + 2, y))
     return up, down, across
 
 
-def end_exchange(own5, up, down, across, turned):
+def end_exchange(own, up, down, across, turned):
     eight = move(turned, lambda x, y: (x, y - 1) if x < 2 else (x, y + 1))
     aslant = move(across, lambda x, y: (x, y + 1) if x < 2 else (x, y - 1))
     wrap = move(turned, lambda x, y: (3 - x, y) if x in (0, 3) else None)
-    left = move(own5, lambda x, y: (x + 1, y) if x < 3 else None)
-    right = move(own5, lambda x, y: (x - 1, y) if x > 0 else None)
+    left = move(own, lambda x, y: (x + 1, y) if x < 3 else None)
+    right = move(own, lambda x, y: (x - 1, y) if x > 0 else None)
     return up, down, eight, across, aslant, wrap, left, right
 
 
@@ -490,8 +489,9 @@
     qg = pack(pos, block_frame, rates, queries, grad_output)
     kv_own = slots_of(kv[:, :, 0], kv[:, :, 1], zh, p)
     up, down, across = start_exchange(kv_own)
-    qg, up, down, across = lax.optimization_barrier((qg, up, down, across))
-    kv_parts = end_exchange(kv_own[:5], up, down, across, jnp.where(low, down, up))
+    own5 = kv_own[:5]
+    across, down, up, own5, qg = lax.optimization_barrier((across, down, up, own5, qg))
+    kv_parts = end_exchange(own5, up, down, across, jnp.where(low, down, up))
     qg = gather_heads(qg)
     qg_own = slots_of(qg[:, :, 0], qg[:, :, 1], zh, p)
     qg_own, kv_some = lax.optimization_barrier((qg_own, kv_parts[2:6]))
@@ -499,16 +499,16 @@
     up, down, across = start_exchange(qg_own)
     att, stats = forward_side(pos, block_mask, kv, qg, kv_parts)
     turned = jnp.where(low, down, up)
-    own5, turned, across, att, stats = lax.optimization_barrier(
-        (qg_own[:5], turned, across, att, stats)
+    own, turned, across, att, stats = lax.optimization_barrier(
+        (qg_own, turned, across, att, stats)
     )
-    qg_parts = end_exchange(own5, up, down, across, turned)
+    qg_parts = end_exchange(own, up, down, across, turned)
     every = lax.all_to_all(
         jnp.broadcast_to(stats[None], (GROUPS, SROWS, E)), ("zh", "p"), 0, 0, tiled=True
     )
     scalars = (pos, block_frame, rates)
     am, ax = query_side(scalars, block_mask, kv, qg, att, stats, kv_parts)
-    am, ax, every, qg_parts = lax.optimization_barrier((am, ax, every, qg_parts))
+    am, every = lax.optimization_barrier((am, every))
     bm = key_side(scalars, block_mask, kv, qg, every, qg_parts)
     out = lax.all_to_all(am.reshape(16, 2, QTR, E), ("zh", "h"), 0, 0, tiled=True)
     out, bm = lax.optimization_barrier((out, bm))

time: 215 us -> 212 us (0.986)
  waiting for transfers between devices: 83.7 us -> 72.8 us
  starting transfers between devices: 64.5 us -> 72.9 us
    ppermute x16, waiting for transfers between devices: 26.8 us -> 17.7 us  [move(): return lax.ppermute(value, 'p', pairs)]
    ppermute x16, starting transfers between devices: 31.7 us -> 36 us  [move(): return lax.ppermute(value, 'p', pairs)]
  transfers between devices with their start and end apart: 24 -> 24, of which waited for: 15 -> 13; matrix products, arithmetic and copies ran while one was open for 2% -> 2% of each run, Pallas kernels for 23% -> 23%
where the time goes in v5:
time: 212 us; the launch traced here: 211 us
  starting transfers between devices  72.9 us (34%)
  waiting for transfers between devices  72.8 us (34%)
  Pallas kernels  54.9 us (26%)
  local copies, waits for them, and re-layouts  5.08 us (2%)
  other arithmetic  4.64 us (2%)
    pallas_call x4, Pallas kernels, side(): pl.pallas_call(kernel, out_shape=out_shape, in_specs=specs + [HBM] * len(...  46.5 us
    all_to_all x2, waiting for transfers between devices, gather_heads(): wide = lax.all_to_all(packed, ('zh', 'h'), 0, 0, tiled=True)  42.8 us
    ppermute x16, starting transfers between devices, move(): return lax.ppermute(value, 'p', pairs)  36 us
    ppermute x16, waiting for transfers between devices, move(): return lax.ppermute(value, 'p', pairs)  17.7 us
    all_to_all x2, starting transfers between devices, gather_heads(): wide = lax.all_to_all(packed, ('zh', 'h'), 0, 0, tiled=True)  14.1 us
    all_to_all x1, starting transfers between devices, shards(): lax.all_to_all(am.reshape(16, 2, QTR, E), ('zh', 'h'), 0, 0, tiled=True)  9.94 us
    ppermute x3, waiting for transfers between devices, shards(): lax.ppermute(pieces[n], 'h', [(i, (i + n) % 4) for i in range(4)])  8.71 us
    all_to_all x1, starting transfers between devices, shards(): lax.all_to_all(jnp.broadcast_to(stats[None], (GROUPS, SROWS, E)), ('zh',...  6.38 us
  transfers between devices with their start and end apart: 24, of which 13 were waited for; matrix products, arithmetic and copies ran while one was open for 2% of the time, Pallas kernels for 23%

profile of v5, /device:TPU:1, one launch (start us, length us, event | category | flops | bytes accessed | tf_op | source)
XLA Modules:
  0.0 211.2 jit_solution(3051911965031909795)
XLA Ops:
  0.6 0.6 pad_add_fusion.pos
  1.2 3.0 %pack.2 = bf16[16,2,2,64,128]{4,3,2,1,0:T(8,128)(2,1)} custom-call(s32[3]{0:T(128)} %pad_add_fusion.pos, s32[128]{0:T(128)} %frames.9, f32[8,128]{1,0:T(8,128)} %constant.36.clone.rates, bf16[20,64,128]{2,1,0:T(8,128)(2,1)} %bitcast.40, bf16[20,64,128]{2,1,0:T(8,128)(2,1)} %bitcast.41), custom_call_target="tpu_custom_call" | custom-call | tf_op jit(solution)/shard_map/pack/pallas_call | solution.py:67
  4.2 10.0 %all-to-all-start = ((bf16[16,2,2,64,128]{4,3,2,1,0:T(8,128)(2,1)}), bf16[16,2,2,64,128]{4,3,2,1,0:T(8,128)(2,1)S(1)}, u32[]{:S(2)}, u32[]{:S(2)}) async-start(bf16[16,2,2,64,128]{4,3,2,1,0:T(8,128)(2,1)} %pack.2), calls=%async_computation | async-start | bytes 2097152 | tf_op jit(solution)/shard_map/all_to_all | solution.py:479
  14.2 27.9 %all-to-all-done = bf16[16,2,2,64,128]{4,3,2,1,0:T(8,128)(2,1)S(1)} async-done(((bf16[16,2,2,64,128]{4,3,2,1,0:T(8,128)(2,1)}), bf16[16,2,2,64,128]{4,3,2,1,0:T(8,128)(2,1)S(1)}, u32[]{:S(2)}, u32[]{:S(2)}) %all-to-all-start) | async-done | bytes 1048608 | tf_op jit(solution)/shard_map/all_to_all | solution.py:479
  42.3 0.9 copy-done
  43.4 1.4 collective-permute-start.2
  44.8 1.5 collective-permute-start.1
  46.3 2.7 %collective-permute-start = (bf16[6,4,2,64,128]{4,3,2,1,0:T(8,128)(2,1)S(1)}, bf16[6,4,2,64,128]{4,3,2,1,0:T(8,128)(2,1)S(1)}, u32[]{:S(2)}, u32[]{:S(2)}) collective-permute-start(bf16[6,4,2,64,128]{4,3,2,1,0:T(8,128)(2,1)S(1)} %pad_maximum_fusion), channel_id=1, source_target_pairs={{0,8},{4,12},{8,0},{12,4},{16,24},{20,28},{24,16},{28,20},{32,40},... | collective-permute-start | bytes 2359304 | tf_op jit(solution)/shard_map/ppermute | solution.py:453
  49.1 3.0 %pack.3 = bf16[16,2,2,64,128]{4,3,2,1,0:T(8,128)(2,1)} custom-call(s32[3]{0:T(128)} %pad_add_fusion.pos, s32[128]{0:T(128)} %frames.9, f32[8,128]{1,0:T(8,128)} %constant.36.clone.rates, bf16[20,64,128]{2,1,0:T(8,128)(2,1)} %bitcast.42, bf16[20,64,128]{2,1,0:T(8,128)(2,1)} %bitcast.43), custom_call_target="tpu_custom_call" | custom-call | tf_op jit(solution)/shard_map/pack/pallas_call | solution.py:67
  52.1 0.9 pad_maximum_fusion.2
  53.0 10.6 %collective-permute-done.2.refs_0_ = bf16[6,4,2,64,128]{4,3,2,1,0:T(8,128)(2,1)S(1)} collective-permute-done((bf16[6,4,2,64,128]{4,3,2,1,0:T(8,128)(2,1)S(1)}, bf16[6,4,2,64,128]{4,3,2,1,0:T(8,128)(2,1)S(1)}, u32[]{:S(2)}, u32[]{:S(2)}) %collective-permute-start.2) | collective-permute-done | bytes 786464 | tf_op jit(solution)/shard_map/ppermute | solution.py:453
  63.9 2.9 %collective-permute-done.refs_3_ = bf16[6,4,2,64,128]{4,3,2,1,0:T(8,128)(2,1)S(1)} collective-permute-done((bf16[6,4,2,64,128]{4,3,2,1,0:T(8,128)(2,1)S(1)}, bf16[6,4,2,64,128]{4,3,2,1,0:T(8,128)(2,1)S(1)}, u32[]{:S(2)}, u32[]{:S(2)}) %collective-permute-start) | collective-permute-done | bytes 786464 | tf_op jit(solution)/shard_map/ppermute | solution.py:453
  66.8 4.1 %all-to-all-start.1 = ((bf16[16,2,2,64,128]{4,3,2,1,0:T(8,128)(2,1)}), bf16[16,2,2,64,128]{4,3,2,1,0:T(8,128)(2,1)S(1)}, u32[]{:S(2)}, u32[]{:S(2)}) async-start(bf16[16,2,2,64,128]{4,3,2,1,0:T(8,128)(2,1)} %pack.3), calls=%async_computation.1 | async-start | bytes 2097152 | tf_op jit(solution)/shard_map/all_to_all | solution.py:479
  70.9 1.0 broadcast_select_fusion.1
  71.9 4.4 %collective-permute-start.5 = (bf16[6,4,2,64,128]{4,3,2,1,0:T(8,128)(2,1)}, bf16[6,4,2,64,128]{4,3,2,1,0:T(8,128)(2,1)S(1)}, u32[]{:S(2)}, u32[]{:S(2)}) collective-permute-start(bf16[6,4,2,64,128]{4,3,2,1,0:T(8,128)(2,1)} %broadcast_select_fusion.1), channel_id=1, source_target_pairs={{0,12},{12,0},{16,28},{28,16},{32,44},{44,32},{48,60},{60,48},{1,1... | collective-permute-start | bytes 2359304 | tf_op jit(solution)/shard_map/ppermute | solution.py:453
  76.3 1.4 collective-permute-start.3
  77.8 1.3 collective-permute-start.7
  79.1 4.8 %collective-permute-start.6 = (bf16[5,4,2,64,128]{4,3,2,1,0:T(8,128)(2,1)}, bf16[5,4,2,64,128]{4,3,2,1,0:T(8,128)(2,1)}, u32[]{:S(2)}, u32[]{:S(2)}) collective-permute-start(bf16[5,4,2,64,128]{4,3,2,1,0:T(8,128)(2,1)} %pad_maximum_fusion.2), channel_id=1, source_target_pairs={{0,4},{4,8},{8,12},{16,20},{20,24},{24,28},{32,36},{36,40},{40,44}... | collective-permute-start | bytes 1966088 | tf_op jit(solution)/shard_map/ppermute | solution.py:453
  84.0 14.9 %all-to-all-done.1 = bf16[16,2,2,64,128]{4,3,2,1,0:T(8,128)(2,1)S(1)} async-done(((bf16[16,2,2,64,128]{4,3,2,1,0:T(8,128)(2,1)}), bf16[16,2,2,64,128]{4,3,2,1,0:T(8,128)(2,1)S(1)}, u32[]{:S(2)}, u32[]{:S(2)}) %all-to-all-start.1) | async-done | bytes 1048608 | tf_op jit(solution)/shard_map/all_to_all | solution.py:479
  98.9 0.9 copy-done.1
  99.8 1.0 pad_maximum_fusion.1
  101.0 2.7 %collective-permute-start.8 = (bf16[6,4,2,64,128]{4,3,2,1,0:T(8,128)(2,1)}, bf16[6,4,2,64,128]{4,3,2,1,0:T(8,128)(2,1)S(1)}, u32[]{:S(2)}, u32[]{:S(2)}) collective-permute-start(bf16[6,4,2,64,128]{4,3,2,1,0:T(8,128)(2,1)} %pad_maximum_fusion.1), channel_id=1, source_target_pairs={{0,48},{4,52},{8,56},{12,60},{16,0},{20,4},{24,8},{28,12},{32,16},... | collective-permute-start | bytes 2359304 | tf_op jit(solution)/shard_map/ppermute | solution.py:453
  103.6 2.7 %collective-permute-start.10 = (bf16[6,4,2,64,128]{4,3,2,1,0:T(8,128)(2,1)}, bf16[6,4,2,64,128]{4,3,2,1,0:T(8,128)(2,1)S(1)}, u32[]{:S(2)}, u32[]{:S(2)}) collective-permute-start(bf16[6,4,2,64,128]{4,3,2,1,0:T(8,128)(2,1)} %pad_maximum_fusion.1), channel_id=1, source_target_pairs={{0,8},{4,12},{8,0},{12,4},{16,24},{20,28},{24,16},{28,20},{32,40},... | collective-permute-start | bytes 2359304 | tf_op jit(solution)/shard_map/ppermute | solution.py:453
  106.4 13.9 %forward_kernel.1 = (bf16[5,4,1,64,128]{4,3,2,1,0:T(8,128)(2,1)}, f32[24,128]{1,0:T(8,128)}) custom-call(s32[3]{0:T(128)} %pad_add_fusion.pos, bf16[6,4,2,64,128]{4,3,2,1,0:T(8,128)(2,1)} %copy-done.2, bf16[6,4,2,64,128]{4,3,2,1,0:T(8,128)(2,1)} %copy-done.3, bf16[6,4,2,64,128]{4,3,2,1,0:T(8,128)(2,1)} %collective-permute-done.3.refs_2_, ...), custom_call_target="tpu_custom_call" | custom-call | flops 2181038080 | bytes 8388608 | tf_op jit(solution)/shard_map/forward_kernel/pallas_call | solution.py:395
  120.3 1.0 collective-permute-done.9.refs_0_
  121.2 1.1 broadcast_select_fusion
  122.6 2.0 collective-permute-done.10.refs_3_
  124.6 1.0 broadcast_in_dim.2
  125.6 6.4 %all-to-all-start.2 = ((f32[64,24,128]{2,1,0:T(8,128)}), f32[64,24,128]{2,1,0:T(8,128)S(1)}, u32[]{:S(2)}, u32[]{:S(2)}) async-start(f32[64,24,128]{2,1,0:T(8,128)} %broadcast_in_dim.2), calls=%async_computation.2 | async-start | bytes 1572864 | tf_op jit(solution)/shard_map/all_to_all | solution.py:506
  132.0 4.1 %collective-permute-start.13 = (bf16[6,4,2,64,128]{4,3,2,1,0:T(8,128)(2,1)}, bf16[6,4,2,64,128]{4,3,2,1,0:T(8,128)(2,1)S(1)}, u32[]{:S(2)}, u32[]{:S(2)}) collective-permute-start(bf16[6,4,2,64,128]{4,3,2,1,0:T(8,128)(2,1)} %broadcast_select_fusion), channel_id=1, source_target_pairs={{0,12},{12,0},{16,28},{28,16},{32,44},{44,32},{48,60},{60,48},{1,1... | collective-permute-start | bytes 2359304 | tf_op jit(solution)/shard_map/ppermute | solution.py:453
  136.2 2.5 %collective-permute-start.11 = (bf16[6,4,2,64,128]{4,3,2,1,0:T(8,128)(2,1)}, bf16[6,4,2,64,128]{4,3,2,1,0:T(8,128)(2,1)}, u32[]{:S(2)}, u32[]{:S(2)}) collective-permute-start(bf16[6,4,2,64,128]{4,3,2,1,0:T(8,128)(2,1)} %broadcast_select_fusion), channel_id=1, source_target_pairs={{0,48},{4,52},{8,24},{12,28},{16,0},{20,4},{24,40},{28,44},{32,16}... | collective-permute-start | bytes 2359304 | tf_op jit(solution)/shard_map/ppermute | solution.py:453
  138.6 1.3 collective-permute-start.15
  139.9 4.9 %collective-permute-start.14 = (bf16[6,4,2,64,128]{4,3,2,1,0:T(8,128)(2,1)}, bf16[6,4,2,64,128]{4,3,2,1,0:T(8,128)(2,1)}, u32[]{:S(2)}, u32[]{:S(2)}) collective-permute-start(bf16[6,4,2,64,128]{4,3,2,1,0:T(8,128)(2,1)} %pad_maximum_fusion.1), channel_id=1, source_target_pairs={{0,4},{4,8},{8,12},{16,20},{20,24},{24,28},{32,36},{36,40},{40,44}... | collective-permute-start | bytes 2359304 | tf_op jit(solution)/shard_map/ppermute | solution.py:453
  144.8 13.6 %query_kernel.1 = (bf16[4,4,2,64,128]{4,3,2,1,0:T(8,128)(2,1)}, bf16[1,4,2,64,128]{4,3,2,1,0:T(8,128)(2,1)}) custom-call(s32[3]{0:T(128)} %pad_add_fusion.pos, s32[128]{0:T(128)} %frames.9, f32[8,128]{1,0:T(8,128)} %constant.36.clone.rates, bf16[6,4,2,64,128]{4,3,2,1,0:T(8,128)(2,1)} %copy-done.2, bf16[6,4,2,64,128]{4,3,2,1,0:T(8,128)(2,1)} %copy-done.3, ...), custom_call_target="tpu_custom_call" | custom-call | flops 3271557120 | bytes 8388608 | tf_op jit(solution)/shard_map/query_kernel/pallas_call | solution.py:395
  158.4 9.9 %all-to-all-start.3 = ((bf16[16,2,64,128]{3,2,1,0:T(8,128)(2,1)}), bf16[16,2,64,128]{3,2,1,0:T(8,128)(2,1)S(1)}, u32[]{:S(2)}, u32[]{:S(2)}) async-start(bf16[16,2,64,128]{3,2,1,0:T(8,128)(2,1)} %bitcast.39), calls=%async_computation.3 | async-start | bytes 1048576 | tf_op jit(solution)/shard_map/all_to_all | solution.py:513
  168.4 0.9 collective-permute-done.12.refs_4_
  169.3 13.5 %key_kernel.1 = bf16[4,4,2,64,128]{4,3,2,1,0:T(8,128)(2,1)} custom-call(s32[3]{0:T(128)} %pad_add_fusion.pos, s32[128]{0:T(128)} %frames.9, f32[8,128]{1,0:T(8,128)} %constant.36.clone.rates, bf16[6,4,2,64,128]{4,3,2,1,0:T(8,128)(2,1)} %copy-done.4, bf16[6,4,2,64,128]{4,3,2,1,0:T(8,128)(2,1)} %copy-done.5, ...), custom_call_target="tpu_custom_call" | custom-call | flops 3489660928 | bytes 8388608 | tf_op jit(solution)/shard_map/key_kernel/pallas_call | solution.py:395
  182.8 2.9 %all-to-all-done.3.a_ref = bf16[16,2,64,128]{3,2,1,0:T(8,128)(2,1)S(1)} async-done(((bf16[16,2,64,128]{3,2,1,0:T(8,128)(2,1)}), bf16[16,2,64,128]{3,2,1,0:T(8,128)(2,1)S(1)}, u32[]{:S(2)}, u32[]{:S(2)}) %all-to-all-start.3) | async-done | bytes 524320 | tf_op jit(solution)/shard_map/all_to_all | solution.py:513
  185.7 0.8 copy-done.7
  186.5 4.3 %all-to-all-start.4 = ((bf16[16,2,64,128]{3,2,1,0:T(8,128)(2,1)}), bf16[16,2,64,128]{3,2,1,0:T(8,128)(2,1)S(1)}, u32[]{:S(2)}, u32[]{:S(2)}) async-start(bf16[16,2,64,128]{3,2,1,0:T(8,128)(2,1)} %bitcast.38), calls=%async_computation.4 | async-start | bytes 1048576 | tf_op jit(solution)/shard_map/all_to_all | solution.py:518
  190.8 5.6 %extra_key_kernel.1 = (bf16[4,64,128]{2,1,0:T(8,128)(2,1)}, bf16[4,64,128]{2,1,0:T(8,128)(2,1)}, bf16[4,64,128]{2,1,0:T(8,128)(2,1)}, bf16[4,64,128]{2,1,0:T(8,128)(2,1)}) custom-call(s32[3]{0:T(128)} %pad_add_fusion.pos, s32[128]{0:T(128)} %frames.9, f32[8,128]{1,0:T(8,128)} %constant.36.clone.rates, bf16[6,4,2,64,128]{4,3,2,1,0:T(8,128)(2,1)} %copy-done.4, ...), custom_call_target="tpu_custom_call" | custom-call | flops 872415232 | bytes 8388608 | tf_op jit(solution)/shard_map/extra_key_kernel/pallas_call | solution.py:395
  196.4 1.7 collective-permute-start.16
  198.1 0.5 collective-permute-start.18
  198.7 4.3 %collective-permute-done.16.refs_1_ = bf16[4,64,128]{2,1,0:T(8,128)(2,1)S(1)} collective-permute-done((bf16[4,64,128]{2,1,0:T(8,128)(2,1)}, bf16[4,64,128]{2,1,0:T(8,128)(2,1)S(1)}, u32[]{:S(2)}, u32[]{:S(2)}) %collective-permute-start.16) | collective-permute-done | bytes 65568 | tf_op jit(solution)/shard_map/ppermute | solution.py:517
  202.9 4.0 %collective-permute-done.17.refs_2_ = bf16[4,64,128]{2,1,0:T(8,128)(2,1)S(1)} collective-permute-done((bf16[4,64,128]{2,1,0:T(8,128)(2,1)}, bf16[4,64,128]{2,1,0:T(8,128)(2,1)S(1)}, u32[]{:S(2)}, u32[]{:S(2)}) %collective-permute-start.17) | collective-permute-done | bytes 65568 | tf_op jit(solution)/shard_map/ppermute | solution.py:517
  207.4 0.7 all-to-all-done.4.b_ref
  208.1 0.8 copy-done.8
  208.9 2.3 %unpack.1 = (bf16[20,64,128]{2,1,0:T(8,128)(2,1)}, bf16[20,64,128]{2,1,0:T(8,128)(2,1)}, bf16[20,64,128]{2,1,0:T(8,128)(2,1)}, bf16[20,64,128]{2,1,0:T(8,128)(2,1)}) custom-call(s32[3]{0:T(128)} %pad_add_fusion.pos, bf16[16,2,64,128]{3,2,1,0:T(8,128)(2,1)} %copy-done.7, bf16[16,2,64,128]{3,2,1,0:T(8,128)(2,1)} %copy-done.8, ...), custom_call_target="tpu_custom_call" | custom-call | tf_op jit(solution)/shard_map/unpack/pallas_call | solution.py:92
  (53 shorter events, 1.9 us)
Async XLA Ops:
  4.2 37.9 %all-to-all-start = ((bf16[16,2,2,64,128]{4,3,2,1,0:T(8,128)(2,1)}), bf16[16,2,2,64,128]{4,3,2,1,0:T(8,128)(2,1)S(1)}, u32[]{:S(2)}, u32[]{:S(2)}) async-start(bf16[16,2,2,64,128]{4,3,2,1,0:T(8,128)(2,1)} %pack.2), calls=%async_computation | async-start | bytes 2097152 | tf_op jit(solution)/shard_map/all_to_all | solution.py:479
  42.2 1.0 copy-start
  43.4 20.1 %collective-permute-start.2 = (bf16[6,4,2,64,128]{4,3,2,1,0:T(8,128)(2,1)S(1)}, bf16[6,4,2,64,128]{4,3,2,1,0:T(8,128)(2,1)S(1)}, u32[]{:S(2)}, u32[]{:S(2)}) collective-permute-start(bf16[6,4,2,64,128]{4,3,2,1,0:T(8,128)(2,1)S(1)} %pad_maximum_fusion), channel_id=1, source_target_pairs={{0,16},{4,20},{8,24},{12,28},{16,32},{20,36},{24,40},{28,44},{32,4... | collective-permute-start | bytes 2359304 | tf_op jit(solution)/shard_map/ppermute | solution.py:453
  44.8 19.1 %collective-permute-start.1 = (bf16[6,4,2,64,128]{4,3,2,1,0:T(8,128)(2,1)S(1)}, bf16[6,4,2,64,128]{4,3,2,1,0:T(8,128)(2,1)S(1)}, u32[]{:S(2)}, u32[]{:S(2)}) collective-permute-start(bf16[6,4,2,64,128]{4,3,2,1,0:T(8,128)(2,1)S(1)} %pad_maximum_fusion), channel_id=1, source_target_pairs={{0,48},{4,52},{8,56},{12,60},{16,0},{20,4},{24,8},{28,12},{32,16},... | collective-permute-start | bytes 2359304 | tf_op jit(solution)/shard_map/ppermute | solution.py:453
  46.3 20.5 %collective-permute-start = (bf16[6,4,2,64,128]{4,3,2,1,0:T(8,128)(2,1)S(1)}, bf16[6,4,2,64,128]{4,3,2,1,0:T(8,128)(2,1)S(1)}, u32[]{:S(2)}, u32[]{:S(2)}) collective-permute-start(bf16[6,4,2,64,128]{4,3,2,1,0:T(8,128)(2,1)S(1)} %pad_maximum_fusion), channel_id=1, source_target_pairs={{0,8},{4,12},{8,0},{12,4},{16,24},{20,28},{24,16},{28,20},{32,40},... | collective-permute-start | bytes 2359304 | tf_op jit(solution)/shard_map/ppermute | solution.py:453
  63.5 7.4 %copy-start.2 = (bf16[6,4,2,64,128]{4,3,2,1,0:T(8,128)(2,1)}, bf16[6,4,2,64,128]{4,3,2,1,0:T(8,128)(2,1)S(1)}, u32[]{:S(2)}) copy-start(bf16[6,4,2,64,128]{4,3,2,1,0:T(8,128)(2,1)S(1)} %collective-permute-done.2.refs_0_) | copy-start | bytes 2359300
  63.9 7.0 %copy-start.3 = (bf16[6,4,2,64,128]{4,3,2,1,0:T(8,128)(2,1)}, bf16[6,4,2,64,128]{4,3,2,1,0:T(8,128)(2,1)S(1)}, u32[]{:S(2)}) copy-start(bf16[6,4,2,64,128]{4,3,2,1,0:T(8,128)(2,1)S(1)} %collective-permute-done.1.refs_1_) | copy-start | bytes 2359300
  66.8 10.9 %copy-start.9 = (bf16[6,4,2,64,128]{4,3,2,1,0:T(8,128)(2,1)}, bf16[6,4,2,64,128]{4,3,2,1,0:T(8,128)(2,1)S(1)}, u32[]{:S(2)}) copy-start(bf16[6,4,2,64,128]{4,3,2,1,0:T(8,128)(2,1)S(1)} %collective-permute-done.refs_3_) | copy-start | bytes 2359300
  66.8 32.1 %all-to-all-start.1 = ((bf16[16,2,2,64,128]{4,3,2,1,0:T(8,128)(2,1)}), bf16[16,2,2,64,128]{4,3,2,1,0:T(8,128)(2,1)S(1)}, u32[]{:S(2)}, u32[]{:S(2)}) async-start(bf16[16,2,2,64,128]{4,3,2,1,0:T(8,128)(2,1)} %pack.3), calls=%async_computation.1 | async-start | bytes 2097152 | tf_op jit(solution)/shard_map/all_to_all | solution.py:479
  71.9 29.0 %collective-permute-start.5 = (bf16[6,4,2,64,128]{4,3,2,1,0:T(8,128)(2,1)}, bf16[6,4,2,64,128]{4,3,2,1,0:T(8,128)(2,1)S(1)}, u32[]{:S(2)}, u32[]{:S(2)}) collective-permute-start(bf16[6,4,2,64,128]{4,3,2,1,0:T(8,128)(2,1)} %broadcast_select_fusion.1), channel_id=1, source_target_pairs={{0,12},{12,0},{16,28},{28,16},{32,44},{44,32},{48,60},{60,48},{1,1... | collective-permute-start | bytes 2359304 | tf_op jit(solution)/shard_map/ppermute | solution.py:453
  76.3 24.6 %collective-permute-start.3 = (bf16[6,4,2,64,128]{4,3,2,1,0:T(8,128)(2,1)}, bf16[6,4,2,64,128]{4,3,2,1,0:T(8,128)(2,1)}, u32[]{:S(2)}, u32[]{:S(2)}) collective-permute-start(bf16[6,4,2,64,128]{4,3,2,1,0:T(8,128)(2,1)} %broadcast_select_fusion.1), channel_id=1, source_target_pairs={{0,48},{4,52},{8,24},{12,28},{16,0},{20,4},{24,40},{28,44},{32,16}... | collective-permute-start | bytes 2359304 | tf_op jit(solution)/shard_map/ppermute | solution.py:453
  77.7 23.1 %collective-permute-start.4 = (bf16[6,4,2,64,128]{4,3,2,1,0:T(8,128)(2,1)S(1)}, bf16[6,4,2,64,128]{4,3,2,1,0:T(8,128)(2,1)}, u32[]{:S(2)}, u32[]{:S(2)}) collective-permute-start(bf16[6,4,2,64,128]{4,3,2,1,0:T(8,128)(2,1)S(1)} %collective-permute-done.refs_3_), channel_id=1, source_target_pairs={{0,16},{4,20},{8,56},{12,60},{16,32},{20,36},{24,8},{28,12},{32,48... | collective-permute-start | bytes 2359304 | tf_op jit(solution)/shard_map/ppermute | solution.py:453
  77.8 28.5 %collective-permute-start.7 = (bf16[5,4,2,64,128]{4,3,2,1,0:T(8,128)(2,1)}, bf16[5,4,2,64,128]{4,3,2,1,0:T(8,128)(2,1)}, u32[]{:S(2)}, u32[]{:S(2)}) collective-permute-start(bf16[5,4,2,64,128]{4,3,2,1,0:T(8,128)(2,1)} %pad_maximum_fusion.2), channel_id=1, source_target_pairs={{4,0},{8,4},{12,8},{20,16},{24,20},{28,24},{36,32},{40,36},{44,40}... | collective-permute-start | bytes 1966088 | tf_op jit(solution)/shard_map/ppermute | solution.py:453
  79.1 27.3 %collective-permute-start.6 = (bf16[5,4,2,64,128]{4,3,2,1,0:T(8,128)(2,1)}, bf16[5,4,2,64,128]{4,3,2,1,0:T(8,128)(2,1)}, u32[]{:S(2)}, u32[]{:S(2)}) collective-permute-start(bf16[5,4,2,64,128]{4,3,2,1,0:T(8,128)(2,1)} %pad_maximum_fusion.2), channel_id=1, source_target_pairs={{0,4},{4,8},{8,12},{16,20},{20,24},{24,28},{32,36},{36,40},{40,44}... | collective-permute-start | bytes 1966088 | tf_op jit(solution)/shard_map/ppermute | solution.py:453
  98.8 1.0 copy-start.1
  100.9 5.5 %copy-start.10 = (bf16[6,4,2,64,128]{4,3,2,1,0:T(8,128)(2,1)}, bf16[6,4,2,64,128]{4,3,2,1,0:T(8,128)(2,1)S(1)}, u32[]{:S(2)}) copy-start(bf16[6,4,2,64,128]{4,3,2,1,0:T(8,128)(2,1)S(1)} %collective-permute-done.5.refs_5_) | copy-start | bytes 2359300
  100.9 20.3 %collective-permute-start.9 = (bf16[6,4,2,64,128]{4,3,2,1,0:T(8,128)(2,1)}, bf16[6,4,2,64,128]{4,3,2,1,0:T(8,128)(2,1)S(1)}, u32[]{:S(2)}, u32[]{:S(2)}) collective-permute-start(bf16[6,4,2,64,128]{4,3,2,1,0:T(8,128)(2,1)} %pad_maximum_fusion.1), channel_id=1, source_target_pairs={{0,16},{4,20},{8,24},{12,28},{16,32},{20,36},{24,40},{28,44},{32,4... | collective-permute-start | bytes 2359304 | tf_op jit(solution)/shard_map/ppermute | solution.py:453
  101.0 20.3 %collective-permute-start.8 = (bf16[6,4,2,64,128]{4,3,2,1,0:T(8,128)(2,1)}, bf16[6,4,2,64,128]{4,3,2,1,0:T(8,128)(2,1)S(1)}, u32[]{:S(2)}, u32[]{:S(2)}) collective-permute-start(bf16[6,4,2,64,128]{4,3,2,1,0:T(8,128)(2,1)} %pad_maximum_fusion.1), channel_id=1, source_target_pairs={{0,48},{4,52},{8,56},{12,60},{16,0},{20,4},{24,8},{28,12},{32,16},... | collective-permute-start | bytes 2359304 | tf_op jit(solution)/shard_map/ppermute | solution.py:453
  103.6 21.0 %collective-permute-start.10 = (bf16[6,4,2,64,128]{4,3,2,1,0:T(8,128)(2,1)}, bf16[6,4,2,64,128]{4,3,2,1,0:T(8,128)(2,1)S(1)}, u32[]{:S(2)}, u32[]{:S(2)}) collective-permute-start(bf16[6,4,2,64,128]{4,3,2,1,0:T(8,128)(2,1)} %pad_maximum_fusion.1), channel_id=1, source_target_pairs={{0,8},{4,12},{8,0},{12,4},{16,24},{20,28},{24,16},{28,20},{32,40},... | collective-permute-start | bytes 2359304 | tf_op jit(solution)/shard_map/ppermute | solution.py:453
  121.2 1.2 copy-start.4
  121.2 1.4 copy-start.5
  121.2 3.4 %copy-start.16 = (f32[24,128]{1,0:T(8,128)S(1)}, f32[24,128]{1,0:T(8,128)}, u32[]{:S(2)}) copy-start(f32[24,128]{1,0:T(8,128)} %get-tuple-element.48.refs_12_) | copy-start | bytes 36868
  124.6 20.2 %copy-start.11 = (bf16[6,4,2,64,128]{4,3,2,1,0:T(8,128)(2,1)}, bf16[6,4,2,64,128]{4,3,2,1,0:T(8,128)(2,1)S(1)}, u32[]{:S(2)}) copy-start(bf16[6,4,2,64,128]{4,3,2,1,0:T(8,128)(2,1)S(1)} %collective-permute-done.10.refs_3_) | copy-start | bytes 2359300
  125.6 32.8 %all-to-all-start.2 = ((f32[64,24,128]{2,1,0:T(8,128)}), f32[64,24,128]{2,1,0:T(8,128)S(1)}, u32[]{:S(2)}, u32[]{:S(2)}) async-start(f32[64,24,128]{2,1,0:T(8,128)} %broadcast_in_dim.2), calls=%async_computation.2 | async-start | bytes 1572864 | tf_op jit(solution)/shard_map/all_to_all | solution.py:506
  132.0 36.3 %collective-permute-start.13 = (bf16[6,4,2,64,128]{4,3,2,1,0:T(8,128)(2,1)}, bf16[6,4,2,64,128]{4,3,2,1,0:T(8,128)(2,1)S(1)}, u32[]{:S(2)}, u32[]{:S(2)}) collective-permute-start(bf16[6,4,2,64,128]{4,3,2,1,0:T(8,128)(2,1)} %broadcast_select_fusion), channel_id=1, source_target_pairs={{0,12},{12,0},{16,28},{28,16},{32,44},{44,32},{48,60},{60,48},{1,1... | collective-permute-start | bytes 2359304 | tf_op jit(solution)/shard_map/ppermute | solution.py:453
  136.2 32.2 %collective-permute-start.11 = (bf16[6,4,2,64,128]{4,3,2,1,0:T(8,128)(2,1)}, bf16[6,4,2,64,128]{4,3,2,1,0:T(8,128)(2,1)}, u32[]{:S(2)}, u32[]{:S(2)}) collective-permute-start(bf16[6,4,2,64,128]{4,3,2,1,0:T(8,128)(2,1)} %broadcast_select_fusion), channel_id=1, source_target_pairs={{0,48},{4,52},{8,24},{12,28},{16,0},{20,4},{24,40},{28,44},{32,16}... | collective-permute-start | bytes 2359304 | tf_op jit(solution)/shard_map/ppermute | solution.py:453
  138.6 29.8 %collective-permute-start.15 = (bf16[6,4,2,64,128]{4,3,2,1,0:T(8,128)(2,1)}, bf16[6,4,2,64,128]{4,3,2,1,0:T(8,128)(2,1)}, u32[]{:S(2)}, u32[]{:S(2)}) collective-permute-start(bf16[6,4,2,64,128]{4,3,2,1,0:T(8,128)(2,1)} %pad_maximum_fusion.1), channel_id=1, source_target_pairs={{4,0},{8,4},{12,8},{20,16},{24,20},{28,24},{36,32},{40,36},{44,40}... | collective-permute-start | bytes 2359304 | tf_op jit(solution)/shard_map/ppermute | solution.py:453
  139.9 28.5 %collective-permute-start.14 = (bf16[6,4,2,64,128]{4,3,2,1,0:T(8,128)(2,1)}, bf16[6,4,2,64,128]{4,3,2,1,0:T(8,128)(2,1)}, u32[]{:S(2)}, u32[]{:S(2)}) collective-permute-start(bf16[6,4,2,64,128]{4,3,2,1,0:T(8,128)(2,1)} %pad_maximum_fusion.1), channel_id=1, source_target_pairs={{0,4},{4,8},{8,12},{16,20},{20,24},{24,28},{32,36},{36,40},{40,44}... | collective-permute-start | bytes 2359304 | tf_op jit(solution)/shard_map/ppermute | solution.py:453
  144.8 24.5 %collective-permute-start.12 = (bf16[6,4,2,64,128]{4,3,2,1,0:T(8,128)(2,1)S(1)}, bf16[6,4,2,64,128]{4,3,2,1,0:T(8,128)(2,1)}, u32[]{:S(2)}, u32[]{:S(2)}) collective-permute-start(bf16[6,4,2,64,128]{4,3,2,1,0:T(8,128)(2,1)S(1)} %collective-permute-done.10.refs_3_), channel_id=1, source_target_pairs={{0,16},{4,20},{8,56},{12,60},{16,32},{20,36},{24,8},{28,12},{32,48... | collective-permute-start | bytes 2359304 | tf_op jit(solution)/shard_map/ppermute | solution.py:453
  158.4 10.9 %copy-start.6 = (f32[64,24,128]{2,1,0:T(8,128)}, f32[64,24,128]{2,1,0:T(8,128)S(1)}, u32[]{:S(2)}) copy-start(f32[64,24,128]{2,1,0:T(8,128)S(1)} %all-to-all-done.2.refs_11_) | copy-start | bytes 2359300
  158.4 27.3 %all-to-all-start.3 = ((bf16[16,2,64,128]{3,2,1,0:T(8,128)(2,1)}), bf16[16,2,64,128]{3,2,1,0:T(8,128)(2,1)S(1)}, u32[]{:S(2)}, u32[]{:S(2)}) async-start(bf16[16,2,64,128]{3,2,1,0:T(8,128)(2,1)} %bitcast.39), calls=%async_computation.3 | async-start | bytes 1048576 | tf_op jit(solution)/shard_map/all_to_all | solution.py:513
  168.4 1.0 copy-start.12
  185.7 0.8 copy-start.7
  186.5 21.6 %all-to-all-start.4 = ((bf16[16,2,64,128]{3,2,1,0:T(8,128)(2,1)}), bf16[16,2,64,128]{3,2,1,0:T(8,128)(2,1)S(1)}, u32[]{:S(2)}, u32[]{:S(2)}) async-start(bf16[16,2,64,128]{3,2,1,0:T(8,128)(2,1)} %bitcast.38), calls=%async_computation.4 | async-start | bytes 1048576 | tf_op jit(solution)/shard_map/all_to_all | solution.py:518
  196.4 6.5 %collective-permute-start.16 = (bf16[4,64,128]{2,1,0:T(8,128)(2,1)}, bf16[4,64,128]{2,1,0:T(8,128)(2,1)S(1)}, u32[]{:S(2)}, u32[]{:S(2)}) collective-permute-start(bf16[4,64,128]{2,1,0:T(8,128)(2,1)} %get-tuple-element.59), channel_id=1, source_target_pairs={{0,1},{1,2},{2,3},{3,0},{4,5},{5,6},{6,7},{7,4},{8,9},{9,10},{10,1... | collective-permute-start | bytes 196616 | tf_op jit(solution)/shard_map/ppermute | solution.py:517
  198.1 8.8 %collective-permute-start.17 = (bf16[4,64,128]{2,1,0:T(8,128)(2,1)}, bf16[4,64,128]{2,1,0:T(8,128)(2,1)S(1)}, u32[]{:S(2)}, u32[]{:S(2)}) collective-permute-start(bf16[4,64,128]{2,1,0:T(8,128)(2,1)} %get-tuple-element.60), channel_id=1, source_target_pairs={{0,2},{1,3},{2,0},{3,1},{4,6},{5,7},{6,4},{7,5},{8,10},{9,11},{10,... | collective-permute-start | bytes 196616 | tf_op jit(solution)/shard_map/ppermute | solution.py:517
  198.1 9.3 %collective-permute-start.18 = (bf16[4,64,128]{2,1,0:T(8,128)(2,1)}, bf16[4,64,128]{2,1,0:T(8,128)(2,1)S(1)}, u32[]{:S(2)}, u32[]{:S(2)}) collective-permute-start(bf16[4,64,128]{2,1,0:T(8,128)(2,1)} %get-tuple-element.61), channel_id=1, source_target_pairs={{0,3},{1,0},{2,1},{3,2},{4,7},{5,4},{6,5},{7,6},{8,11},{9,8},{10,9... | collective-permute-start | bytes 196616 | tf_op jit(solution)/shard_map/ppermute | solution.py:517
  202.9 5.2 %copy-start.13 = (bf16[4,64,128]{2,1,0:T(8,128)(2,1)}, bf16[4,64,128]{2,1,0:T(8,128)(2,1)S(1)}, u32[]{:S(2)}) copy-start(bf16[4,64,128]{2,1,0:T(8,128)(2,1)S(1)} %collective-permute-done.16.refs_1_) | copy-start | bytes 196612
  206.9 1.2 copy-start.14
  207.4 0.7 copy-start.15
  208.1 0.8 copy-start.8

commit v6 on v5

--- a/solution.py
+++ b/solution.py
@@ -79,12 +79,21 @@
     )(pos, frames, rates, *[jnp.transpose(t, (1, 0, 2)) for t in tensors])
 
 
-def unpack_kernel(pos, a_ref, b_ref, *refs):
-    pieces, outs = refs[:4], refs[4:]
+def unpack_kernel(pos, a_hbm, b_hbm, *refs):
+    pieces, outs, sems = refs[:4], refs[4:8], refs[8]
+    copies = []
     for i, o in enumerate(outs):
-        o[:16] = (a_ref, b_ref)[i // 2][:, i % 2]
+        main = (a_hbm, b_hbm)[i // 2]
+        copies.append(
+            pltpu.make_async_copy(main.at[:, i % 2], o.at[pl.ds(0, 16)], sems.at[5 * i])
+        )
         for n, piece in enumerate(pieces):
-            o[16 + lax.rem(pos[2] - n + 4, 4)] = piece[i]
+            to = 16 + lax.rem(pos[2] - n + 4, 4)
+            copies.append(pltpu.make_async_copy(piece.at[i], o.at[to], sems.at[5 * i + n + 1]))
+    for copy in copies:
+        copy.start()
+    for copy in copies:
+        copy.wait()
 
 
 def unpack(pos, a, b, pieces):
@@ -92,9 +101,10 @@
     outs = pl.pallas_call(
         unpack_kernel,
         out_shape=(shape,) * 4,
-        in_specs=[SMEM] + [VMEM] * 6,
-        out_specs=(VMEM,) * 4,
-        compiler_params=LIMIT,
+        in_specs=[SMEM] + [pl.BlockSpec(memory_space=pl.ANY)] * 6,
+        out_specs=(HBM,) * 4,
+        scratch_shapes=[pltpu.SemaphoreType.DMA((20,))],
+        compiler_params=pltpu.CompilerParams(vmem_limit_bytes=2**20),
         name="unpack",
     )(pos, a, b, *pieces)
     return tuple(jnp.transpose(o, (1, 0, 2)) for o in outs)
@@ -490,7 +500,7 @@
     kv_own = slots_of(kv[:, :, 0], kv[:, :, 1], zh, p)
     up, down, across = start_exchange(kv_own)
     own5 = kv_own[:5]
-    across, down, up, own5, qg = lax.optimization_barrier((across, down, up, own5, qg))
+    across, down, up, own5 = lax.optimization_barrier((across, down, up, own5))
     kv_parts = end_exchange(own5, up, down, across, jnp.where(low, down, up))
     qg = gather_heads(qg)
     qg_own = slots_of(qg[:, :, 0], qg[:, :, 1], zh, p)

time: 212 us -> 207 us (0.976)
  waiting for transfers between devices: 72.8 us -> 63.9 us
  local copies, waits for them, and re-layouts: 5.08 us -> 7.33 us
    all_to_all x2, waiting for transfers between devices: 42.8 us -> 24.9 us  [gather_heads(): wide = lax.all_to_all(packed, ('zh', 'h'), 0, 0, tiled=True)]
    ppermute x16, waiting for transfers between devices: 17.7 us -> 26.7 us  [move(): return lax.ppermute(value, 'p', pairs)]
    all_to_all x1, starting transfers between devices: 6.38 us -> 9.33 us  [shards(): lax.all_to_all(jnp.broadcast_to(stats[None], (GROUPS, SROWS, E)), ('zh',...]
    ppermute x16, starting transfers between devices: 36 us -> 33 us  [move(): return lax.ppermute(value, 'p', pairs)]
    unnamed x34 -> x32, local copies, waits for them, and re-layouts: 3.73 us -> 5.97 us
  transfers between devices with their start and end apart: 24 -> 24, of which waited for: 13 -> 13; matrix products, arithmetic and copies ran while one was open for 2% -> 3% of each run, Pallas kernels for 23% -> 24%
where the time goes in v6:
time: 207 us; the launch traced here: 206 us
  starting transfers between devices  74.2 us (36%)
  waiting for transfers between devices  63.9 us (31%)
  Pallas kernels  54.4 us (26%)
  local copies, waits for them, and re-layouts  7.33 us (4%)
  other arithmetic  5.51 us (3%)
    pallas_call x4, Pallas kernels, side(): pl.pallas_call(kernel, out_shape=out_shape, in_specs=specs + [HBM] * len(...  46.6 us
    ppermute x16, starting transfers between devices, move(): return lax.ppermute(value, 'p', pairs)  33 us
    ppermute x16, waiting for transfers between devices, move(): return lax.ppermute(value, 'p', pairs)  26.7 us
    all_to_all x2, waiting for transfers between devices, gather_heads(): wide = lax.all_to_all(packed, ('zh', 'h'), 0, 0, tiled=True)  24.9 us
    all_to_all x2, starting transfers between devices, gather_heads(): wide = lax.all_to_all(packed, ('zh', 'h'), 0, 0, tiled=True)  13.5 us
    all_to_all x1, starting transfers between devices, shards(): lax.all_to_all(am.reshape(16, 2, QTR, E), ('zh', 'h'), 0, 0, tiled=True)  11.8 us
    all_to_all x1, starting transfers between devices, shards(): lax.all_to_all(jnp.broadcast_to(stats[None], (GROUPS, SROWS, E)), ('zh',...  9.33 us
    ppermute x3, waiting for transfers between devices, shards(): lax.ppermute(pieces[n], 'h', [(i, (i + n) % 4) for i in range(4)])  8.73 us
  transfers between devices with their start and end apart: 24, of which 13 were waited for; matrix products, arithmetic and copies ran while one was open for 3% of the time, Pallas kernels for 24%

profile of v6, /device:TPU:1, one launch (start us, length us, event | category | flops | bytes accessed | tf_op | source)
XLA Modules:
  0.0 206.4 jit_solution(11035687408181587224)
XLA Ops:
  1.2 3.0 %pack.2 = bf16[16,2,2,64,128]{4,3,2,1,0:T(8,128)(2,1)} custom-call(s32[3]{0:T(128)} %pad_add_fusion.pos, s32[128]{0:T(128)} %frames.9, f32[8,128]{1,0:T(8,128)} %constant.36.clone.rates, bf16[20,64,128]{2,1,0:T(8,128)(2,1)} %bitcast.40, bf16[20,64,128]{2,1,0:T(8,128)(2,1)} %bitcast.41), custom_call_target="tpu_custom_call" | custom-call | tf_op jit(solution)/shard_map/pack/pallas_call | solution.py:67
  4.2 10.0 %all-to-all-start = ((bf16[16,2,2,64,128]{4,3,2,1,0:T(8,128)(2,1)}), bf16[16,2,2,64,128]{4,3,2,1,0:T(8,128)(2,1)S(1)}, u32[]{:S(2)}, u32[]{:S(2)}) async-start(bf16[16,2,2,64,128]{4,3,2,1,0:T(8,128)(2,1)} %pack.2), calls=%async_computation | async-start | bytes 2097152 | tf_op jit(solution)/shard_map/all_to_all | solution.py:489
  14.2 3.0 %pack.3 = bf16[16,2,2,64,128]{4,3,2,1,0:T(8,128)(2,1)} custom-call(s32[3]{0:T(128)} %pad_add_fusion.pos, s32[128]{0:T(128)} %frames.9, f32[8,128]{1,0:T(8,128)} %constant.36.clone.rates, bf16[20,64,128]{2,1,0:T(8,128)(2,1)} %bitcast.42, bf16[20,64,128]{2,1,0:T(8,128)(2,1)} %bitcast.43), custom_call_target="tpu_custom_call" | custom-call | tf_op jit(solution)/shard_map/pack/pallas_call | solution.py:67
  17.3 24.9 %all-to-all-done = bf16[16,2,2,64,128]{4,3,2,1,0:T(8,128)(2,1)S(1)} async-done(((bf16[16,2,2,64,128]{4,3,2,1,0:T(8,128)(2,1)}), bf16[16,2,2,64,128]{4,3,2,1,0:T(8,128)(2,1)S(1)}, u32[]{:S(2)}, u32[]{:S(2)}) %all-to-all-start) | async-done | bytes 1048608 | tf_op jit(solution)/shard_map/all_to_all | solution.py:489
  42.2 3.6 %all-to-all-start.1 = ((bf16[16,2,2,64,128]{4,3,2,1,0:T(8,128)(2,1)}), bf16[16,2,2,64,128]{4,3,2,1,0:T(8,128)(2,1)S(1)}, u32[]{:S(2)}, u32[]{:S(2)}) async-start(bf16[16,2,2,64,128]{4,3,2,1,0:T(8,128)(2,1)} %pack.3), calls=%async_computation.1 | async-start | bytes 2097152 | tf_op jit(solution)/shard_map/all_to_all | solution.py:489
  46.0 1.0 pad_maximum_fusion
  47.0 1.3 collective-permute-start.2
  48.3 1.4 collective-permute-start.1
  49.7 2.7 %collective-permute-start = (bf16[6,4,2,64,128]{4,3,2,1,0:T(8,128)(2,1)}, bf16[6,4,2,64,128]{4,3,2,1,0:T(8,128)(2,1)}, u32[]{:S(2)}, u32[]{:S(2)}) collective-permute-start(bf16[6,4,2,64,128]{4,3,2,1,0:T(8,128)(2,1)} %pad_maximum_fusion), channel_id=1, source_target_pairs={{0,8},{4,12},{8,0},{12,4},{16,24},{20,28},{24,16},{28,20},{32,40},... | collective-permute-start | bytes 2359304 | tf_op jit(solution)/shard_map/ppermute | solution.py:463
  52.5 0.9 pad_maximum_fusion.2
  53.4 14.4 %collective-permute-done.2.refs_0_ = bf16[6,4,2,64,128]{4,3,2,1,0:T(8,128)(2,1)S(1)} collective-permute-done((bf16[6,4,2,64,128]{4,3,2,1,0:T(8,128)(2,1)}, bf16[6,4,2,64,128]{4,3,2,1,0:T(8,128)(2,1)S(1)}, u32[]{:S(2)}, u32[]{:S(2)}) %collective-permute-start.2) | collective-permute-done | bytes 786464 | tf_op jit(solution)/shard_map/ppermute | solution.py:463
  67.7 2.3 %collective-permute-done.refs_3_ = bf16[6,4,2,64,128]{4,3,2,1,0:T(8,128)(2,1)} collective-permute-done((bf16[6,4,2,64,128]{4,3,2,1,0:T(8,128)(2,1)}, bf16[6,4,2,64,128]{4,3,2,1,0:T(8,128)(2,1)}, u32[]{:S(2)}, u32[]{:S(2)}) %collective-permute-start) | collective-permute-done | bytes 786464 | tf_op jit(solution)/shard_map/ppermute | solution.py:463
  70.1 1.0 broadcast_select_fusion.1
  71.1 4.4 %collective-permute-start.5 = (bf16[6,4,2,64,128]{4,3,2,1,0:T(8,128)(2,1)}, bf16[6,4,2,64,128]{4,3,2,1,0:T(8,128)(2,1)}, u32[]{:S(2)}, u32[]{:S(2)}) collective-permute-start(bf16[6,4,2,64,128]{4,3,2,1,0:T(8,128)(2,1)} %broadcast_select_fusion.1), channel_id=1, source_target_pairs={{0,12},{12,0},{16,28},{28,16},{32,44},{44,32},{48,60},{60,48},{1,1... | collective-permute-start | bytes 2359304 | tf_op jit(solution)/shard_map/ppermute | solution.py:463
  75.5 1.5 collective-permute-start.3
  77.1 0.9 copy-done.3
  78.5 1.3 collective-permute-start.7
  79.8 4.8 %collective-permute-start.6 = (bf16[5,4,2,64,128]{4,3,2,1,0:T(8,128)(2,1)S(1)}, bf16[5,4,2,64,128]{4,3,2,1,0:T(8,128)(2,1)}, u32[]{:S(2)}, u32[]{:S(2)}) collective-permute-start(bf16[5,4,2,64,128]{4,3,2,1,0:T(8,128)(2,1)S(1)} %copy-done.14), channel_id=1, source_target_pairs={{0,4},{4,8},{8,12},{16,20},{20,24},{24,28},{32,36},{36,40},{40,44}... | collective-permute-start | bytes 1966088 | tf_op jit(solution)/shard_map/ppermute | solution.py:463
  84.6 1.0 pad_maximum_fusion.1
  85.6 6.5 %collective-permute-done.5.refs_5_ = bf16[6,4,2,64,128]{4,3,2,1,0:T(8,128)(2,1)} collective-permute-done((bf16[6,4,2,64,128]{4,3,2,1,0:T(8,128)(2,1)}, bf16[6,4,2,64,128]{4,3,2,1,0:T(8,128)(2,1)}, u32[]{:S(2)}, u32[]{:S(2)}) %collective-permute-start.5) | collective-permute-done | bytes 786464 | tf_op jit(solution)/shard_map/ppermute | solution.py:463
  92.1 1.1 collective-permute-done.3.refs_2_
  93.2 0.9 copy-done.10
  94.1 1.2 collective-permute-done.4.refs_4_
  95.3 0.9 copy-done.11
  96.2 2.7 %collective-permute-start.8 = (bf16[6,4,2,64,128]{4,3,2,1,0:T(8,128)(2,1)}, bf16[6,4,2,64,128]{4,3,2,1,0:T(8,128)(2,1)S(1)}, u32[]{:S(2)}, u32[]{:S(2)}) collective-permute-start(bf16[6,4,2,64,128]{4,3,2,1,0:T(8,128)(2,1)} %pad_maximum_fusion.1), channel_id=1, source_target_pairs={{0,48},{4,52},{8,56},{12,60},{16,0},{20,4},{24,8},{28,12},{32,16},... | collective-permute-start | bytes 2359304 | tf_op jit(solution)/shard_map/ppermute | solution.py:463
  98.9 0.8 copy-done.13
  99.8 13.8 %forward_kernel.1 = (bf16[5,4,1,64,128]{4,3,2,1,0:T(8,128)(2,1)}, f32[24,128]{1,0:T(8,128)}) custom-call(s32[3]{0:T(128)} %pad_add_fusion.pos, bf16[6,4,2,64,128]{4,3,2,1,0:T(8,128)(2,1)} %copy-done.4, bf16[6,4,2,64,128]{4,3,2,1,0:T(8,128)(2,1)} %copy-done.5, bf16[6,4,2,64,128]{4,3,2,1,0:T(8,128)(2,1)} %copy-done.10, ...), custom_call_target="tpu_custom_call" | custom-call | flops 2181038080 | bytes 8388608 | tf_op jit(solution)/shard_map/forward_kernel/pallas_call | solution.py:405
  113.7 1.1 broadcast_select_fusion
  115.1 1.0 collective-permute-done.10.refs_3_
  116.1 1.0 broadcast_in_dim.2
  117.1 9.3 %all-to-all-start.2 = ((f32[64,24,128]{2,1,0:T(8,128)}), f32[64,24,128]{2,1,0:T(8,128)S(1)}, u32[]{:S(2)}, u32[]{:S(2)}) async-start(f32[64,24,128]{2,1,0:T(8,128)} %broadcast_in_dim.2), calls=%async_computation.2 | async-start | bytes 1572864 | tf_op jit(solution)/shard_map/all_to_all | solution.py:516
  126.5 4.1 %collective-permute-start.13 = (bf16[6,4,2,64,128]{4,3,2,1,0:T(8,128)(2,1)}, bf16[6,4,2,64,128]{4,3,2,1,0:T(8,128)(2,1)S(1)}, u32[]{:S(2)}, u32[]{:S(2)}) collective-permute-start(bf16[6,4,2,64,128]{4,3,2,1,0:T(8,128)(2,1)} %broadcast_select_fusion), channel_id=1, source_target_pairs={{0,12},{12,0},{16,28},{28,16},{32,44},{44,32},{48,60},{60,48},{1,1... | collective-permute-start | bytes 2359304 | tf_op jit(solution)/shard_map/ppermute | solution.py:463
  130.6 2.5 %collective-permute-start.11 = (bf16[6,4,2,64,128]{4,3,2,1,0:T(8,128)(2,1)}, bf16[6,4,2,64,128]{4,3,2,1,0:T(8,128)(2,1)}, u32[]{:S(2)}, u32[]{:S(2)}) collective-permute-start(bf16[6,4,2,64,128]{4,3,2,1,0:T(8,128)(2,1)} %broadcast_select_fusion), channel_id=1, source_target_pairs={{0,48},{4,52},{8,24},{12,28},{16,0},{20,4},{24,40},{28,44},{32,16}... | collective-permute-start | bytes 2359304 | tf_op jit(solution)/shard_map/ppermute | solution.py:463
  133.1 1.3 collective-permute-start.15
  134.4 4.9 %collective-permute-start.14 = (bf16[6,4,2,64,128]{4,3,2,1,0:T(8,128)(2,1)}, bf16[6,4,2,64,128]{4,3,2,1,0:T(8,128)(2,1)}, u32[]{:S(2)}, u32[]{:S(2)}) collective-permute-start(bf16[6,4,2,64,128]{4,3,2,1,0:T(8,128)(2,1)} %pad_maximum_fusion.1), channel_id=1, source_target_pairs={{0,4},{4,8},{8,12},{16,20},{20,24},{24,28},{32,36},{36,40},{40,44}... | collective-permute-start | bytes 2359304 | tf_op jit(solution)/shard_map/ppermute | solution.py:463
  139.3 13.6 %query_kernel.1 = (bf16[4,4,2,64,128]{4,3,2,1,0:T(8,128)(2,1)}, bf16[1,4,2,64,128]{4,3,2,1,0:T(8,128)(2,1)}) custom-call(s32[3]{0:T(128)} %pad_add_fusion.pos, s32[128]{0:T(128)} %frames.9, f32[8,128]{1,0:T(8,128)} %constant.36.clone.rates, bf16[6,4,2,64,128]{4,3,2,1,0:T(8,128)(2,1)} %copy-done.4, bf16[6,4,2,64,128]{4,3,2,1,0:T(8,128)(2,1)} %copy-done.5, ...), custom_call_target="tpu_custom_call" | custom-call | flops 3271557120 | bytes 8388608 | tf_op jit(solution)/shard_map/query_kernel/pallas_call | solution.py:405
  152.9 11.8 %all-to-all-start.3 = ((bf16[16,2,64,128]{3,2,1,0:T(8,128)(2,1)}), bf16[16,2,64,128]{3,2,1,0:T(8,128)(2,1)S(1)}, u32[]{:S(2)}, u32[]{:S(2)}) async-start(bf16[16,2,64,128]{3,2,1,0:T(8,128)(2,1)} %bitcast.39), calls=%async_computation.3 | async-start | bytes 1048576 | tf_op jit(solution)/shard_map/all_to_all | solution.py:523
  164.8 0.9 copy-done.12
  165.6 13.5 %key_kernel.1 = bf16[4,4,2,64,128]{4,3,2,1,0:T(8,128)(2,1)} custom-call(s32[3]{0:T(128)} %pad_add_fusion.pos, s32[128]{0:T(128)} %frames.9, f32[8,128]{1,0:T(8,128)} %constant.36.clone.rates, bf16[6,4,2,64,128]{4,3,2,1,0:T(8,128)(2,1)} %copy-done.6, bf16[6,4,2,64,128]{4,3,2,1,0:T(8,128)(2,1)} %copy-done.7, ...), custom_call_target="tpu_custom_call" | custom-call | flops 3489660928 | bytes 8388608 | tf_op jit(solution)/shard_map/key_kernel/pallas_call | solution.py:405
  179.1 2.9 %all-to-all-done.3.a_hbm = bf16[16,2,64,128]{3,2,1,0:T(8,128)(2,1)S(1)} async-done(((bf16[16,2,64,128]{3,2,1,0:T(8,128)(2,1)}), bf16[16,2,64,128]{3,2,1,0:T(8,128)(2,1)S(1)}, u32[]{:S(2)}, u32[]{:S(2)}) %all-to-all-start.3) | async-done | bytes 524320 | tf_op jit(solution)/shard_map/all_to_all | solution.py:523
  182.0 4.3 %all-to-all-start.4 = ((bf16[16,2,64,128]{3,2,1,0:T(8,128)(2,1)}), bf16[16,2,64,128]{3,2,1,0:T(8,128)(2,1)S(1)}, u32[]{:S(2)}, u32[]{:S(2)}) async-start(bf16[16,2,64,128]{3,2,1,0:T(8,128)(2,1)} %bitcast.38), calls=%async_computation.4 | async-start | bytes 1048576 | tf_op jit(solution)/shard_map/all_to_all | solution.py:528
  186.3 5.6 %extra_key_kernel.1 = (bf16[4,64,128]{2,1,0:T(8,128)(2,1)}, bf16[4,64,128]{2,1,0:T(8,128)(2,1)}, bf16[4,64,128]{2,1,0:T(8,128)(2,1)}, bf16[4,64,128]{2,1,0:T(8,128)(2,1)}) custom-call(s32[3]{0:T(128)} %pad_add_fusion.pos, s32[128]{0:T(128)} %frames.9, f32[8,128]{1,0:T(8,128)} %constant.36.clone.rates, bf16[6,4,2,64,128]{4,3,2,1,0:T(8,128)(2,1)} %copy-done.6, ...), custom_call_target="tpu_custom_call" | custom-call | flops 872415232 | bytes 8388608 | tf_op jit(solution)/shard_map/extra_key_kernel/pallas_call | solution.py:405
  192.0 1.7 collective-permute-start.16
  194.2 4.3 %collective-permute-done.16.refs_1_ = bf16[4,64,128]{2,1,0:T(8,128)(2,1)S(1)} collective-permute-done((bf16[4,64,128]{2,1,0:T(8,128)(2,1)}, bf16[4,64,128]{2,1,0:T(8,128)(2,1)S(1)}, u32[]{:S(2)}, u32[]{:S(2)}) %collective-permute-start.16) | collective-permute-done | bytes 65568 | tf_op jit(solution)/shard_map/ppermute | solution.py:527
  198.5 4.0 %collective-permute-done.17.refs_2_ = bf16[4,64,128]{2,1,0:T(8,128)(2,1)S(1)} collective-permute-done((bf16[4,64,128]{2,1,0:T(8,128)(2,1)}, bf16[4,64,128]{2,1,0:T(8,128)(2,1)S(1)}, u32[]{:S(2)}, u32[]{:S(2)}) %collective-permute-start.17) | collective-permute-done | bytes 65568 | tf_op jit(solution)/shard_map/ppermute | solution.py:527
  203.0 0.7 all-to-all-done.4.b_hbm
  203.7 0.8 copy-done
  204.5 1.7 unpack.1
  (51 shorter events, 2.9 us)
Async XLA Ops:
  4.2 37.9 %all-to-all-start = ((bf16[16,2,2,64,128]{4,3,2,1,0:T(8,128)(2,1)}), bf16[16,2,2,64,128]{4,3,2,1,0:T(8,128)(2,1)S(1)}, u32[]{:S(2)}, u32[]{:S(2)}) async-start(bf16[16,2,2,64,128]{4,3,2,1,0:T(8,128)(2,1)} %pack.2), calls=%async_computation | async-start | bytes 2097152 | tf_op jit(solution)/shard_map/all_to_all | solution.py:489
  42.2 3.6 %copy-start.2 = (bf16[16,2,2,64,128]{4,3,2,1,0:T(8,128)(2,1)}, bf16[16,2,2,64,128]{4,3,2,1,0:T(8,128)(2,1)S(1)}, u32[]{:S(2)}) copy-start(bf16[16,2,2,64,128]{4,3,2,1,0:T(8,128)(2,1)S(1)} %all-to-all-done) | copy-start | bytes 3145732
  42.2 34.8 %all-to-all-start.1 = ((bf16[16,2,2,64,128]{4,3,2,1,0:T(8,128)(2,1)}), bf16[16,2,2,64,128]{4,3,2,1,0:T(8,128)(2,1)S(1)}, u32[]{:S(2)}, u32[]{:S(2)}) async-start(bf16[16,2,2,64,128]{4,3,2,1,0:T(8,128)(2,1)} %pack.3), calls=%async_computation.1 | async-start | bytes 2097152 | tf_op jit(solution)/shard_map/all_to_all | solution.py:489
  47.0 20.8 %collective-permute-start.2 = (bf16[6,4,2,64,128]{4,3,2,1,0:T(8,128)(2,1)}, bf16[6,4,2,64,128]{4,3,2,1,0:T(8,128)(2,1)S(1)}, u32[]{:S(2)}, u32[]{:S(2)}) collective-permute-start(bf16[6,4,2,64,128]{4,3,2,1,0:T(8,128)(2,1)} %pad_maximum_fusion), channel_id=1, source_target_pairs={{0,16},{4,20},{8,24},{12,28},{16,32},{20,36},{24,40},{28,44},{32,4... | collective-permute-start | bytes 2359304 | tf_op jit(solution)/shard_map/ppermute | solution.py:463
  48.3 19.5 %collective-permute-start.1 = (bf16[6,4,2,64,128]{4,3,2,1,0:T(8,128)(2,1)}, bf16[6,4,2,64,128]{4,3,2,1,0:T(8,128)(2,1)S(1)}, u32[]{:S(2)}, u32[]{:S(2)}) collective-permute-start(bf16[6,4,2,64,128]{4,3,2,1,0:T(8,128)(2,1)} %pad_maximum_fusion), channel_id=1, source_target_pairs={{0,48},{4,52},{8,56},{12,60},{16,0},{20,4},{24,8},{28,12},{32,16},... | collective-permute-start | bytes 2359304 | tf_op jit(solution)/shard_map/ppermute | solution.py:463
  49.7 20.4 %collective-permute-start = (bf16[6,4,2,64,128]{4,3,2,1,0:T(8,128)(2,1)}, bf16[6,4,2,64,128]{4,3,2,1,0:T(8,128)(2,1)}, u32[]{:S(2)}, u32[]{:S(2)}) collective-permute-start(bf16[6,4,2,64,128]{4,3,2,1,0:T(8,128)(2,1)} %pad_maximum_fusion), channel_id=1, source_target_pairs={{0,8},{4,12},{8,0},{12,4},{16,24},{20,28},{24,16},{28,20},{32,40},... | collective-permute-start | bytes 2359304 | tf_op jit(solution)/shard_map/ppermute | solution.py:463
  67.7 3.3 %copy-start.4 = (bf16[6,4,2,64,128]{4,3,2,1,0:T(8,128)(2,1)}, bf16[6,4,2,64,128]{4,3,2,1,0:T(8,128)(2,1)S(1)}, u32[]{:S(2)}) copy-start(bf16[6,4,2,64,128]{4,3,2,1,0:T(8,128)(2,1)S(1)} %collective-permute-done.2.refs_0_) | copy-start | bytes 2359300
  67.7 3.3 %copy-start.5 = (bf16[6,4,2,64,128]{4,3,2,1,0:T(8,128)(2,1)}, bf16[6,4,2,64,128]{4,3,2,1,0:T(8,128)(2,1)S(1)}, u32[]{:S(2)}) copy-start(bf16[6,4,2,64,128]{4,3,2,1,0:T(8,128)(2,1)S(1)} %collective-permute-done.1.refs_1_) | copy-start | bytes 2359300
  71.1 21.0 %collective-permute-start.5 = (bf16[6,4,2,64,128]{4,3,2,1,0:T(8,128)(2,1)}, bf16[6,4,2,64,128]{4,3,2,1,0:T(8,128)(2,1)}, u32[]{:S(2)}, u32[]{:S(2)}) collective-permute-start(bf16[6,4,2,64,128]{4,3,2,1,0:T(8,128)(2,1)} %broadcast_select_fusion.1), channel_id=1, source_target_pairs={{0,12},{12,0},{16,28},{28,16},{32,44},{44,32},{48,60},{60,48},{1,1... | collective-permute-start | bytes 2359304 | tf_op jit(solution)/shard_map/ppermute | solution.py:463
  75.5 17.7 %collective-permute-start.3 = (bf16[6,4,2,64,128]{4,3,2,1,0:T(8,128)(2,1)}, bf16[6,4,2,64,128]{4,3,2,1,0:T(8,128)(2,1)S(1)}, u32[]{:S(2)}, u32[]{:S(2)}) collective-permute-start(bf16[6,4,2,64,128]{4,3,2,1,0:T(8,128)(2,1)} %broadcast_select_fusion.1), channel_id=1, source_target_pairs={{0,48},{4,52},{8,24},{12,28},{16,0},{20,4},{24,40},{28,44},{32,16}... | collective-permute-start | bytes 2359304 | tf_op jit(solution)/shard_map/ppermute | solution.py:463
  76.9 18.4 %collective-permute-start.4 = (bf16[6,4,2,64,128]{4,3,2,1,0:T(8,128)(2,1)}, bf16[6,4,2,64,128]{4,3,2,1,0:T(8,128)(2,1)S(1)}, u32[]{:S(2)}, u32[]{:S(2)}) collective-permute-start(bf16[6,4,2,64,128]{4,3,2,1,0:T(8,128)(2,1)} %collective-permute-done.refs_3_), channel_id=1, source_target_pairs={{0,16},{4,20},{8,56},{12,60},{16,32},{20,36},{24,8},{28,12},{32,48... | collective-permute-start | bytes 2359304 | tf_op jit(solution)/shard_map/ppermute | solution.py:463
  77.0 1.0 copy-start.3
  77.0 1.5 copy-start.14
  78.5 20.4 %collective-permute-start.7 = (bf16[5,4,2,64,128]{4,3,2,1,0:T(8,128)(2,1)S(1)}, bf16[5,4,2,64,128]{4,3,2,1,0:T(8,128)(2,1)S(1)}, u32[]{:S(2)}, u32[]{:S(2)}) collective-permute-start(bf16[5,4,2,64,128]{4,3,2,1,0:T(8,128)(2,1)S(1)} %copy-done.14), channel_id=1, source_target_pairs={{4,0},{8,4},{12,8},{20,16},{24,20},{28,24},{36,32},{40,36},{44,40}... | collective-permute-start | bytes 1966088 | tf_op jit(solution)/shard_map/ppermute | solution.py:463
  79.8 19.1 %collective-permute-start.6 = (bf16[5,4,2,64,128]{4,3,2,1,0:T(8,128)(2,1)S(1)}, bf16[5,4,2,64,128]{4,3,2,1,0:T(8,128)(2,1)}, u32[]{:S(2)}, u32[]{:S(2)}) collective-permute-start(bf16[5,4,2,64,128]{4,3,2,1,0:T(8,128)(2,1)S(1)} %copy-done.14), channel_id=1, source_target_pairs={{0,4},{4,8},{8,12},{16,20},{20,24},{24,28},{32,36},{36,40},{40,44}... | collective-permute-start | bytes 1966088 | tf_op jit(solution)/shard_map/ppermute | solution.py:463
  93.2 0.9 copy-start.10
  95.3 0.9 copy-start.11
  96.2 17.5 %collective-permute-start.9 = (bf16[6,4,2,64,128]{4,3,2,1,0:T(8,128)(2,1)}, bf16[6,4,2,64,128]{4,3,2,1,0:T(8,128)(2,1)S(1)}, u32[]{:S(2)}, u32[]{:S(2)}) collective-permute-start(bf16[6,4,2,64,128]{4,3,2,1,0:T(8,128)(2,1)} %pad_maximum_fusion.1), channel_id=1, source_target_pairs={{0,16},{4,20},{8,24},{12,28},{16,32},{20,36},{24,40},{28,44},{32,4... | collective-permute-start | bytes 2359304 | tf_op jit(solution)/shard_map/ppermute | solution.py:463
  96.2 17.5 %collective-permute-start.8 = (bf16[6,4,2,64,128]{4,3,2,1,0:T(8,128)(2,1)}, bf16[6,4,2,64,128]{4,3,2,1,0:T(8,128)(2,1)S(1)}, u32[]{:S(2)}, u32[]{:S(2)}) collective-permute-start(bf16[6,4,2,64,128]{4,3,2,1,0:T(8,128)(2,1)} %pad_maximum_fusion.1), channel_id=1, source_target_pairs={{0,48},{4,52},{8,56},{12,60},{16,0},{20,4},{24,8},{28,12},{32,16},... | collective-permute-start | bytes 2359304 | tf_op jit(solution)/shard_map/ppermute | solution.py:463
  98.9 17.2 %collective-permute-start.10 = (bf16[6,4,2,64,128]{4,3,2,1,0:T(8,128)(2,1)}, bf16[6,4,2,64,128]{4,3,2,1,0:T(8,128)(2,1)S(1)}, u32[]{:S(2)}, u32[]{:S(2)}) collective-permute-start(bf16[6,4,2,64,128]{4,3,2,1,0:T(8,128)(2,1)} %pad_maximum_fusion.1), channel_id=1, source_target_pairs={{0,8},{4,12},{8,0},{12,4},{16,24},{20,28},{24,16},{28,20},{32,40},... | collective-permute-start | bytes 2359304 | tf_op jit(solution)/shard_map/ppermute | solution.py:463
  98.9 0.8 copy-start.13
  113.7 1.1 copy-start.6
  113.7 1.4 copy-start.7
  113.7 2.4 %copy-start.15 = (f32[24,128]{1,0:T(8,128)S(1)}, f32[24,128]{1,0:T(8,128)}, u32[]{:S(2)}) copy-start(f32[24,128]{1,0:T(8,128)} %get-tuple-element.46.refs_12_) | copy-start | bytes 36868
  116.1 23.2 %copy-start.9 = (bf16[6,4,2,64,128]{4,3,2,1,0:T(8,128)(2,1)}, bf16[6,4,2,64,128]{4,3,2,1,0:T(8,128)(2,1)S(1)}, u32[]{:S(2)}) copy-start(bf16[6,4,2,64,128]{4,3,2,1,0:T(8,128)(2,1)S(1)} %collective-permute-done.10.refs_3_) | copy-start | bytes 2359300
  117.1 35.8 %all-to-all-start.2 = ((f32[64,24,128]{2,1,0:T(8,128)}), f32[64,24,128]{2,1,0:T(8,128)S(1)}, u32[]{:S(2)}, u32[]{:S(2)}) async-start(f32[64,24,128]{2,1,0:T(8,128)} %broadcast_in_dim.2), calls=%async_computation.2 | async-start | bytes 1572864 | tf_op jit(solution)/shard_map/all_to_all | solution.py:516
  126.5 38.3 %collective-permute-start.13 = (bf16[6,4,2,64,128]{4,3,2,1,0:T(8,128)(2,1)}, bf16[6,4,2,64,128]{4,3,2,1,0:T(8,128)(2,1)S(1)}, u32[]{:S(2)}, u32[]{:S(2)}) collective-permute-start(bf16[6,4,2,64,128]{4,3,2,1,0:T(8,128)(2,1)} %broadcast_select_fusion), channel_id=1, source_target_pairs={{0,12},{12,0},{16,28},{28,16},{32,44},{44,32},{48,60},{60,48},{1,1... | collective-permute-start | bytes 2359304 | tf_op jit(solution)/shard_map/ppermute | solution.py:463
  130.6 34.1 %collective-permute-start.11 = (bf16[6,4,2,64,128]{4,3,2,1,0:T(8,128)(2,1)}, bf16[6,4,2,64,128]{4,3,2,1,0:T(8,128)(2,1)}, u32[]{:S(2)}, u32[]{:S(2)}) collective-permute-start(bf16[6,4,2,64,128]{4,3,2,1,0:T(8,128)(2,1)} %broadcast_select_fusion), channel_id=1, source_target_pairs={{0,48},{4,52},{8,24},{12,28},{16,0},{20,4},{24,40},{28,44},{32,16}... | collective-permute-start | bytes 2359304 | tf_op jit(solution)/shard_map/ppermute | solution.py:463
  133.1 31.7 %collective-permute-start.15 = (bf16[6,4,2,64,128]{4,3,2,1,0:T(8,128)(2,1)}, bf16[6,4,2,64,128]{4,3,2,1,0:T(8,128)(2,1)}, u32[]{:S(2)}, u32[]{:S(2)}) collective-permute-start(bf16[6,4,2,64,128]{4,3,2,1,0:T(8,128)(2,1)} %pad_maximum_fusion.1), channel_id=1, source_target_pairs={{4,0},{8,4},{12,8},{20,16},{24,20},{28,24},{36,32},{40,36},{44,40}... | collective-permute-start | bytes 2359304 | tf_op jit(solution)/shard_map/ppermute | solution.py:463
  134.4 30.4 %collective-permute-start.14 = (bf16[6,4,2,64,128]{4,3,2,1,0:T(8,128)(2,1)}, bf16[6,4,2,64,128]{4,3,2,1,0:T(8,128)(2,1)}, u32[]{:S(2)}, u32[]{:S(2)}) collective-permute-start(bf16[6,4,2,64,128]{4,3,2,1,0:T(8,128)(2,1)} %pad_maximum_fusion.1), channel_id=1, source_target_pairs={{0,4},{4,8},{8,12},{16,20},{20,24},{24,28},{32,36},{36,40},{40,44}... | collective-permute-start | bytes 2359304 | tf_op jit(solution)/shard_map/ppermute | solution.py:463
  139.3 25.5 %collective-permute-start.12 = (bf16[6,4,2,64,128]{4,3,2,1,0:T(8,128)(2,1)S(1)}, bf16[6,4,2,64,128]{4,3,2,1,0:T(8,128)(2,1)}, u32[]{:S(2)}, u32[]{:S(2)}) collective-permute-start(bf16[6,4,2,64,128]{4,3,2,1,0:T(8,128)(2,1)S(1)} %collective-permute-done.10.refs_3_), channel_id=1, source_target_pairs={{0,16},{4,20},{8,56},{12,60},{16,32},{20,36},{24,8},{28,12},{32,48... | collective-permute-start | bytes 2359304 | tf_op jit(solution)/shard_map/ppermute | solution.py:463
  152.9 11.8 %copy-start.8 = (f32[64,24,128]{2,1,0:T(8,128)}, f32[64,24,128]{2,1,0:T(8,128)S(1)}, u32[]{:S(2)}) copy-start(f32[64,24,128]{2,1,0:T(8,128)S(1)} %all-to-all-done.2.refs_11_) | copy-start | bytes 2359300
  152.9 29.1 %all-to-all-start.3 = ((bf16[16,2,64,128]{3,2,1,0:T(8,128)(2,1)}), bf16[16,2,64,128]{3,2,1,0:T(8,128)(2,1)S(1)}, u32[]{:S(2)}, u32[]{:S(2)}) async-start(bf16[16,2,64,128]{3,2,1,0:T(8,128)(2,1)} %bitcast.39), calls=%async_computation.3 | async-start | bytes 1048576 | tf_op jit(solution)/shard_map/all_to_all | solution.py:523
  164.7 0.9 copy-start.12
  182.0 21.6 %all-to-all-start.4 = ((bf16[16,2,64,128]{3,2,1,0:T(8,128)(2,1)}), bf16[16,2,64,128]{3,2,1,0:T(8,128)(2,1)S(1)}, u32[]{:S(2)}, u32[]{:S(2)}) async-start(bf16[16,2,64,128]{3,2,1,0:T(8,128)(2,1)} %bitcast.38), calls=%async_computation.4 | async-start | bytes 1048576 | tf_op jit(solution)/shard_map/all_to_all | solution.py:528
  192.0 6.5 %collective-permute-start.16 = (bf16[4,64,128]{2,1,0:T(8,128)(2,1)}, bf16[4,64,128]{2,1,0:T(8,128)(2,1)S(1)}, u32[]{:S(2)}, u32[]{:S(2)}) collective-permute-start(bf16[4,64,128]{2,1,0:T(8,128)(2,1)} %get-tuple-element.57), channel_id=1, source_target_pairs={{0,1},{1,2},{2,3},{3,0},{4,5},{5,6},{6,7},{7,4},{8,9},{9,10},{10,1... | collective-permute-start | bytes 196616 | tf_op jit(solution)/shard_map/ppermute | solution.py:527
  193.7 8.8 %collective-permute-start.17 = (bf16[4,64,128]{2,1,0:T(8,128)(2,1)}, bf16[4,64,128]{2,1,0:T(8,128)(2,1)S(1)}, u32[]{:S(2)}, u32[]{:S(2)}) collective-permute-start(bf16[4,64,128]{2,1,0:T(8,128)(2,1)} %get-tuple-element.58), channel_id=1, source_target_pairs={{0,2},{1,3},{2,0},{3,1},{4,6},{5,7},{6,4},{7,5},{8,10},{9,11},{10,... | collective-permute-start | bytes 196616 | tf_op jit(solution)/shard_map/ppermute | solution.py:527
  193.7 10.0 %copy-start.1 = (s32[3]{0:T(128)S(1)}, s32[3]{0:T(128)}, u32[]{:S(2)}) copy-start(s32[3]{0:T(128)} %pad_add_fusion.pos) | copy-start | bytes 40
  193.7 9.3 %collective-permute-start.18 = (bf16[4,64,128]{2,1,0:T(8,128)(2,1)}, bf16[4,64,128]{2,1,0:T(8,128)(2,1)S(1)}, u32[]{:S(2)}, u32[]{:S(2)}) collective-permute-start(bf16[4,64,128]{2,1,0:T(8,128)(2,1)} %get-tuple-element.59), channel_id=1, source_target_pairs={{0,3},{1,0},{2,1},{3,2},{4,7},{5,4},{6,5},{7,6},{8,11},{9,8},{10,9... | collective-permute-start | bytes 196616 | tf_op jit(solution)/shard_map/ppermute | solution.py:527
  203.7 0.8 copy-start

commit v7 on v6

--- a/solution.py
+++ b/solution.py
@@ -314,21 +314,24 @@
     z = jnp.where(unit == 4, zh, unit)
     k = near(kv, z, unit, 0)
     v = near(kv, z, unit, 1)
-    weights, dscores, queries, grads = big
+    weights, dscores, queries, grads, scores, products = big
     for n, offset in enumerate(OFFSETS):
         if offset == FIRST_FAR:
             rest()
-        group, other, valid, slot = source(offset, unit, zh, p)
+        slot = source(offset, unit, zh, p)[3]
+        cols = slice(n * TOK, (n + 1) * TOK)
+        queries[cols] = pool_rows(offset, slot, unit, qg, pool, 0)
+        grads[cols] = pool_rows(offset, slot, unit, qg, pool, 1)
+    scores[...] = dot(k, queries[...], 1, 1)
+    products[...] = dot(v, grads[...], 1, 1)
+    for n, offset in enumerate(OFFSETS):
+        group, other, valid, _ = source(offset, unit, zh, p)
         total, delta = stats_of(other)
-        q = pool_rows(offset, slot, unit, qg, pool, 0)
-        g = pool_rows(offset, slot, unit, qg, pool, 1)
-        st = add_bias(dot(k, q, 1, 1), bias_of(mask, other, group, valid))
+        cols = slice(n * TOK, (n + 1) * TOK)
+        st = add_bias(scores[:, cols], bias_of(mask, other, group, valid))
         w = jnp.exp2(st * COEF - total)
-        cols = slice(n * TOK, (n + 1) * TOK)
         weights[:, cols] = w.astype(BF16)
-        dscores[:, cols] = (w * (dot(v, g, 1, 1) - delta)).astype(BF16)
-        queries[cols] = q
-        grads[cols] = g
+        dscores[:, cols] = (w * (products[:, cols] - delta)).astype(BF16)
     return dot(dscores[...], queries[...], 1, 0), dot(weights[...], grads[...], 1, 0)
 
 
@@ -355,8 +358,7 @@
 
 def extra_key_kernel(pos, frames, rates, *refs):
     parts, wholes, others = refs[:PARTS], refs[PARTS : PARTS + 5], refs[PARTS + 5 :]
-    *pieces, pool, sems, mask, kv, qg, stats, done, c0, c1, c2, c3, sums = others
-    big = (c0, c1, c2, c3)
+    pieces, (pool, sems, mask, kv, qg, stats, done, *big, sums) = others[:4], others[4:]
     rest = fetch(parts, pool, sems, list(zip(wholes, (mask, kv, qg, stats, done))), only_x=True)
     zh, p, h = pos[0], pos[1], pos[2]
 
@@ -395,7 +397,8 @@
 ALL_PAIRS = pltpu.VMEM((len(OFFSETS) * TOK, TOK), BF16)
 ALL_ROWS = pltpu.VMEM((len(OFFSETS) * TOK, E), BF16)
 ALL_COLUMNS = pltpu.VMEM((TOK, len(OFFSETS) * TOK), BF16)
-BIG = [ALL_COLUMNS, ALL_COLUMNS, ALL_ROWS, ALL_ROWS]
+WIDE_SUMS = pltpu.VMEM((TOK, len(OFFSETS) * TOK), F32)
+BIG = [ALL_COLUMNS, ALL_COLUMNS, ALL_ROWS, ALL_ROWS, WIDE_SUMS, WIDE_SUMS]
 EVERY = pltpu.VMEM((GROUPS, SROWS, E), F32)
 
 

time: 207 us -> 208 us (level)
  no operation moved by 1% of the time
where the time goes in v7:
time: 208 us; the launch traced here: 207 us
  starting transfers between devices  74.6 us (36%)
  waiting for transfers between devices  63.2 us (30%)
  Pallas kernels  55.1 us (26%)
  local copies, waits for them, and re-layouts  7.33 us (4%)
  other arithmetic  5.51 us (3%)
    pallas_call x4, Pallas kernels, side(): pl.pallas_call(kernel, out_shape=out_shape, in_specs=specs + [HBM] * len(...  47.3 us
    ppermute x16, starting transfers between devices, move(): return lax.ppermute(value, 'p', pairs)  33 us
    ppermute x16, waiting for transfers between devices, move(): return lax.ppermute(value, 'p', pairs)  26.7 us
    all_to_all x2, waiting for transfers between devices, gather_heads(): wide = lax.all_to_all(packed, ('zh', 'h'), 0, 0, tiled=True)  24.9 us
    all_to_all x2, starting transfers between devices, gather_heads(): wide = lax.all_to_all(packed, ('zh', 'h'), 0, 0, tiled=True)  13.5 us
    all_to_all x1, starting transfers between devices, shards(): lax.all_to_all(am.reshape(16, 2, QTR, E), ('zh', 'h'), 0, 0, tiled=True)  11.8 us
    all_to_all x1, starting transfers between devices, shards(): lax.all_to_all(jnp.broadcast_to(stats[None], (GROUPS, SROWS, E)), ('zh',...  9.33 us
    ppermute x3, waiting for transfers between devices, shards(): lax.ppermute(pieces[n], 'h', [(i, (i + n) % 4) for i in range(4)])  8.32 us
  transfers between devices with their start and end apart: 24, of which 13 were waited for; matrix products, arithmetic and copies ran while one was open for 3% of the time, Pallas kernels for 24%

profile of v7, /device:TPU:1, one launch (start us, length us, event | category | flops | bytes accessed | tf_op | source)
XLA Modules:
  0.0 206.8 jit_solution(17731264182293501187)
XLA Ops:
  1.2 3.0 %pack.2 = bf16[16,2,2,64,128]{4,3,2,1,0:T(8,128)(2,1)} custom-call(s32[3]{0:T(128)} %pad_add_fusion.pos, s32[128]{0:T(128)} %frames.9, f32[8,128]{1,0:T(8,128)} %constant.36.clone.rates, bf16[20,64,128]{2,1,0:T(8,128)(2,1)} %bitcast.40, bf16[20,64,128]{2,1,0:T(8,128)(2,1)} %bitcast.41), custom_call_target="tpu_custom_call" | custom-call | tf_op jit(solution)/shard_map/pack/pallas_call | solution.py:67
  4.2 10.0 %all-to-all-start = ((bf16[16,2,2,64,128]{4,3,2,1,0:T(8,128)(2,1)}), bf16[16,2,2,64,128]{4,3,2,1,0:T(8,128)(2,1)S(1)}, u32[]{:S(2)}, u32[]{:S(2)}) async-start(bf16[16,2,2,64,128]{4,3,2,1,0:T(8,128)(2,1)} %pack.2), calls=%async_computation | async-start | bytes 2097152 | tf_op jit(solution)/shard_map/all_to_all | solution.py:492
  14.2 3.0 %pack.3 = bf16[16,2,2,64,128]{4,3,2,1,0:T(8,128)(2,1)} custom-call(s32[3]{0:T(128)} %pad_add_fusion.pos, s32[128]{0:T(128)} %frames.9, f32[8,128]{1,0:T(8,128)} %constant.36.clone.rates, bf16[20,64,128]{2,1,0:T(8,128)(2,1)} %bitcast.42, bf16[20,64,128]{2,1,0:T(8,128)(2,1)} %bitcast.43), custom_call_target="tpu_custom_call" | custom-call | tf_op jit(solution)/shard_map/pack/pallas_call | solution.py:67
  17.3 24.9 %all-to-all-done = bf16[16,2,2,64,128]{4,3,2,1,0:T(8,128)(2,1)S(1)} async-done(((bf16[16,2,2,64,128]{4,3,2,1,0:T(8,128)(2,1)}), bf16[16,2,2,64,128]{4,3,2,1,0:T(8,128)(2,1)S(1)}, u32[]{:S(2)}, u32[]{:S(2)}) %all-to-all-start) | async-done | bytes 1048608 | tf_op jit(solution)/shard_map/all_to_all | solution.py:492
  42.2 3.6 %all-to-all-start.1 = ((bf16[16,2,2,64,128]{4,3,2,1,0:T(8,128)(2,1)}), bf16[16,2,2,64,128]{4,3,2,1,0:T(8,128)(2,1)S(1)}, u32[]{:S(2)}, u32[]{:S(2)}) async-start(bf16[16,2,2,64,128]{4,3,2,1,0:T(8,128)(2,1)} %pack.3), calls=%async_computation.1 | async-start | bytes 2097152 | tf_op jit(solution)/shard_map/all_to_all | solution.py:492
  46.0 1.0 pad_maximum_fusion
  47.0 1.3 collective-permute-start.2
  48.3 1.4 collective-permute-start.1
  49.7 2.7 %collective-permute-start = (bf16[6,4,2,64,128]{4,3,2,1,0:T(8,128)(2,1)}, bf16[6,4,2,64,128]{4,3,2,1,0:T(8,128)(2,1)}, u32[]{:S(2)}, u32[]{:S(2)}) collective-permute-start(bf16[6,4,2,64,128]{4,3,2,1,0:T(8,128)(2,1)} %pad_maximum_fusion), channel_id=1, source_target_pairs={{0,8},{4,12},{8,0},{12,4},{16,24},{20,28},{24,16},{28,20},{32,40},... | collective-permute-start | bytes 2359304 | tf_op jit(solution)/shard_map/ppermute | solution.py:466
  52.5 0.9 pad_maximum_fusion.2
  53.4 14.4 %collective-permute-done.2.refs_0_ = bf16[6,4,2,64,128]{4,3,2,1,0:T(8,128)(2,1)S(1)} collective-permute-done((bf16[6,4,2,64,128]{4,3,2,1,0:T(8,128)(2,1)}, bf16[6,4,2,64,128]{4,3,2,1,0:T(8,128)(2,1)S(1)}, u32[]{:S(2)}, u32[]{:S(2)}) %collective-permute-start.2) | collective-permute-done | bytes 786464 | tf_op jit(solution)/shard_map/ppermute | solution.py:466
  67.7 2.3 %collective-permute-done.refs_3_ = bf16[6,4,2,64,128]{4,3,2,1,0:T(8,128)(2,1)} collective-permute-done((bf16[6,4,2,64,128]{4,3,2,1,0:T(8,128)(2,1)}, bf16[6,4,2,64,128]{4,3,2,1,0:T(8,128)(2,1)}, u32[]{:S(2)}, u32[]{:S(2)}) %collective-permute-start) | collective-permute-done | bytes 786464 | tf_op jit(solution)/shard_map/ppermute | solution.py:466
  70.1 1.0 broadcast_select_fusion.1
  71.1 4.4 %collective-permute-start.5 = (bf16[6,4,2,64,128]{4,3,2,1,0:T(8,128)(2,1)}, bf16[6,4,2,64,128]{4,3,2,1,0:T(8,128)(2,1)}, u32[]{:S(2)}, u32[]{:S(2)}) collective-permute-start(bf16[6,4,2,64,128]{4,3,2,1,0:T(8,128)(2,1)} %broadcast_select_fusion.1), channel_id=1, source_target_pairs={{0,12},{12,0},{16,28},{28,16},{32,44},{44,32},{48,60},{60,48},{1,1... | collective-permute-start | bytes 2359304 | tf_op jit(solution)/shard_map/ppermute | solution.py:466
  75.5 1.5 collective-permute-start.3
  77.1 0.9 copy-done.3
  78.5 1.3 collective-permute-start.7
  79.8 4.8 %collective-permute-start.6 = (bf16[5,4,2,64,128]{4,3,2,1,0:T(8,128)(2,1)S(1)}, bf16[5,4,2,64,128]{4,3,2,1,0:T(8,128)(2,1)}, u32[]{:S(2)}, u32[]{:S(2)}) collective-permute-start(bf16[5,4,2,64,128]{4,3,2,1,0:T(8,128)(2,1)S(1)} %copy-done.14), channel_id=1, source_target_pairs={{0,4},{4,8},{8,12},{16,20},{20,24},{24,28},{32,36},{36,40},{40,44}... | collective-permute-start | bytes 1966088 | tf_op jit(solution)/shard_map/ppermute | solution.py:466
  84.6 1.0 pad_maximum_fusion.1
  85.6 6.5 %collective-permute-done.5.refs_5_ = bf16[6,4,2,64,128]{4,3,2,1,0:T(8,128)(2,1)} collective-permute-done((bf16[6,4,2,64,128]{4,3,2,1,0:T(8,128)(2,1)}, bf16[6,4,2,64,128]{4,3,2,1,0:T(8,128)(2,1)}, u32[]{:S(2)}, u32[]{:S(2)}) %collective-permute-start.5) | collective-permute-done | bytes 786464 | tf_op jit(solution)/shard_map/ppermute | solution.py:466
  92.1 1.1 collective-permute-done.3.refs_2_
  93.2 0.9 copy-done.10
  94.1 1.2 collective-permute-done.4.refs_4_
  95.3 0.9 copy-done.11
  96.2 2.7 %collective-permute-start.8 = (bf16[6,4,2,64,128]{4,3,2,1,0:T(8,128)(2,1)}, bf16[6,4,2,64,128]{4,3,2,1,0:T(8,128)(2,1)S(1)}, u32[]{:S(2)}, u32[]{:S(2)}) collective-permute-start(bf16[6,4,2,64,128]{4,3,2,1,0:T(8,128)(2,1)} %pad_maximum_fusion.1), channel_id=1, source_target_pairs={{0,48},{4,52},{8,56},{12,60},{16,0},{20,4},{24,8},{28,12},{32,16},... | collective-permute-start | bytes 2359304 | tf_op jit(solution)/shard_map/ppermute | solution.py:466
  98.9 0.8 copy-done.13
  99.8 13.8 %forward_kernel.1 = (bf16[5,4,1,64,128]{4,3,2,1,0:T(8,128)(2,1)}, f32[24,128]{1,0:T(8,128)}) custom-call(s32[3]{0:T(128)} %pad_add_fusion.pos, bf16[6,4,2,64,128]{4,3,2,1,0:T(8,128)(2,1)} %copy-done.4, bf16[6,4,2,64,128]{4,3,2,1,0:T(8,128)(2,1)} %copy-done.5, bf16[6,4,2,64,128]{4,3,2,1,0:T(8,128)(2,1)} %copy-done.10, ...), custom_call_target="tpu_custom_call" | custom-call | flops 2181038080 | bytes 8388608 | tf_op jit(solution)/shard_map/forward_kernel/pallas_call | solution.py:408
  113.7 1.1 broadcast_select_fusion
  115.1 1.0 collective-permute-done.10.refs_3_
  116.1 1.0 broadcast_in_dim.2
  117.1 9.3 %all-to-all-start.2 = ((f32[64,24,128]{2,1,0:T(8,128)}), f32[64,24,128]{2,1,0:T(8,128)S(1)}, u32[]{:S(2)}, u32[]{:S(2)}) async-start(f32[64,24,128]{2,1,0:T(8,128)} %broadcast_in_dim.2), calls=%async_computation.2 | async-start | bytes 1572864 | tf_op jit(solution)/shard_map/all_to_all | solution.py:519
  126.5 4.1 %collective-permute-start.13 = (bf16[6,4,2,64,128]{4,3,2,1,0:T(8,128)(2,1)}, bf16[6,4,2,64,128]{4,3,2,1,0:T(8,128)(2,1)S(1)}, u32[]{:S(2)}, u32[]{:S(2)}) collective-permute-start(bf16[6,4,2,64,128]{4,3,2,1,0:T(8,128)(2,1)} %broadcast_select_fusion), channel_id=1, source_target_pairs={{0,12},{12,0},{16,28},{28,16},{32,44},{44,32},{48,60},{60,48},{1,1... | collective-permute-start | bytes 2359304 | tf_op jit(solution)/shard_map/ppermute | solution.py:466
  130.6 2.5 %collective-permute-start.11 = (bf16[6,4,2,64,128]{4,3,2,1,0:T(8,128)(2,1)}, bf16[6,4,2,64,128]{4,3,2,1,0:T(8,128)(2,1)}, u32[]{:S(2)}, u32[]{:S(2)}) collective-permute-start(bf16[6,4,2,64,128]{4,3,2,1,0:T(8,128)(2,1)} %broadcast_select_fusion), channel_id=1, source_target_pairs={{0,48},{4,52},{8,24},{12,28},{16,0},{20,4},{24,40},{28,44},{32,16}... | collective-permute-start | bytes 2359304 | tf_op jit(solution)/shard_map/ppermute | solution.py:466
  133.1 1.3 collective-permute-start.15
  134.4 4.9 %collective-permute-start.14 = (bf16[6,4,2,64,128]{4,3,2,1,0:T(8,128)(2,1)}, bf16[6,4,2,64,128]{4,3,2,1,0:T(8,128)(2,1)}, u32[]{:S(2)}, u32[]{:S(2)}) collective-permute-start(bf16[6,4,2,64,128]{4,3,2,1,0:T(8,128)(2,1)} %pad_maximum_fusion.1), channel_id=1, source_target_pairs={{0,4},{4,8},{8,12},{16,20},{20,24},{24,28},{32,36},{36,40},{40,44}... | collective-permute-start | bytes 2359304 | tf_op jit(solution)/shard_map/ppermute | solution.py:466
  139.3 13.6 %query_kernel.1 = (bf16[4,4,2,64,128]{4,3,2,1,0:T(8,128)(2,1)}, bf16[1,4,2,64,128]{4,3,2,1,0:T(8,128)(2,1)}) custom-call(s32[3]{0:T(128)} %pad_add_fusion.pos, s32[128]{0:T(128)} %frames.9, f32[8,128]{1,0:T(8,128)} %constant.36.clone.rates, bf16[6,4,2,64,128]{4,3,2,1,0:T(8,128)(2,1)} %copy-done.4, bf16[6,4,2,64,128]{4,3,2,1,0:T(8,128)(2,1)} %copy-done.5, ...), custom_call_target="tpu_custom_call" | custom-call | flops 3271557120 | bytes 8388608 | tf_op jit(solution)/shard_map/query_kernel/pallas_call | solution.py:408
  152.9 11.8 %all-to-all-start.3 = ((bf16[16,2,64,128]{3,2,1,0:T(8,128)(2,1)}), bf16[16,2,64,128]{3,2,1,0:T(8,128)(2,1)S(1)}, u32[]{:S(2)}, u32[]{:S(2)}) async-start(bf16[16,2,64,128]{3,2,1,0:T(8,128)(2,1)} %bitcast.39), calls=%async_computation.3 | async-start | bytes 1048576 | tf_op jit(solution)/shard_map/all_to_all | solution.py:526
  164.8 0.9 copy-done.12
  165.6 13.8 %key_kernel.1 = bf16[4,4,2,64,128]{4,3,2,1,0:T(8,128)(2,1)} custom-call(s32[3]{0:T(128)} %pad_add_fusion.pos, s32[128]{0:T(128)} %frames.9, f32[8,128]{1,0:T(8,128)} %constant.36.clone.rates, bf16[6,4,2,64,128]{4,3,2,1,0:T(8,128)(2,1)} %copy-done.6, bf16[6,4,2,64,128]{4,3,2,1,0:T(8,128)(2,1)} %copy-done.7, ...), custom_call_target="tpu_custom_call" | custom-call | flops 3489660928 | bytes 8388608 | tf_op jit(solution)/shard_map/key_kernel/pallas_call | solution.py:408
  179.4 2.6 %all-to-all-done.3.a_hbm = bf16[16,2,64,128]{3,2,1,0:T(8,128)(2,1)S(1)} async-done(((bf16[16,2,64,128]{3,2,1,0:T(8,128)(2,1)}), bf16[16,2,64,128]{3,2,1,0:T(8,128)(2,1)S(1)}, u32[]{:S(2)}, u32[]{:S(2)}) %all-to-all-start.3) | async-done | bytes 524320 | tf_op jit(solution)/shard_map/all_to_all | solution.py:526
  182.0 4.7 %all-to-all-start.4 = ((bf16[16,2,64,128]{3,2,1,0:T(8,128)(2,1)}), bf16[16,2,64,128]{3,2,1,0:T(8,128)(2,1)S(1)}, u32[]{:S(2)}, u32[]{:S(2)}) async-start(bf16[16,2,64,128]{3,2,1,0:T(8,128)(2,1)} %bitcast.38), calls=%async_computation.4 | async-start | bytes 1048576 | tf_op jit(solution)/shard_map/all_to_all | solution.py:531
  186.7 6.0 %extra_key_kernel.1 = (bf16[4,64,128]{2,1,0:T(8,128)(2,1)}, bf16[4,64,128]{2,1,0:T(8,128)(2,1)}, bf16[4,64,128]{2,1,0:T(8,128)(2,1)}, bf16[4,64,128]{2,1,0:T(8,128)(2,1)}) custom-call(s32[3]{0:T(128)} %pad_add_fusion.pos, s32[128]{0:T(128)} %frames.9, f32[8,128]{1,0:T(8,128)} %constant.36.clone.rates, bf16[6,4,2,64,128]{4,3,2,1,0:T(8,128)(2,1)} %copy-done.6, ...), custom_call_target="tpu_custom_call" | custom-call | flops 872415232 | bytes 8388608 | tf_op jit(solution)/shard_map/extra_key_kernel/pallas_call | solution.py:408
  192.7 1.7 collective-permute-start.16
  195.0 3.9 %collective-permute-done.16.refs_1_ = bf16[4,64,128]{2,1,0:T(8,128)(2,1)S(1)} collective-permute-done((bf16[4,64,128]{2,1,0:T(8,128)(2,1)}, bf16[4,64,128]{2,1,0:T(8,128)(2,1)S(1)}, u32[]{:S(2)}, u32[]{:S(2)}) %collective-permute-start.16) | collective-permute-done | bytes 65568 | tf_op jit(solution)/shard_map/ppermute | solution.py:530
  198.9 4.0 %collective-permute-done.17.refs_2_ = bf16[4,64,128]{2,1,0:T(8,128)(2,1)S(1)} collective-permute-done((bf16[4,64,128]{2,1,0:T(8,128)(2,1)}, bf16[4,64,128]{2,1,0:T(8,128)(2,1)S(1)}, u32[]{:S(2)}, u32[]{:S(2)}) %collective-permute-start.17) | collective-permute-done | bytes 65568 | tf_op jit(solution)/shard_map/ppermute | solution.py:530
  203.3 0.7 all-to-all-done.4.b_hbm
  204.0 0.8 copy-done
  204.9 1.7 unpack.1
  (51 shorter events, 2.9 us)
Async XLA Ops:
  4.2 37.9 %all-to-all-start = ((bf16[16,2,2,64,128]{4,3,2,1,0:T(8,128)(2,1)}), bf16[16,2,2,64,128]{4,3,2,1,0:T(8,128)(2,1)S(1)}, u32[]{:S(2)}, u32[]{:S(2)}) async-start(bf16[16,2,2,64,128]{4,3,2,1,0:T(8,128)(2,1)} %pack.2), calls=%async_computation | async-start | bytes 2097152 | tf_op jit(solution)/shard_map/all_to_all | solution.py:492
  42.2 3.6 %copy-start.2 = (bf16[16,2,2,64,128]{4,3,2,1,0:T(8,128)(2,1)}, bf16[16,2,2,64,128]{4,3,2,1,0:T(8,128)(2,1)S(1)}, u32[]{:S(2)}) copy-start(bf16[16,2,2,64,128]{4,3,2,1,0:T(8,128)(2,1)S(1)} %all-to-all-done) | copy-start | bytes 3145732
  42.2 34.8 %all-to-all-start.1 = ((bf16[16,2,2,64,128]{4,3,2,1,0:T(8,128)(2,1)}), bf16[16,2,2,64,128]{4,3,2,1,0:T(8,128)(2,1)S(1)}, u32[]{:S(2)}, u32[]{:S(2)}) async-start(bf16[16,2,2,64,128]{4,3,2,1,0:T(8,128)(2,1)} %pack.3), calls=%async_computation.1 | async-start | bytes 2097152 | tf_op jit(solution)/shard_map/all_to_all | solution.py:492
  47.0 20.8 %collective-permute-start.2 = (bf16[6,4,2,64,128]{4,3,2,1,0:T(8,128)(2,1)}, bf16[6,4,2,64,128]{4,3,2,1,0:T(8,128)(2,1)S(1)}, u32[]{:S(2)}, u32[]{:S(2)}) collective-permute-start(bf16[6,4,2,64,128]{4,3,2,1,0:T(8,128)(2,1)} %pad_maximum_fusion), channel_id=1, source_target_pairs={{0,16},{4,20},{8,24},{12,28},{16,32},{20,36},{24,40},{28,44},{32,4... | collective-permute-start | bytes 2359304 | tf_op jit(solution)/shard_map/ppermute | solution.py:466
  48.3 19.5 %collective-permute-start.1 = (bf16[6,4,2,64,128]{4,3,2,1,0:T(8,128)(2,1)}, bf16[6,4,2,64,128]{4,3,2,1,0:T(8,128)(2,1)S(1)}, u32[]{:S(2)}, u32[]{:S(2)}) collective-permute-start(bf16[6,4,2,64,128]{4,3,2,1,0:T(8,128)(2,1)} %pad_maximum_fusion), channel_id=1, source_target_pairs={{0,48},{4,52},{8,56},{12,60},{16,0},{20,4},{24,8},{28,12},{32,16},... | collective-permute-start | bytes 2359304 | tf_op jit(solution)/shard_map/ppermute | solution.py:466
  49.7 20.4 %collective-permute-start = (bf16[6,4,2,64,128]{4,3,2,1,0:T(8,128)(2,1)}, bf16[6,4,2,64,128]{4,3,2,1,0:T(8,128)(2,1)}, u32[]{:S(2)}, u32[]{:S(2)}) collective-permute-start(bf16[6,4,2,64,128]{4,3,2,1,0:T(8,128)(2,1)} %pad_maximum_fusion), channel_id=1, source_target_pairs={{0,8},{4,12},{8,0},{12,4},{16,24},{20,28},{24,16},{28,20},{32,40},... | collective-permute-start | bytes 2359304 | tf_op jit(solution)/shard_map/ppermute | solution.py:466
  67.7 3.3 %copy-start.4 = (bf16[6,4,2,64,128]{4,3,2,1,0:T(8,128)(2,1)}, bf16[6,4,2,64,128]{4,3,2,1,0:T(8,128)(2,1)S(1)}, u32[]{:S(2)}) copy-start(bf16[6,4,2,64,128]{4,3,2,1,0:T(8,128)(2,1)S(1)} %collective-permute-done.2.refs_0_) | copy-start | bytes 2359300
  67.7 3.3 %copy-start.5 = (bf16[6,4,2,64,128]{4,3,2,1,0:T(8,128)(2,1)}, bf16[6,4,2,64,128]{4,3,2,1,0:T(8,128)(2,1)S(1)}, u32[]{:S(2)}) copy-start(bf16[6,4,2,64,128]{4,3,2,1,0:T(8,128)(2,1)S(1)} %collective-permute-done.1.refs_1_) | copy-start | bytes 2359300
  71.1 21.0 %collective-permute-start.5 = (bf16[6,4,2,64,128]{4,3,2,1,0:T(8,128)(2,1)}, bf16[6,4,2,64,128]{4,3,2,1,0:T(8,128)(2,1)}, u32[]{:S(2)}, u32[]{:S(2)}) collective-permute-start(bf16[6,4,2,64,128]{4,3,2,1,0:T(8,128)(2,1)} %broadcast_select_fusion.1), channel_id=1, source_target_pairs={{0,12},{12,0},{16,28},{28,16},{32,44},{44,32},{48,60},{60,48},{1,1... | collective-permute-start | bytes 2359304 | tf_op jit(solution)/shard_map/ppermute | solution.py:466
  75.5 17.7 %collective-permute-start.3 = (bf16[6,4,2,64,128]{4,3,2,1,0:T(8,128)(2,1)}, bf16[6,4,2,64,128]{4,3,2,1,0:T(8,128)(2,1)S(1)}, u32[]{:S(2)}, u32[]{:S(2)}) collective-permute-start(bf16[6,4,2,64,128]{4,3,2,1,0:T(8,128)(2,1)} %broadcast_select_fusion.1), channel_id=1, source_target_pairs={{0,48},{4,52},{8,24},{12,28},{16,0},{20,4},{24,40},{28,44},{32,16}... | collective-permute-start | bytes 2359304 | tf_op jit(solution)/shard_map/ppermute | solution.py:466
  76.9 18.4 %collective-permute-start.4 = (bf16[6,4,2,64,128]{4,3,2,1,0:T(8,128)(2,1)}, bf16[6,4,2,64,128]{4,3,2,1,0:T(8,128)(2,1)S(1)}, u32[]{:S(2)}, u32[]{:S(2)}) collective-permute-start(bf16[6,4,2,64,128]{4,3,2,1,0:T(8,128)(2,1)} %collective-permute-done.refs_3_), channel_id=1, source_target_pairs={{0,16},{4,20},{8,56},{12,60},{16,32},{20,36},{24,8},{28,12},{32,48... | collective-permute-start | bytes 2359304 | tf_op jit(solution)/shard_map/ppermute | solution.py:466
  77.0 1.0 copy-start.3
  77.0 1.5 copy-start.14
  78.5 20.4 %collective-permute-start.7 = (bf16[5,4,2,64,128]{4,3,2,1,0:T(8,128)(2,1)S(1)}, bf16[5,4,2,64,128]{4,3,2,1,0:T(8,128)(2,1)S(1)}, u32[]{:S(2)}, u32[]{:S(2)}) collective-permute-start(bf16[5,4,2,64,128]{4,3,2,1,0:T(8,128)(2,1)S(1)} %copy-done.14), channel_id=1, source_target_pairs={{4,0},{8,4},{12,8},{20,16},{24,20},{28,24},{36,32},{40,36},{44,40}... | collective-permute-start | bytes 1966088 | tf_op jit(solution)/shard_map/ppermute | solution.py:466
  79.8 19.1 %collective-permute-start.6 = (bf16[5,4,2,64,128]{4,3,2,1,0:T(8,128)(2,1)S(1)}, bf16[5,4,2,64,128]{4,3,2,1,0:T(8,128)(2,1)}, u32[]{:S(2)}, u32[]{:S(2)}) collective-permute-start(bf16[5,4,2,64,128]{4,3,2,1,0:T(8,128)(2,1)S(1)} %copy-done.14), channel_id=1, source_target_pairs={{0,4},{4,8},{8,12},{16,20},{20,24},{24,28},{32,36},{36,40},{40,44}... | collective-permute-start | bytes 1966088 | tf_op jit(solution)/shard_map/ppermute | solution.py:466
  93.2 0.9 copy-start.10
  95.3 0.9 copy-start.11
  96.2 17.5 %collective-permute-start.9 = (bf16[6,4,2,64,128]{4,3,2,1,0:T(8,128)(2,1)}, bf16[6,4,2,64,128]{4,3,2,1,0:T(8,128)(2,1)S(1)}, u32[]{:S(2)}, u32[]{:S(2)}) collective-permute-start(bf16[6,4,2,64,128]{4,3,2,1,0:T(8,128)(2,1)} %pad_maximum_fusion.1), channel_id=1, source_target_pairs={{0,16},{4,20},{8,24},{12,28},{16,32},{20,36},{24,40},{28,44},{32,4... | collective-permute-start | bytes 2359304 | tf_op jit(solution)/shard_map/ppermute | solution.py:466
  96.2 17.5 %collective-permute-start.8 = (bf16[6,4,2,64,128]{4,3,2,1,0:T(8,128)(2,1)}, bf16[6,4,2,64,128]{4,3,2,1,0:T(8,128)(2,1)S(1)}, u32[]{:S(2)}, u32[]{:S(2)}) collective-permute-start(bf16[6,4,2,64,128]{4,3,2,1,0:T(8,128)(2,1)} %pad_maximum_fusion.1), channel_id=1, source_target_pairs={{0,48},{4,52},{8,56},{12,60},{16,0},{20,4},{24,8},{28,12},{32,16},... | collective-permute-start | bytes 2359304 | tf_op jit(solution)/shard_map/ppermute | solution.py:466
  98.9 17.2 %collective-permute-start.10 = (bf16[6,4,2,64,128]{4,3,2,1,0:T(8,128)(2,1)}, bf16[6,4,2,64,128]{4,3,2,1,0:T(8,128)(2,1)S(1)}, u32[]{:S(2)}, u32[]{:S(2)}) collective-permute-start(bf16[6,4,2,64,128]{4,3,2,1,0:T(8,128)(2,1)} %pad_maximum_fusion.1), channel_id=1, source_target_pairs={{0,8},{4,12},{8,0},{12,4},{16,24},{20,28},{24,16},{28,20},{32,40},... | collective-permute-start | bytes 2359304 | tf_op jit(solution)/shard_map/ppermute | solution.py:466
  98.9 0.8 copy-start.13
  113.7 1.1 copy-start.6
  113.7 1.4 copy-start.7
  113.7 2.4 %copy-start.15 = (f32[24,128]{1,0:T(8,128)S(1)}, f32[24,128]{1,0:T(8,128)}, u32[]{:S(2)}) copy-start(f32[24,128]{1,0:T(8,128)} %get-tuple-element.46.refs_12_) | copy-start | bytes 36868
  116.1 23.2 %copy-start.9 = (bf16[6,4,2,64,128]{4,3,2,1,0:T(8,128)(2,1)}, bf16[6,4,2,64,128]{4,3,2,1,0:T(8,128)(2,1)S(1)}, u32[]{:S(2)}) copy-start(bf16[6,4,2,64,128]{4,3,2,1,0:T(8,128)(2,1)S(1)} %collective-permute-done.10.refs_3_) | copy-start | bytes 2359300
  117.1 35.8 %all-to-all-start.2 = ((f32[64,24,128]{2,1,0:T(8,128)}), f32[64,24,128]{2,1,0:T(8,128)S(1)}, u32[]{:S(2)}, u32[]{:S(2)}) async-start(f32[64,24,128]{2,1,0:T(8,128)} %broadcast_in_dim.2), calls=%async_computation.2 | async-start | bytes 1572864 | tf_op jit(solution)/shard_map/all_to_all | solution.py:519
  126.5 38.3 %collective-permute-start.13 = (bf16[6,4,2,64,128]{4,3,2,1,0:T(8,128)(2,1)}, bf16[6,4,2,64,128]{4,3,2,1,0:T(8,128)(2,1)S(1)}, u32[]{:S(2)}, u32[]{:S(2)}) collective-permute-start(bf16[6,4,2,64,128]{4,3,2,1,0:T(8,128)(2,1)} %broadcast_select_fusion), channel_id=1, source_target_pairs={{0,12},{12,0},{16,28},{28,16},{32,44},{44,32},{48,60},{60,48},{1,1... | collective-permute-start | bytes 2359304 | tf_op jit(solution)/shard_map/ppermute | solution.py:466
  130.6 34.1 %collective-permute-start.11 = (bf16[6,4,2,64,128]{4,3,2,1,0:T(8,128)(2,1)}, bf16[6,4,2,64,128]{4,3,2,1,0:T(8,128)(2,1)}, u32[]{:S(2)}, u32[]{:S(2)}) collective-permute-start(bf16[6,4,2,64,128]{4,3,2,1,0:T(8,128)(2,1)} %broadcast_select_fusion), channel_id=1, source_target_pairs={{0,48},{4,52},{8,24},{12,28},{16,0},{20,4},{24,40},{28,44},{32,16}... | collective-permute-start | bytes 2359304 | tf_op jit(solution)/shard_map/ppermute | solution.py:466
  133.1 31.7 %collective-permute-start.15 = (bf16[6,4,2,64,128]{4,3,2,1,0:T(8,128)(2,1)}, bf16[6,4,2,64,128]{4,3,2,1,0:T(8,128)(2,1)}, u32[]{:S(2)}, u32[]{:S(2)}) collective-permute-start(bf16[6,4,2,64,128]{4,3,2,1,0:T(8,128)(2,1)} %pad_maximum_fusion.1), channel_id=1, source_target_pairs={{4,0},{8,4},{12,8},{20,16},{24,20},{28,24},{36,32},{40,36},{44,40}... | collective-permute-start | bytes 2359304 | tf_op jit(solution)/shard_map/ppermute | solution.py:466
  134.4 30.4 %collective-permute-start.14 = (bf16[6,4,2,64,128]{4,3,2,1,0:T(8,128)(2,1)}, bf16[6,4,2,64,128]{4,3,2,1,0:T(8,128)(2,1)}, u32[]{:S(2)}, u32[]{:S(2)}) collective-permute-start(bf16[6,4,2,64,128]{4,3,2,1,0:T(8,128)(2,1)} %pad_maximum_fusion.1), channel_id=1, source_target_pairs={{0,4},{4,8},{8,12},{16,20},{20,24},{24,28},{32,36},{36,40},{40,44}... | collective-permute-start | bytes 2359304 | tf_op jit(solution)/shard_map/ppermute | solution.py:466
  139.3 25.5 %collective-permute-start.12 = (bf16[6,4,2,64,128]{4,3,2,1,0:T(8,128)(2,1)S(1)}, bf16[6,4,2,64,128]{4,3,2,1,0:T(8,128)(2,1)}, u32[]{:S(2)}, u32[]{:S(2)}) collective-permute-start(bf16[6,4,2,64,128]{4,3,2,1,0:T(8,128)(2,1)S(1)} %collective-permute-done.10.refs_3_), channel_id=1, source_target_pairs={{0,16},{4,20},{8,56},{12,60},{16,32},{20,36},{24,8},{28,12},{32,48... | collective-permute-start | bytes 2359304 | tf_op jit(solution)/shard_map/ppermute | solution.py:466
  152.9 11.8 %copy-start.8 = (f32[64,24,128]{2,1,0:T(8,128)}, f32[64,24,128]{2,1,0:T(8,128)S(1)}, u32[]{:S(2)}) copy-start(f32[64,24,128]{2,1,0:T(8,128)S(1)} %all-to-all-done.2.refs_11_) | copy-start | bytes 2359300
  152.9 29.1 %all-to-all-start.3 = ((bf16[16,2,64,128]{3,2,1,0:T(8,128)(2,1)}), bf16[16,2,64,128]{3,2,1,0:T(8,128)(2,1)S(1)}, u32[]{:S(2)}, u32[]{:S(2)}) async-start(bf16[16,2,64,128]{3,2,1,0:T(8,128)(2,1)} %bitcast.39), calls=%async_computation.3 | async-start | bytes 1048576 | tf_op jit(solution)/shard_map/all_to_all | solution.py:526
  164.7 0.9 copy-start.12
  182.0 22.0 %all-to-all-start.4 = ((bf16[16,2,64,128]{3,2,1,0:T(8,128)(2,1)}), bf16[16,2,64,128]{3,2,1,0:T(8,128)(2,1)S(1)}, u32[]{:S(2)}, u32[]{:S(2)}) async-start(bf16[16,2,64,128]{3,2,1,0:T(8,128)(2,1)} %bitcast.38), calls=%async_computation.4 | async-start | bytes 1048576 | tf_op jit(solution)/shard_map/all_to_all | solution.py:531
  192.7 6.1 %collective-permute-start.16 = (bf16[4,64,128]{2,1,0:T(8,128)(2,1)}, bf16[4,64,128]{2,1,0:T(8,128)(2,1)S(1)}, u32[]{:S(2)}, u32[]{:S(2)}) collective-permute-start(bf16[4,64,128]{2,1,0:T(8,128)(2,1)} %get-tuple-element.57), channel_id=1, source_target_pairs={{0,1},{1,2},{2,3},{3,0},{4,5},{5,6},{6,7},{7,4},{8,9},{9,10},{10,1... | collective-permute-start | bytes 196616 | tf_op jit(solution)/shard_map/ppermute | solution.py:530
  194.4 8.4 %collective-permute-start.17 = (bf16[4,64,128]{2,1,0:T(8,128)(2,1)}, bf16[4,64,128]{2,1,0:T(8,128)(2,1)S(1)}, u32[]{:S(2)}, u32[]{:S(2)}) collective-permute-start(bf16[4,64,128]{2,1,0:T(8,128)(2,1)} %get-tuple-element.58), channel_id=1, source_target_pairs={{0,2},{1,3},{2,0},{3,1},{4,6},{5,7},{6,4},{7,5},{8,10},{9,11},{10,... | collective-permute-start | bytes 196616 | tf_op jit(solution)/shard_map/ppermute | solution.py:530
  194.4 9.6 %copy-start.1 = (s32[3]{0:T(128)S(1)}, s32[3]{0:T(128)}, u32[]{:S(2)}) copy-start(s32[3]{0:T(128)} %pad_add_fusion.pos) | copy-start | bytes 40
  194.4 8.9 %collective-permute-start.18 = (bf16[4,64,128]{2,1,0:T(8,128)(2,1)}, bf16[4,64,128]{2,1,0:T(8,128)(2,1)S(1)}, u32[]{:S(2)}, u32[]{:S(2)}) collective-permute-start(bf16[4,64,128]{2,1,0:T(8,128)(2,1)} %get-tuple-element.59), channel_id=1, source_target_pairs={{0,3},{1,0},{2,1},{3,2},{4,7},{5,4},{6,5},{7,6},{8,11},{9,8},{10,9... | collective-permute-start | bytes 196616 | tf_op jit(solution)/shard_map/ppermute | solution.py:530
  204.0 0.8 copy-start
